TPU v7x, 128 devices: a whole 4x4x4 slice. The times are simulated.
128 devices in a mesh: wide: 32 (over x, z, core), quad: 4 (over y).
Axes of the slice: x: 4, y: 4, z: 4, core: 2. Of those that a mesh axis runs over, the one named last changes fastest.
Arguments:
- fine_pops: float32 [19, 256, 128, 128], P(None, 'wide', 'quad'), may hold values from 0.36 to 8.24, as said below
- coarse_pops: float32 [19, 64, 64, 128], P(None, 'wide', 'quad'), may hold values from 0.36 to 8.24, as said below
- fine_solid: int32 [256, 128, 128], P('wide', 'quad'), may hold values 0 or 1
- coarse_solid: int32 [64, 64, 128], P('wide', 'quad'), may hold values 0 or 1
- fine_active: int32 [64, 32, 32], P('wide', 'quad'), may hold values from 0 to 1, as said below
- coarse_covered: int32 [64, 64, 128], P('wide', 'quad'), may hold values from 0 to 1, as said below
- rates: float32 [15], replicated, may hold values from 0.7 to 1.7
Outputs:
- fine_out: float32 [19, 256, 128, 128], P(None, 'wide', 'quad')
- coarse_out: float32 [19, 64, 64, 128], P(None, 'wide', 'quad')
Inputs may be any that keep to these rules, and one draw needn't show every extreme that they name: `fine_pops`: populations are positive, each near w_q times 19. `coarse_pops`: populations are positive, each near w_q times 19. `fine_active`: 1 for an active fine block, 0 otherwise. coarse_covered[z, y, x] equals fine_active[x // 2, y // 2, z // 2].
All inputs are finite; a program needn't handle non-finite values. No bound on the sum of `fine_solid` or of `coarse_solid` on one device may be relied on, other than what follows from the above.
Results may differ from a plain program's by a relative error of at most 0.0003.
Values sent between devices are 32-bit elements; how exact they have to be, the bound alone decides.
No kernel may reach another device: no remote copies, remote signals or barrier semaphores. Data moves between devices by JAX's collectives and lax.ppermute only.
A program may use at most 128 MiB of HBM per device.

v0:
```python
import jax
import jax.numpy as jnp
from jax import lax
from jax.sharding import PartitionSpec as P

velocity_list = [
    (0, 0, 0),
    (1, 0, 0),
    (-1, 0, 0),
    (0, 1, 0),
    (0, -1, 0),
    (0, 0, 1),
    (0, 0, -1),
    (1, 1, 0),
    (-1, -1, 0),
    (1, -1, 0),
    (-1, 1, 0),
    (1, 0, 1),
    (-1, 0, -1),
    (1, 0, -1),
    (-1, 0, 1),
    (0, 1, 1),
    (0, -1, -1),
    (0, 1, -1),
    (0, -1, 1),
]
opposite_list = [0, 2, 1, 4, 3, 6, 5, 8, 7, 10, 9, 12, 11, 14, 13, 16, 15, 18, 17]
weight_list = [1.0 / 3.0] + [1.0 / 18.0] * 6 + [1.0 / 36.0] * 12
moment_patterns = [
    (0, 0, 0),
    (1, 0, 0),
    (0, 1, 0),
    (0, 0, 1),
    (1, 1, 0),
    (1, 0, 1),
    (0, 1, 1),
    (2, 0, 0),
    (0, 2, 0),
    (0, 0, 2),
    (1, 2, 0),
    (1, 0, 2),
    (2, 1, 0),
    (0, 1, 2),
    (2, 0, 1),
    (0, 2, 1),
    (2, 2, 0),
    (2, 0, 2),
    (0, 2, 2),
]


def extended(shard, sides, width):
    for axis, dim in sides:
        count, length = (lax.axis_size(axis), shard.shape[dim])
        up = [(i, (i + 1) % count) for i in range(count - 1)]
        down = [(j, i) for i, j in up]
        last = lax.slice_in_dim(shard, length - width, length, axis=dim)
        first = lax.slice_in_dim(shard, 0, width, axis=dim)
        before = lax.ppermute(last, axis, up)
        after = lax.ppermute(first, axis, down)
        shard = jnp.concatenate([before, shard, after], axis=dim)
    return shard


def velocity_columns():
    return [[float(entry[axis_index]) for entry in velocity_list] for axis_index in range(3)]


def velocity_rows():
    return [[float(part_value) for part_value in entry] for entry in velocity_list]


def build_moments():
    columns = velocity_columns()
    table_rows = []
    for power_x, power_y, power_z in moment_patterns:
        table_rows.append(
            [
                columns[0][slot] ** power_x
                * columns[1][slot] ** power_y
                * columns[2][slot] ** power_z
                for slot in range(19)
            ]
        )
    return table_rows


def invert_table(table_rows):
    order_size = len(table_rows)
    working = [
        list(table_rows[line]) + [1.0 if line == other else 0.0 for other in range(order_size)]
        for line in range(order_size)
    ]
    for column in range(order_size):
        pivot_line = max(range(column, order_size), key=lambda line: abs(working[line][column]))
        working[column], working[pivot_line] = (working[pivot_line], working[column])
        leading = working[column][column]
        working[column] = [entry / leading for entry in working[column]]
        for line in range(order_size):
            if line != column:
                factor = working[line][column]
                working[line] = [
                    entry - factor * pivot_entry
                    for entry, pivot_entry in zip(working[line], working[column])
                ]
    return [line_values[order_size:] for line_values in working]


def make_kernel(rates_full):
    moment_table = build_moments()
    moment_inverse = invert_table(moment_table)
    inverse_rows = jnp.asarray(moment_inverse, jnp.float32) * rates_full[None, :]
    return jnp.dot(
        inverse_rows,
        jnp.asarray(moment_table, jnp.float32),
        precision=lax.Precision.HIGHEST,
        preferred_element_type=jnp.float32,
    )


def collide(populations, kernel):
    shape_all = populations.shape
    flat = populations.reshape(19, -1)
    density = jnp.sum(flat, axis=0)
    momentum = jnp.dot(
        jnp.asarray(velocity_columns(), jnp.float32),
        flat,
        precision=lax.Precision.HIGHEST,
        preferred_element_type=jnp.float32,
    )
    velocity = momentum / density[None, :]
    speed_square = jnp.sum(velocity * velocity, axis=0)
    along = jnp.dot(
        jnp.asarray(velocity_rows(), jnp.float32),
        velocity,
        precision=lax.Precision.HIGHEST,
        preferred_element_type=jnp.float32,
    )
    weights = jnp.asarray(weight_list, jnp.float32)[:, None]
    equilibrium = (
        weights
        * density[None, :]
        * (1.0 + 3.0 * along + 4.5 * along * along - 1.5 * speed_square[None, :])
    )
    post = flat - jnp.dot(
        kernel,
        flat - equilibrium,
        precision=lax.Precision.HIGHEST,
        preferred_element_type=jnp.float32,
    )
    return post.reshape(shape_all)


def stream(padded, post, order):
    extent = post.shape[1:]
    pieces = []
    for index in range(19):
        starts = [1 - velocity_list[index][axis] for axis in order]
        window = tuple((slice(start, start + length) for start, length in zip(starts, extent)))
        moved = padded[(index,) + window]
        fluid_near = padded[(19,) + window]
        pieces.append(jnp.where(fluid_near > 0.5, moved, post[opposite_list[index]]))
    return jnp.stack(pieces)


def expand_blocks(mask):
    blocks_x, blocks_y, blocks_z = mask.shape
    grown = jnp.broadcast_to(
        mask[:, None, :, None, :, None], (blocks_x, 4, blocks_y, 4, blocks_z, 4)
    )
    return grown.reshape(blocks_x * 4, blocks_y * 4, blocks_z * 4)


def children_sum(populations):
    depth, extent_x, extent_y, extent_z = populations.shape
    grouped = populations.reshape(depth, extent_x // 2, 2, extent_y // 2, 2, extent_z // 2, 2).sum(
        axis=(2, 4, 6)
    )
    return jnp.transpose(grouped, (0, 3, 2, 1))


def fine_substep(populations, live, fluid, kernel):
    post = collide(populations, kernel)
    source = jnp.where(live[None], post, populations)
    stacked = jnp.concatenate([source, fluid[None]], axis=0)
    padded = extended(stacked, (("wide", 1), ("quad", 2)), 1)
    padded = jnp.pad(padded, ((0, 0), (0, 0), (0, 0), (1, 1)))
    moved = stream(padded, post, (0, 1, 2))
    return jnp.where(live[None], moved, populations)


def send_children(populations):
    return lax.all_to_all(
        children_sum(populations), "wide", split_axis=1, concat_axis=3, tiled=True
    )


def shards(fine_pops, coarse_pops, fine_solid, coarse_solid, fine_active, coarse_covered, rates):
    zeros_four = jnp.zeros((4,), jnp.float32)
    fine_kernel = make_kernel(jnp.concatenate([zeros_four, rates]))
    coarse_kernel = make_kernel(jnp.concatenate([zeros_four, 1.0 / (2.0 / rates - 0.5)]))
    fluid_fine = fine_solid == 0
    live_fine = (expand_blocks(fine_active) == 1) & fluid_fine
    fluid_fine_value = fluid_fine.astype(jnp.float32)
    first = fine_substep(fine_pops, live_fine, fluid_fine_value, fine_kernel)
    first_sums = send_children(first)
    fine_out = fine_substep(first, live_fine, fluid_fine_value, fine_kernel)
    second_sums = send_children(fine_out)
    restricted = (first_sums + second_sums) * 0.0625
    coarse_pre = jnp.where(coarse_covered[None] == 1, restricted, coarse_pops)
    live_coarse = coarse_solid == 0
    post = collide(coarse_pre, coarse_kernel)
    source = jnp.where(live_coarse[None], post, coarse_pre)
    stacked = jnp.concatenate([source, live_coarse.astype(jnp.float32)[None]], axis=0)
    padded = extended(stacked, (("wide", 1), ("quad", 2)), 1)
    padded = jnp.pad(padded, ((0, 0), (0, 0), (0, 0), (1, 1)))
    moved = stream(padded, post, (2, 1, 0))
    coarse_out = jnp.where(live_coarse[None], moved, coarse_pre)
    return (fine_out, coarse_out)


def solution(mesh):
    in_specs = (
        P(None, "wide", "quad", None),
        P(None, "wide", "quad", None),
        P("wide", "quad", None),
        P("wide", "quad", None),
        P("wide", "quad", None),
        P("wide", "quad", None),
        P(),
    )
    out_specs = (P(None, "wide", "quad", None), P(None, "wide", "quad", None))
    return jax.shard_map(shards, mesh=mesh, in_specs=in_specs, out_specs=out_specs, check_vma=False)
```

profile of v0, /device:TPU:18, one launch (start us, length us, event | category | flops | bytes accessed | tf_op | source)
XLA Modules:
  0.0 211.0 jit_solution(7992019591359151614)
XLA Ops:
  0.6 0.9 broadcast_compare_fusion.3
  1.5 0.7 concatenate.105
  2.2 1.9 reduce_sum.72
  4.1 0.9 convert_bitcast_fusion
  5.1 1.3 broadcast_in_dim.39
  6.4 4.9 %eq.31 = pred[8,32,128]{2,1,0:T(8,128)(4,1)S(1)} reshape(pred[2,4,8,4,32,4]{5,4,3,2,1,0:T(8,128)(4,1)} %broadcast_in_dim.39) | data formatting | bytes 65536 | tf_op jit(solution)/shard_map/eq | solution.py:203
  11.6 1.8 copy.99
  13.5 2.0 multiply_reduce_fusion.1
  15.5 2.6 %fusion.180 = f32[19,32768]{1,0:T(8,128)S(1)} fusion(f32[19,3]{1,0:T(8,128)S(1)} %copy-done.22, f32[3,32768]{1,0:T(4,128)S(1)} %get-tuple-element.92), kind=kOutput, calls=%fused_computation.380 | convolution fusion | flops 22413312 | bytes 2883812 | tf_op jit(solution)/shard_map/dot_general | solution.py:133
  18.3 3.7 %convolution_subtract_fusion.1 = f32[19,32768]{1,0:T(8,128)S(1)} fusion(f32[19,32768]{1,0:T(8,128)S(1)} %bitcast.144, f32[19,19]{1,0:T(8,128)S(1)} %fusion.160, f32[19,32768]{1,0:T(8,128)S(1)} %fusion.180, f32[32768]{0:T(1024)S(1)} %broadcast_multiply_fusion.1, f32[32768]{0:T(1024)S(1)} %bitcast.165, f32[19]{0:T(128)S(1)} %copy-done.27), kind=kOutput, calls=%fused_computation.41 | convolution fusion | flops 148176896 | bytes 7734768 | tf_op jit(solution)/shard_map/dot_general | solution.py:145
  23.5 5.4 %collective-permute-start.1 = (f32[20,1,32,128]{3,2,1,0:T(8,128)S(1)}, f32[20,1,32,128]{3,2,1,0:T(8,128)S(1)}, u32[]{:S(2)}, u32[]{:S(2)}) collective-permute-start(f32[20,1,32,128]{3,2,1,0:T(8,128)S(1)} %get-tuple-element.66), channel_id=1, source_target_pairs={{4,0},{8,4},{12,8},{16,12},{20,16},{24,20},{28,24},{32,28},{36,32}... | collective-permute-start | bytes 983048 | tf_op jit(solution)/shard_map/ppermute | solution.py:60
  28.9 1.9 collective-permute-start
  30.8 2.4 %fusion.178 = (f32[1,32768]{1,0:T(1,128)S(1)}, f32[1,32768]{1,0:T(1,128)S(1)}, f32[1,32768]{1,0:T(1,128)S(1)}, f32[1,32768]{1,0:T(1,128)S(1)}, f32[1,32768]{1,0:...) fusion(f32[19,32768]{1,0:T(8,128)S(1)} %convolution_subtract_fu, ...), kind=kLoop, calls=%fused_computation.376 | loop fusion | bytes 4980736 | tf_op jit(solution)/shard_map/slice | solution.py:162
  33.5 5.9 %collective-permute-done = f32[20,1,32,128]{3,2,1,0:T(8,128)S(1)} collective-permute-done((f32[20,1,32,128]{3,2,1,0:T(8,128)S(1)}, f32[20,1,32,128]{3,2,1,0:T(8,128)S(1)}, u32[]{:S(2)}, u32[]{:S(2)}) %collective-permute-start) | collective-permute-done | bytes 327712 | tf_op jit(solution)/shard_map/ppermute | solution.py:59
  40.0 2.4 %collective-permute-start.3 = (f32[20,10,1,128]{3,2,1,0:T(1,128)S(1)}, f32[20,10,1,128]{3,2,1,0:T(1,128)S(1)}, u32[]{:S(2)}, u32[]{:S(2)}) collective-permute-start(f32[20,10,1,128]{3,2,1,0:T(1,128)S(1)} %get-tuple-element.20), channel_id=1, source_target_pairs={{1,0},{2,1},{3,2},{5,4},{6,5},{7,6},{9,8},{10,9},{11,10},{13,12},{... | collective-permute-start | bytes 307208 | tf_op jit(solution)/shard_map/ppermute | solution.py:60
  42.4 3.5 %collective-permute-start.2 = (f32[20,10,1,128]{3,2,1,0:T(1,128)S(1)}, f32[20,10,1,128]{3,2,1,0:T(1,128)S(1)}, u32[]{:S(2)}, u32[]{:S(2)}) collective-permute-start(f32[20,10,1,128]{3,2,1,0:T(1,128)S(1)} %get-tuple-element.21), channel_id=1, source_target_pairs={{0,1},{1,2},{2,3},{4,5},{5,6},{6,7},{8,9},{9,10},{10,11},{12,13},{... | collective-permute-start | bytes 307208 | tf_op jit(solution)/shard_map/ppermute | solution.py:59
  45.9 0.9 fusion.40
  46.8 2.1 collective-permute-done.2
  48.9 1.5 fusion.10
  50.5 1.3 fusion.3
  54.3 1.8 copy.101
  56.1 2.5 %multiply_reduce_fusion = (f32[32768]{0:T(1024)S(1)}, f32[32768,3]{0,1:T(4,128)S(1)}) fusion(f32[32768]{0:T(1024)S(1)} %bitcast.186, f32[19,32768]{1,0:T(8,128)S(1)} %bitcast.145, f32[3,19]{1,0:T(4,128)S(1)} %copy-done.29), kind=kOutput, calls=%fused_computation.131 | convolution fusion | flops 22675456 | bytes 3145956 | tf_op jit(solution)/shard_map/dot_general | solution.py:125
  58.6 2.7 %fusion.181 = f32[19,32768]{1,0:T(8,128)S(1)} fusion(f32[19,3]{1,0:T(8,128)S(1)} %copy-done.22, f32[32768,3]{0,1:T(4,128)S(1)} %get-tuple-element.94), kind=kOutput, calls=%fused_computation.381 | convolution fusion | flops 22413312 | bytes 2883812 | tf_op jit(solution)/shard_map/dot_general | solution.py:133
  61.3 3.8 %convolution_subtract_fusion = f32[19,32768]{1,0:T(8,128)S(1)} fusion(f32[19,32768]{1,0:T(8,128)S(1)} %bitcast.146, f32[19,19]{1,0:T(8,128)S(1)} %fusion.160, f32[19,32768]{1,0:T(8,128)S(1)} %fusion.181, f32[32768]{0:T(1024)S(1)} %broadcast_multiply_fusion, f32[32768]{0:T(1024)S(1)} %bitcast.187, f32[19]{0:T(128)S(1)} %copy-done.27), kind=kOutput, calls=%fused_computation.40 | convolution fusion | flops 148176896 | bytes 7734768 | tf_op jit(solution)/shard_map/dot_general | solution.py:145
  66.4 0.9 pad_maximum_fusion.12
  67.3 1.9 collective-permute-start.5
  69.3 2.4 %collective-permute-start.4 = (f32[20,1,32,128]{3,2,1,0:T(8,128)}, f32[20,1,32,128]{3,2,1,0:T(8,128)S(1)}, u32[]{:S(2)}, u32[]{:S(2)}) collective-permute-start(f32[20,1,32,128]{3,2,1,0:T(8,128)} %get-tuple-element.63), channel_id=1, source_target_pairs={{0,4},{4,8},{8,12},{12,16},{16,20},{20,24},{24,28},{28,32},{32,36}... | collective-permute-start | bytes 983048 | tf_op jit(solution)/shard_map/ppermute | solution.py:59
  71.7 2.8 %fusion.177 = (f32[1,32768]{1,0:T(1,128)S(1)}, f32[1,32768]{1,0:T(1,128)}, f32[1,32768]{1,0:T(1,128)}, f32[1,32768]{1,0:T(1,128)}, f32[1,32768]{1,0:T(1,128)}, /...) fusion(f32[19,32768]{1,0:T(8,128)S(1)} %convolution_subtract_fusion), kind=kLoop, calls=%fused_computation.375 | loop fusion | bytes 4980736 | tf_op jit(solution)/shard_map/slice | solution.py:162
  74.5 10.3 %copy.93 = f32[19,8,32,128]{0,3,2,1:T(8,128)} copy(f32[19,8,32,128]{3,2,1,0:T(8,128)} %copy-done) | data formatting | bytes 4980736 | tf_op jit(solution)/shard_map/jit(_where)/select_n | solution.py:189
  84.8 13.1 %reduce_sum.76 = f32[19,4,16,64]{0,3,2,1:T(8,128)} reduce(f32[19,4,2,16,2,64,2]{0,6,5,4,3,2,1:T(2,128)} %bitcast.135, f32[]{:T(128)} %constant.19.clone.1), dimensions={2,4,6}, to_apply=%region_4.5 | reduce | flops 544768 | bytes 2801668 | tf_op jit(solution)/shard_map/reduce_sum | solution.py:176
  97.8 4.1 %copy.108 = f32[19,64,16,4]{0,2,3,1:T(8,128)} copy(f32[19,64,16,4]{0,1,2,3:T(8,128)} %bitcast.155) | data formatting | bytes 622592 | tf_op jit(solution)/shard_map/transpose | solution.py:179
  102.0 4.0 %reshape.249 = f32[32,1,2432]{2,1,0:T(1,128)} reshape(f32[64,4,16,19]{3,2,1,0:T(8,128)} %bitcast.152) | data formatting | bytes 622592
  106.0 7.9 %all-to-all-start = ((f32[32,1,2432]{2,1,0:T(1,128)}), f32[32,1,2432]{2,1,0:T(1,128)}, u32[]{:S(2)}, u32[]{:S(2)}) async-start(f32[32,1,2432]{2,1,0:T(1,128)} %reshape.249), calls=%async_computation | async-start | bytes 622592 | tf_op jit(solution)/shard_map/all_to_all | solution.py:193
  113.9 0.9 fusion.122
  115.3 2.4 %collective-permute-start.7 = (f32[20,10,1,128]{3,2,1,0:T(1,128)S(1)}, f32[20,10,1,128]{3,2,1,0:T(1,128)S(1)}, u32[]{:S(2)}, u32[]{:S(2)}) collective-permute-start(f32[20,10,1,128]{3,2,1,0:T(1,128)S(1)} %get-tuple-element.16), channel_id=1, source_target_pairs={{1,0},{2,1},{3,2},{5,4},{6,5},{7,6},{9,8},{10,9},{11,10},{13,12},{... | collective-permute-start | bytes 307208 | tf_op jit(solution)/shard_map/ppermute | solution.py:60
  117.7 3.6 %collective-permute-start.6 = (f32[20,10,1,128]{3,2,1,0:T(1,128)S(1)}, f32[20,10,1,128]{3,2,1,0:T(1,128)S(1)}, u32[]{:S(2)}, u32[]{:S(2)}) collective-permute-start(f32[20,10,1,128]{3,2,1,0:T(1,128)S(1)} %get-tuple-element.17), channel_id=1, source_target_pairs={{0,1},{1,2},{2,3},{4,5},{5,6},{6,7},{8,9},{9,10},{10,11},{12,13},{... | collective-permute-start | bytes 307208 | tf_op jit(solution)/shard_map/ppermute | solution.py:59
  121.4 0.7 fusion.41
  122.2 2.2 %collective-permute-done.6 = f32[20,10,1,128]{3,2,1,0:T(1,128)S(1)} collective-permute-done((f32[20,10,1,128]{3,2,1,0:T(1,128)S(1)}, f32[20,10,1,128]{3,2,1,0:T(1,128)S(1)}, u32[]{:S(2)}, u32[]{:S(2)}) %collective-permute-start.6) | collective-permute-done | bytes 102432 | tf_op jit(solution)/shard_map/ppermute | solution.py:59
  124.4 1.7 fusion.13
  126.2 1.3 fusion.7
  129.8 0.7 copy-done.8
  131.9 0.7 copy-done.4
  132.9 1.6 copy-done.1
  135.1 8.9 %copy.95 = f32[19,8,32,128]{0,3,2,1:T(8,128)} copy(f32[19,8,32,128]{3,2,1,0:T(8,128)S(1)} %broadcast_select_fusion) | data formatting | bytes 4980736 | tf_op jit(solution)/shard_map/jit(_where)/select_n | solution.py:189
  144.0 13.1 %reduce_sum.77 = f32[19,4,16,64]{0,3,2,1:T(8,128)} reduce(f32[19,4,2,16,2,64,2]{0,6,5,4,3,2,1:T(2,128)} %bitcast.136, f32[]{:T(128)} %constant.19.clone.1), dimensions={2,4,6}, to_apply=%region_5.6 | reduce | flops 544768 | bytes 2801668 | tf_op jit(solution)/shard_map/reduce_sum | solution.py:176
  157.1 2.8 %copy.107 = f32[19,64,16,4]{0,2,3,1:T(8,128)S(1)} copy(f32[19,64,16,4]{0,1,2,3:T(8,128)} %bitcast.156) | data formatting | bytes 622592 | tf_op jit(solution)/shard_map/transpose | solution.py:179
  159.9 2.6 %reshape.251 = f32[32,1,2432]{2,1,0:T(1,128)} reshape(f32[64,4,16,19]{3,2,1,0:T(8,128)S(1)} %bitcast.153) | data formatting | bytes 622592
  162.6 7.7 %all-to-all-start.1 = ((f32[32,1,2432]{2,1,0:T(1,128)}), f32[32,1,2432]{2,1,0:T(1,128)S(1)}, u32[]{:S(2)}, u32[]{:S(2)}) async-start(f32[32,1,2432]{2,1,0:T(1,128)} %reshape.251), calls=%async_computation.1 | async-start | bytes 622592 | tf_op jit(solution)/shard_map/all_to_all | solution.py:193
  171.1 2.4 %reduce.6 = f32[32,2432]{1,0:T(8,128)S(1)} reduce(f32[32,1,2432]{2,1,0:T(1,128)} %all-to-all-done, f32[]{:T(128)} %broadcast.260), dimensions={1}, to_apply=%all_to_all.4.reduce_sub_computation | reduce | bytes 622596 | tf_op jit(solution)/shard_map/all_to_all | solution.py:193
  173.5 2.3 %reshape.250 = f32[64,4,16,19]{3,2,1,0:T(8,128)S(1)} reshape(f32[32,2432]{1,0:T(8,128)S(1)} %reduce.6) | data formatting | bytes 622592
  175.8 2.5 %all-to-all-done.1 = f32[32,1,2432]{2,1,0:T(1,128)S(1)} async-done(((f32[32,1,2432]{2,1,0:T(1,128)}), f32[32,1,2432]{2,1,0:T(1,128)S(1)}, u32[]{:S(2)}, u32[]{:S(2)}) %all-to-all-start.1) | async-done | bytes 311328 | tf_op jit(solution)/shard_map/all_to_all | solution.py:193
  178.3 1.4 reduce.5
  179.7 3.6 %reshape.252 = f32[64,4,16,19]{3,2,1,0:T(8,128)} reshape(f32[32,2432]{1,0:T(8,128)S(1)} %reduce.5) | data formatting | bytes 622592
  183.3 2.0 add_multiply_fusion
  185.6 0.9 copy.98
  188.5 2.3 %collective-permute-start.8 = (f32[20,1,16,128]{3,2,1,0:T(8,128)S(1)}, f32[20,1,16,128]{3,2,1,0:T(8,128)S(1)}, u32[]{:S(2)}, u32[]{:S(2)}) collective-permute-start(f32[20,1,16,128]{3,2,1,0:T(8,128)S(1)} %get-tuple-element.89), channel_id=1, source_target_pairs={{0,4},{4,8},{8,12},{12,16},{16,20},{20,24},{24,28},{28,32},{32,36}... | collective-permute-start | bytes 491528 | tf_op jit(solution)/shard_map/ppermute | solution.py:59
  190.8 5.4 %collective-permute-start.9 = (f32[20,1,16,128]{3,2,1,0:T(8,128)S(1)}, f32[20,1,16,128]{3,2,1,0:T(8,128)S(1)}, u32[]{:S(2)}, u32[]{:S(2)}) collective-permute-start(f32[20,1,16,128]{3,2,1,0:T(8,128)S(1)} %get-tuple-element.90), channel_id=1, source_target_pairs={{4,0},{8,4},{12,8},{16,12},{20,16},{24,20},{28,24},{32,28},{36,32}... | collective-permute-start | bytes 491528 | tf_op jit(solution)/shard_map/ppermute | solution.py:60
  196.4 0.8 collective-permute-done.8
  197.3 1.8 collective-permute-done.9
  199.1 3.5 %collective-permute-start.10 = (f32[20,4,1,128]{3,2,1,0:T(1,128)S(1)}, f32[20,4,1,128]{3,2,1,0:T(1,128)S(1)}, u32[]{:S(2)}, u32[]{:S(2)}) collective-permute-start(f32[20,4,1,128]{3,2,1,0:T(1,128)S(1)} %get-tuple-element.68), channel_id=1, source_target_pairs={{0,1},{1,2},{2,3},{4,5},{5,6},{6,7},{8,9},{9,10},{10,11},{12,13},{... | collective-permute-start | bytes 122888 | tf_op jit(solution)/shard_map/ppermute | solution.py:59
  202.6 2.4 %collective-permute-start.11 = (f32[20,4,1,128]{3,2,1,0:T(1,128)S(1)}, f32[20,4,1,128]{3,2,1,0:T(1,128)S(1)}, u32[]{:S(2)}, u32[]{:S(2)}) collective-permute-start(f32[20,4,1,128]{3,2,1,0:T(1,128)S(1)} %get-tuple-element.69), channel_id=1, source_target_pairs={{1,0},{2,1},{3,2},{5,4},{6,5},{7,6},{9,8},{10,9},{11,10},{13,12},{... | collective-permute-start | bytes 122888 | tf_op jit(solution)/shard_map/ppermute | solution.py:60
  205.0 3.5 %collective-permute-done.11 = f32[20,4,1,128]{3,2,1,0:T(1,128)S(1)} collective-permute-done((f32[20,4,1,128]{3,2,1,0:T(1,128)S(1)}, f32[20,4,1,128]{3,2,1,0:T(1,128)S(1)}, u32[]{:S(2)}, u32[]{:S(2)}) %collective-permute-start.11) | collective-permute-done | bytes 40992 | tf_op jit(solution)/shard_map/ppermute | solution.py:60
  208.5 0.9 select_maximum_fusion
  210.0 0.8 broadcast_select_fusion.5
  (159 shorter events, 15.3 us)
Async XLA Ops:
  0.6 10.7 %copy-start.2 = (f32[19,8,32,128]{3,2,1,0:T(8,128)S(1)}, f32[19,8,32,128]{3,2,1,0:T(8,128)}, u32[]{:S(2)}) copy-start(f32[19,8,32,128]{3,2,1,0:T(8,128)} %param.20) | copy-start | bytes 7471108
  11.6 1.9 copy-start.29
  13.4 2.1 copy-start.22
  15.5 2.7 %copy-start.23 = (f32[19,19]{1,0:T(8,128)S(1)}, f32[19,19]{1,0:T(8,128)}, u32[]{:S(2)}) copy-start(f32[19,19]{1,0:T(8,128)} %constant.9.clone) | copy-start | bytes 4336
  15.5 2.7 %copy-start.24 = (f32[19,19]{1,0:T(8,128)S(1)}, f32[19,19]{1,0:T(8,128)}, u32[]{:S(2)}) copy-start(f32[19,19]{1,0:T(8,128)} %constant.8.clone) | copy-start | bytes 4336
  15.5 2.8 %copy-start.27 = (f32[19]{0:T(128)S(1)}, f32[19]{0:T(128)}, u32[]{:S(2)}) copy-start(f32[19]{0:T(128)} %constant.12.clone) | copy-start | bytes 232
  23.5 9.8 %copy-start.26 = (s32[2,16,128]{2,1,0:T(8,128)S(1)}, s32[2,16,128]{2,1,0:T(8,128)}, u32[]{:S(2)}) copy-start(s32[2,16,128]{2,1,0:T(8,128)} %param.23) | copy-start | bytes 49156
  23.5 9.8 %copy-start.25 = (s32[2,16,128]{2,1,0:T(8,128)S(1)}, s32[2,16,128]{2,1,0:T(8,128)}, u32[]{:S(2)}) copy-start(s32[2,16,128]{2,1,0:T(8,128)} %param.25) | copy-start | bytes 49156
  23.5 9.9 %collective-permute-start.1 = (f32[20,1,32,128]{3,2,1,0:T(8,128)S(1)}, f32[20,1,32,128]{3,2,1,0:T(8,128)S(1)}, u32[]{:S(2)}, u32[]{:S(2)}) collective-permute-start(f32[20,1,32,128]{3,2,1,0:T(8,128)S(1)} %get-tuple-element.66), channel_id=1, source_target_pairs={{4,0},{8,4},{12,8},{16,12},{20,16},{24,20},{28,24},{32,28},{36,32}... | collective-permute-start | bytes 983048 | tf_op jit(solution)/shard_map/ppermute | solution.py:60
  28.9 10.5 %collective-permute-start = (f32[20,1,32,128]{3,2,1,0:T(8,128)S(1)}, f32[20,1,32,128]{3,2,1,0:T(8,128)S(1)}, u32[]{:S(2)}, u32[]{:S(2)}) collective-permute-start(f32[20,1,32,128]{3,2,1,0:T(8,128)S(1)} %get-tuple-element.67), channel_id=1, source_target_pairs={{0,4},{4,8},{8,12},{12,16},{16,20},{20,24},{24,28},{28,32},{32,36}... | collective-permute-start | bytes 983048 | tf_op jit(solution)/shard_map/ppermute | solution.py:59
  40.0 6.8 %collective-permute-start.3 = (f32[20,10,1,128]{3,2,1,0:T(1,128)S(1)}, f32[20,10,1,128]{3,2,1,0:T(1,128)S(1)}, u32[]{:S(2)}, u32[]{:S(2)}) collective-permute-start(f32[20,10,1,128]{3,2,1,0:T(1,128)S(1)} %get-tuple-element.20), channel_id=1, source_target_pairs={{1,0},{2,1},{3,2},{5,4},{6,5},{7,6},{9,8},{10,9},{11,10},{13,12},{... | collective-permute-start | bytes 307208 | tf_op jit(solution)/shard_map/ppermute | solution.py:60
  42.4 6.6 %collective-permute-start.2 = (f32[20,10,1,128]{3,2,1,0:T(1,128)S(1)}, f32[20,10,1,128]{3,2,1,0:T(1,128)S(1)}, u32[]{:S(2)}, u32[]{:S(2)}) collective-permute-start(f32[20,10,1,128]{3,2,1,0:T(1,128)S(1)} %get-tuple-element.21), channel_id=1, source_target_pairs={{0,1},{1,2},{2,3},{4,5},{5,6},{6,7},{8,9},{9,10},{10,11},{12,13},{... | collective-permute-start | bytes 307208 | tf_op jit(solution)/shard_map/ppermute | solution.py:59
  53.9 11.9 %copy-start = (f32[19,8,32,128]{3,2,1,0:T(8,128)}, f32[19,8,32,128]{3,2,1,0:T(8,128)S(1)}, u32[]{:S(2)}) copy-start(f32[19,8,32,128]{3,2,1,0:T(8,128)S(1)} %get-tuple-element.11) | copy-start | bytes 7471108
  67.3 47.5 %collective-permute-start.5 = (f32[20,1,32,128]{3,2,1,0:T(8,128)}, f32[20,1,32,128]{3,2,1,0:T(8,128)S(1)}, u32[]{:S(2)}, u32[]{:S(2)}) collective-permute-start(f32[20,1,32,128]{3,2,1,0:T(8,128)} %get-tuple-element.62), channel_id=1, source_target_pairs={{4,0},{8,4},{12,8},{16,12},{20,16},{24,20},{28,24},{32,28},{36,32}... | collective-permute-start | bytes 983048 | tf_op jit(solution)/shard_map/ppermute | solution.py:60
  69.3 45.6 %collective-permute-start.4 = (f32[20,1,32,128]{3,2,1,0:T(8,128)}, f32[20,1,32,128]{3,2,1,0:T(8,128)S(1)}, u32[]{:S(2)}, u32[]{:S(2)}) collective-permute-start(f32[20,1,32,128]{3,2,1,0:T(8,128)} %get-tuple-element.63), channel_id=1, source_target_pairs={{0,4},{4,8},{8,12},{12,16},{16,20},{20,24},{24,28},{28,32},{32,36}... | collective-permute-start | bytes 983048 | tf_op jit(solution)/shard_map/ppermute | solution.py:59
  106.0 56.6 %all-to-all-start = ((f32[32,1,2432]{2,1,0:T(1,128)}), f32[32,1,2432]{2,1,0:T(1,128)}, u32[]{:S(2)}, u32[]{:S(2)}) async-start(f32[32,1,2432]{2,1,0:T(1,128)} %reshape.249), calls=%async_computation | async-start | bytes 622592 | tf_op jit(solution)/shard_map/all_to_all | solution.py:193
  115.3 6.9 %collective-permute-start.7 = (f32[20,10,1,128]{3,2,1,0:T(1,128)S(1)}, f32[20,10,1,128]{3,2,1,0:T(1,128)S(1)}, u32[]{:S(2)}, u32[]{:S(2)}) collective-permute-start(f32[20,10,1,128]{3,2,1,0:T(1,128)S(1)} %get-tuple-element.16), channel_id=1, source_target_pairs={{1,0},{2,1},{3,2},{5,4},{6,5},{7,6},{9,8},{10,9},{11,10},{13,12},{... | collective-permute-start | bytes 307208 | tf_op jit(solution)/shard_map/ppermute | solution.py:60
  117.7 4.4 %copy-start.20 = (f32[1,32768]{1,0:T(1,128)S(1)}, f32[1,32768]{1,0:T(1,128)}, u32[]{:S(2)}) copy-start(f32[1,32768]{1,0:T(1,128)} %get-tuple-element.39) | copy-start | bytes 393220
  117.7 4.4 %copy-start.19 = (f32[1,32768]{1,0:T(1,128)S(1)}, f32[1,32768]{1,0:T(1,128)}, u32[]{:S(2)}) copy-start(f32[1,32768]{1,0:T(1,128)} %get-tuple-element.38) | copy-start | bytes 393220
  117.7 6.7 %collective-permute-start.6 = (f32[20,10,1,128]{3,2,1,0:T(1,128)S(1)}, f32[20,10,1,128]{3,2,1,0:T(1,128)S(1)}, u32[]{:S(2)}, u32[]{:S(2)}) collective-permute-start(f32[20,10,1,128]{3,2,1,0:T(1,128)S(1)} %get-tuple-element.17), channel_id=1, source_target_pairs={{0,1},{1,2},{2,3},{4,5},{5,6},{6,7},{8,9},{9,10},{10,11},{12,13},{... | collective-permute-start | bytes 307208 | tf_op jit(solution)/shard_map/ppermute | solution.py:59
  122.2 3.9 %copy-start.18 = (f32[1,32768]{1,0:T(1,128)S(1)}, f32[1,32768]{1,0:T(1,128)}, u32[]{:S(2)}) copy-start(f32[1,32768]{1,0:T(1,128)} %get-tuple-element.37) | copy-start | bytes 393220
  122.2 3.9 %copy-start.17 = (f32[1,32768]{1,0:T(1,128)S(1)}, f32[1,32768]{1,0:T(1,128)}, u32[]{:S(2)}) copy-start(f32[1,32768]{1,0:T(1,128)} %get-tuple-element.36) | copy-start | bytes 393220
  126.2 1.3 copy-start.12
  127.5 0.9 copy-start.11
  127.7 0.9 copy-start.16
  127.7 1.0 copy-start.15
  127.7 1.0 copy-start.14
  128.4 1.0 copy-start.13
  128.4 1.0 copy-start.10
  128.7 0.9 copy-start.9
  129.6 0.9 copy-start.8
  129.8 0.9 copy-start.7
  130.6 0.9 copy-start.6
  130.8 0.9 copy-start.5
  131.7 0.9 copy-start.4
  132.7 1.7 copy-start.1
  135.1 9.0 %copy-start.3 = (f32[19,8,32,128]{3,2,1,0:T(8,128)}, f32[19,8,32,128]{3,2,1,0:T(8,128)S(1)}, u32[]{:S(2)}) copy-start(f32[19,8,32,128]{3,2,1,0:T(8,128)S(1)} %broadcast_select_fusion) | copy-start | bytes 7471108
  157.1 13.2 %copy-start.28 = (f32[15]{0:T(128)S(1)}, f32[15]{0:T(128)}, u32[]{:S(2)}) copy-start(f32[15]{0:T(128)} %param.26) | copy-start | bytes 184
  162.6 15.8 %all-to-all-start.1 = ((f32[32,1,2432]{2,1,0:T(1,128)}), f32[32,1,2432]{2,1,0:T(1,128)S(1)}, u32[]{:S(2)}, u32[]{:S(2)}) async-start(f32[32,1,2432]{2,1,0:T(1,128)} %reshape.251), calls=%async_computation.1 | async-start | bytes 622592 | tf_op jit(solution)/shard_map/all_to_all | solution.py:193
  185.3 1.2 copy-start.21
  188.5 8.7 %collective-permute-start.8 = (f32[20,1,16,128]{3,2,1,0:T(8,128)S(1)}, f32[20,1,16,128]{3,2,1,0:T(8,128)S(1)}, u32[]{:S(2)}, u32[]{:S(2)}) collective-permute-start(f32[20,1,16,128]{3,2,1,0:T(8,128)S(1)} %get-tuple-element.89), channel_id=1, source_target_pairs={{0,4},{4,8},{8,12},{12,16},{16,20},{20,24},{24,28},{28,32},{32,36}... | collective-permute-start | bytes 491528 | tf_op jit(solution)/shard_map/ppermute | solution.py:59
  190.8 8.2 %collective-permute-start.9 = (f32[20,1,16,128]{3,2,1,0:T(8,128)S(1)}, f32[20,1,16,128]{3,2,1,0:T(8,128)S(1)}, u32[]{:S(2)}, u32[]{:S(2)}) collective-permute-start(f32[20,1,16,128]{3,2,1,0:T(8,128)S(1)} %get-tuple-element.90), channel_id=1, source_target_pairs={{4,0},{8,4},{12,8},{16,12},{20,16},{24,20},{28,24},{32,28},{36,32}... | collective-permute-start | bytes 491528 | tf_op jit(solution)/shard_map/ppermute | solution.py:60
  199.1 5.9 %collective-permute-start.10 = (f32[20,4,1,128]{3,2,1,0:T(1,128)S(1)}, f32[20,4,1,128]{3,2,1,0:T(1,128)S(1)}, u32[]{:S(2)}, u32[]{:S(2)}) collective-permute-start(f32[20,4,1,128]{3,2,1,0:T(1,128)S(1)} %get-tuple-element.68), channel_id=1, source_target_pairs={{0,1},{1,2},{2,3},{4,5},{5,6},{6,7},{8,9},{9,10},{10,11},{12,13},{... | collective-permute-start | bytes 122888 | tf_op jit(solution)/shard_map/ppermute | solution.py:59
  202.6 5.9 %collective-permute-start.11 = (f32[20,4,1,128]{3,2,1,0:T(1,128)S(1)}, f32[20,4,1,128]{3,2,1,0:T(1,128)S(1)}, u32[]{:S(2)}, u32[]{:S(2)}) collective-permute-start(f32[20,4,1,128]{3,2,1,0:T(1,128)S(1)} %get-tuple-element.69), channel_id=1, source_target_pairs={{1,0},{2,1},{3,2},{5,4},{6,5},{7,6},{9,8},{10,9},{11,10},{13,12},{... | collective-permute-start | bytes 122888 | tf_op jit(solution)/shard_map/ppermute | solution.py:60
where the time goes:
time: 215 us; the launch traced here: 211 us
  local copies, waits for them, and re-layouts  64.8 us (30%)
  other arithmetic  53.7 us (25%)
  starting transfers between devices  52.5 us (24%)
  matrix products  18.9 us (9%)
  waiting for transfers between devices  18.9 us (9%)
  between operations  2.15 us (1%)
    reduce_sum x2, other arithmetic, children_sum(): populations.reshape(depth, extent_x // 2, 2, extent_y // 2, 2, extent_z /...  26.1 us
    unnamed x76, local copies, waits for them, and re-layouts  24 us
    ppermute x6, starting transfers between devices, extended(): after = lax.ppermute(first, axis, down)  19.7 us
    select_n x2, local copies, waits for them, and re-layouts, fine_substep(): return jnp.where(live[None], moved, populations)  19.2 us
    ppermute x6, starting transfers between devices, extended(): before = lax.ppermute(last, axis, up)  17.2 us
    all_to_all x2, starting transfers between devices, send_children(): lax.all_to_all(children_sum(populations), 'wide', split_axis=1, concat_ax...  15.6 us
    ppermute x6, waiting for transfers between devices, extended(): before = lax.ppermute(last, axis, up)  11.1 us
    concatenate x9, other arithmetic, extended(): shard = jnp.concatenate([before, shard, after], axis=dim)  9.11 us
  transfers between devices with their start and end apart: 14, of which 8 were waited for; matrix products, arithmetic and copies ran while one was open for 37% of the time, Pallas kernels for 0%

commit v1 on v0

v1 whole, which is shorter than its diff:
```python
import jax
import jax.numpy as jnp
from jax import lax
from jax.experimental import pallas as pl
from jax.experimental.pallas import tpu as pltpu
from jax.sharding import PartitionSpec as P

VEL = [
    (0, 0, 0),
    (1, 0, 0),
    (-1, 0, 0),
    (0, 1, 0),
    (0, -1, 0),
    (0, 0, 1),
    (0, 0, -1),
    (1, 1, 0),
    (-1, -1, 0),
    (1, -1, 0),
    (-1, 1, 0),
    (1, 0, 1),
    (-1, 0, -1),
    (1, 0, -1),
    (-1, 0, 1),
    (0, 1, 1),
    (0, -1, -1),
    (0, 1, -1),
    (0, -1, 1),
]
OPP = [0, 2, 1, 4, 3, 6, 5, 8, 7, 10, 9, 12, 11, 14, 13, 16, 15, 18, 17]


def moving(axis, sign):
    return [q for q in range(19) if VEL[q][axis] == sign]


XP, XM = moving(0, 1), moving(0, -1)
YP, YM = moving(1, 1), moving(1, -1)
ZP, ZM = moving(2, 1), moving(2, -1)
WALL = 1e30
WALL_TEST = 1e29
F32 = jnp.float32
MIB = 1 << 20

Y_FINE = 80
Y_TILES = Y_FINE + 2
X_FINE = 125
X_TILES = X_FINE + 13


def collide(f, rate):
    r_xy, r_xz, r_yz, r_xx, r_yy, r_zz = rate[:6]
    r_xyy, r_xzz, r_yxx, r_yzz, r_zxx, r_zyy, r_xxyy, r_xxzz, r_yyzz = rate[6:]
    sx, dx = f[1] + f[2], f[1] - f[2]
    sy, dy = f[3] + f[4], f[3] - f[4]
    sz, dz = f[5] + f[6], f[5] - f[6]

    def plane(i):
        a, b = f[i] + f[i + 1], f[i + 2] + f[i + 3]
        c, d = f[i] - f[i + 1], f[i + 2] - f[i + 3]
        return a + b, a - b, c + d, c - d

    m_xxyy, m_xy, m_xyy, m_yxx = plane(7)
    m_xxzz, m_xz, m_xzz, m_zxx = plane(11)
    m_yyzz, m_yz, m_yzz, m_zyy = plane(15)
    m_xx = sx + (m_xxyy + m_xxzz)
    m_yy = sy + (m_xxyy + m_yyzz)
    m_zz = sz + (m_xxzz + m_yyzz)
    jx = dx + (m_xyy + m_xzz)
    jy = dy + (m_yxx + m_yzz)
    jz = dz + (m_zxx + m_zyy)
    rho = (f[0] + sx) + (sy + sz) + ((m_xxyy + m_xxzz) + m_yyzz)
    inv = 1.0 / rho
    ux, uy, uz = jx * inv, jy * inv, jz * inv
    xx, yy, zz = jx * ux, jy * uy, jz * uz
    third = rho * (1.0 / 3.0)
    ninth = rho * (1.0 / 9.0)
    jx3, jy3, jz3 = jx * (1.0 / 3.0), jy * (1.0 / 3.0), jz * (1.0 / 3.0)
    xx3, yy3, zz3 = xx * (1.0 / 3.0), yy * (1.0 / 3.0), zz * (1.0 / 3.0)
    h_xx = (m_xx - third - xx) * r_xx
    h_yy = (m_yy - third - yy) * r_yy
    h_zz = (m_zz - third - zz) * r_zz
    post = [None] * 19

    def diagonal(i, fourth, cross, first, second):
        p, m = fourth + cross, fourth - cross
        s, d = first + second, first - second
        post[i] = f[i] - (p + s)
        post[i + 1] = f[i + 1] - (p - s)
        post[i + 2] = f[i + 2] - (m + d)
        post[i + 3] = f[i + 3] - (m - d)

    a_xy = (m_xxyy - ninth - (xx3 + yy3 - 0.5 * zz3)) * r_xxyy
    a_xz = (m_xxzz - ninth - (xx3 + zz3 - 0.5 * yy3)) * r_xxzz
    a_yz = (m_yyzz - ninth - (yy3 + zz3 - 0.5 * xx3)) * r_yyzz
    c_xyy, c_yxx = (m_xyy - jx3) * r_xyy, (m_yxx - jy3) * r_yxx
    c_xzz, c_zxx = (m_xzz - jx3) * r_xzz, (m_zxx - jz3) * r_zxx
    c_yzz, c_zyy = (m_yzz - jy3) * r_yzz, (m_zyy - jz3) * r_zyy
    diagonal(7, a_xy, (m_xy - jx * uy) * r_xy, c_xyy, c_yxx)
    diagonal(11, a_xz, (m_xz - jx * uz) * r_xz, c_xzz, c_zxx)
    diagonal(15, a_yz, (m_yz - jy * uz) * r_yz, c_yzz, c_zyy)

    def straight(i, h, a, c):
        p, n = h - 2.0 * a, 2.0 * c
        post[i] = f[i] - (p - n)
        post[i + 1] = f[i + 1] - (p + n)

    straight(1, h_xx, a_xy + a_xz, c_xyy + c_xzz)
    straight(3, h_yy, a_xy + a_yz, c_yxx + c_yzz)
    straight(5, h_zz, a_xz + a_yz, c_zxx + c_zyy)
    post[0] = f[0] + (2.0 * (h_xx + h_yy + h_zz) - 4.0 * (a_xy + a_xz + a_yz))
    return post


def scaled_rates(rates_ref, coarse):
    base = 15 if coarse else 0
    return [rates_ref[base + i] for i in range(15)]


def iota(shape, axis):
    return lax.broadcasted_iota(jnp.int32, shape, axis)


def wall_where(code, value):
    return jnp.where(code > 0.5, value, WALL)


def first_kernel(
    rates, f, solid, active, cp, c_solid, c_cov, src, xu, xd, yu, yd, zu, zd, act
):
    fine = scaled_rates(rates, False)
    coarse = scaled_rates(rates, True)
    grow_z = (iota((32, 128), 1) // 4 == iota((32, 128), 0)).astype(F32)
    grow_y = (iota((32, 8), 0) // 4 == iota((32, 8), 1)).astype(F32)
    for b in range(2):
        wide_z = jnp.dot(active[b].astype(F32), grow_z, preferred_element_type=F32)
        act[b] = jnp.dot(grow_y, wide_z, preferred_element_type=F32)

    def plane(x, carry):
        for t in range(4):
            rows = pl.ds(8 * t, 8)
            old = [f[q, x, rows] for q in range(19)]
            fluid = solid[x, rows] == 0
            on = act[x // 4, rows]
            live = fluid & (on > 0.5)
            post = collide(old, fine)
            for q in range(19):
                src[q, x, rows] = jnp.where(live, post[q], old[q])
            src[19, x, rows] = jnp.where(fluid, 1.0 + on, 0.0)
        for p in range(10):
            yu[8 * p + x, 0:4] = src[2 * p, x, 28:32]
            yu[8 * p + x, 4:8] = src[2 * p + 1, x, 28:32]
            yd[8 * p + x, 0:4] = src[2 * p, x, 0:4]
            yd[8 * p + x, 4:8] = src[2 * p + 1, x, 0:4]
        return carry

    lax.fori_loop(0, 8, plane, 0)
    for q in range(20):
        xu[q] = src[q, 7]
        xd[q] = src[q, 0]
    for i in range(5):
        xu[20 + i] = wall_where(src[19, 6], src[XP[i], 6])
        xd[20 + i] = wall_where(src[19, 1], src[XM[i], 1])

    for z in range(2):
        for t in range(2):
            rows = pl.ds(8 * t, 8)
            post = collide([cp[q, z, rows] for q in range(19)], coarse)
            code = jnp.where(c_solid[z, rows] == 0, 1.0 + c_cov[z, rows].astype(F32), 0.0)
            values, to = (ZP, zu) if z == 1 else (ZM, zd)
            for i in range(5):
                to[i, rows] = post[values[i]]
            to[5, rows] = code
            values, to, row = (YM, yd, 0) if t == 0 else (YP, yu, 7)
            for i in range(6):
                place = 6 * z + i
                value = code if i == 5 else post[values[i]]
                to[Y_FINE + place // 8, place % 8 : place % 8 + 1] = value[row : row + 1]


def halo_tile(q, x, ru, rd, sub):
    place = 8 * (q // 2) + x
    low, high = rd[place], ru[place]
    if q % 2 == 0:
        high = pltpu.roll(high, 4, 0)
    else:
        low = pltpu.roll(low, 4, 0)
    return jnp.where(sub < 4, low, high)


def halo_code(x, ru, rd, sub, has_prev, has_next):
    inside = jnp.where(sub < 4, has_next, has_prev)
    return halo_tile(19, x, ru, rd, sub) * inside


def edges():
    quad, wide = lax.axis_index("quad"), lax.axis_index("wide")
    return (
        (quad > 0).astype(F32),
        (quad < lax.axis_size("quad") - 1).astype(F32),
        (wide > 0).astype(F32),
        (wide < lax.axis_size("wide") - 1).astype(F32),
    )


def second_kernel(xu, xd, zu, zd, ru, rd, pu, pd):
    has_prev, has_next, _, _ = edges()
    sub = iota((8, 128), 0)
    for face, out, near, far, values in ((xu, pu, 7, 6, XP), (xd, pd, 0, 1, XM)):
        far_code = halo_code(far, ru, rd, sub, has_prev, has_next)
        for i in range(25):
            for t in range(4):
                out[5 * i + t] = face[i, 8 * t : 8 * t + 8]
            if i < 19:
                tile = halo_tile(i, near, ru, rd, sub)
            elif i == 19:
                tile = halo_code(near, ru, rd, sub, has_prev, has_next)
            else:
                tile = wall_where(far_code, halo_tile(values[i - 20], far, ru, rd, sub))
            out[5 * i + 4] = tile
    for face, out, z, up, down in ((zu, pu, 1, 15, 18), (zd, pd, 0, 17, 16)):
        for i in range(6):
            for t in range(2):
                out[X_FINE + 2 * i + t] = face[i, 8 * t : 8 * t + 8]

        def arrived(from_, place):
            return from_[Y_FINE + place // 8, place % 8 : place % 8 + 1]

        last = X_FINE + 12
        out[last] = jnp.zeros((8, 128), F32)
        out[last, 0:1] = arrived(ru, 6 * z + YP.index(up))
        out[last, 1:2] = arrived(rd, 6 * z + YM.index(down))
        out[last, 2:3] = arrived(ru, 6 * z + 5) * has_prev
        out[last, 3:4] = arrived(rd, 6 * z + 5) * has_next


def streamed(q, x, walled, source, live, lane):
    cx, cy, cz = VEL[q]
    if q == 0:
        return source[0, x]
    value = walled[q, x - cx]
    rows = value.shape[0]
    if cy:
        value = pltpu.roll(value, cy % rows, 0)
    if cz:
        value = pltpu.roll(value, cz % 128, 1)
    open_ = value < WALL_TEST
    if cz:
        open_ = open_ & (lane != (0 if cz == 1 else 127))
    return jnp.where(live, jnp.where(open_, value, source[OPP[q], x]), source[q, x])


def third_kernel(
    rates, src, ru, rd, rxu, rxd, fine_out, send, ext, walled, first, ext2, walled2, sums, raw, up, down
):
    has_prev, has_next, has_left, has_right = edges()
    fine = scaled_rates(rates, False)
    coarse = scaled_rates(rates, True)
    sub = iota((8, 128), 0)
    lane = iota((40, 128), 1)

    def own(x, carry):
        code_halo = halo_code(x, ru, rd, sub, has_prev, has_next)
        ext[19, x + 2, 0:32] = src[19, x]
        ext[19, x + 2, 32:40] = code_halo
        for q in range(19):
            tile = halo_tile(q, x, ru, rd, sub)
            ext[q, x + 2, 0:32] = src[q, x]
            ext[q, x + 2, 32:40] = tile
            walled[q, x + 2, 0:32] = wall_where(src[19, x], src[q, x])
            walled[q, x + 2, 32:40] = wall_where(code_halo, tile)
        return carry

    lax.fori_loop(0, 8, own, 0)
    for from_, near, far, values, inside in ((rxu, 1, 0, XP, has_left), (rxd, 10, 11, XM, has_right)):
        for t in range(5):
            rows = pl.ds(8 * t, 8)
            code = from_[5 * 19 + t] * inside
            ext[19, near, rows] = code
            for q in range(19):
                tile = from_[5 * q + t]
                ext[q, near, rows] = tile
                walled[q, near, rows] = wall_where(code, tile)
            for i in range(5):
                tile = from_[5 * (20 + i) + t]
                walled[values[i], far, rows] = jnp.where(inside > 0.5, tile, WALL)

    def substep_one(x, carry):
        live = ext[19, x] > 1.5
        for q in range(19):
            first[q, x] = streamed(q, x, walled, ext, live, lane)
        for t in range(5):
            rows = pl.ds(8 * t, 8)
            code = ext[19, x, rows]
            live_t = code > 1.5
            old = [first[q, x, rows] for q in range(19)]
            post = collide(old, fine)
            for q in range(19):
                value = jnp.where(live_t, post[q], old[q])
                ext2[q, x, rows] = value
                walled2[q, x, rows] = wall_where(code, value)
        return carry

    lax.fori_loop(1, 11, substep_one, 0)

    def substep_two(b, carry):
        x = 2 + 2 * b
        lives = [ext[19, x + e] > 1.5 for e in range(2)]
        for q in range(19):
            total = None
            for e in range(2):
                value = streamed(q, x + e, walled2, ext2, lives[e], lane)
                fine_out[q, 2 * b + e] = value[0:32]
                value = value + first[q, x + e]
                total = value if total is None else total + value
            sums[b, 40 * q : 40 * q + 40] = total
        return carry

    lax.fori_loop(0, 4, substep_two, 0)

    def taken(k, rows_):
        return 2 * iota((rows_, 128), 0) + (k - 1)

    z_lane = iota((32, 128), 1)
    own_1 = jnp.where(z_lane // 2 == taken(1, 32), 0.0625, 0.0)
    own_2 = jnp.where(z_lane // 2 == taken(2, 32), 0.0625, 0.0)
    own_rows = jnp.concatenate([own_1, own_2], axis=0)
    before = (z_lane == 2 * taken(0, 32)).astype(F32)
    after = (z_lane == 2 * taken(3, 32)).astype(F32)
    even = iota((8, 128), 1) % 2 == 0
    raw[...] = jnp.zeros(raw.shape, F32)
    up[...] = jnp.zeros(up.shape, F32)
    down[...] = jnp.zeros(down.shape, F32)
    dims = (((1,), (1,)), ((), ()))

    def block(b, carry):
        for t in range(3):
            cells = []
            for q in range(19):
                start = 40 * q + 16 * t
                value = sums[b, pl.ds(start, 8, stride=2)] + sums[b, pl.ds(start + 1, 8, stride=2)]
                if t < 2:
                    raw[16 * q + 8 * t : 16 * q + 8 * t + 8] = value
                cells.append((value + pltpu.roll(value, 127, 1)) * 0.0625)
            post = collide(cells, coarse)
            if t < 2:
                for i in range(5):
                    up[16 * i + 8 * t : 16 * i + 8 * t + 8] = post[ZP[i]]
                    down[16 * i + 8 * t : 16 * i + 8 * t + 8] = post[ZM[i]]
            else:
                for i in range(5):
                    prev = jnp.where(even, 16.0 * post[YP[i]], 0.0)
                    next_ = jnp.where(even, 16.0 * post[YM[i]], 0.0)
                    raw[304 + i : 305 + i] = prev[3:4]
                    raw[309 + i : 310 + i] = next_[0:1]
                up[80:81] = post[15][3:4]
                up[81:82] = post[18][0:1]
                down[80:81] = post[17][3:4]
                down[81:82] = post[16][0:1]
        for n in range(3):
            got = lax.dot_general(
                own_rows,
                raw[128 * n : 128 * n + 128],
                dims,
                precision=lax.Precision.HIGHEST,
                preferred_element_type=F32,
            )
            for k in range(2):
                send[pl.ds(8 * b + 2 * n + k, 32, stride=32)] = got[32 * k : 32 * k + 32]
        for k, (rows_, ref) in enumerate(((before, up), (after, down))):
            got = lax.dot_general(
                rows_,
                ref[...],
                dims,
                precision=lax.Precision.HIGHEST,
                preferred_element_type=F32,
            )
            send[pl.ds(8 * b + 6 + k, 32, stride=32)] = got
        return carry

    lax.fori_loop(0, 4, block, 0)


def fourth_kernel(
    rates, got, cp, c_solid, c_cov, ru, rd, rxu, rxd, out, turned, pre, walled, source
):
    has_prev, has_next, has_left, has_right = edges()
    coarse = scaled_rates(rates, True)
    for k in range(2):
        for n in range(4):
            turned[k, 128 * n : 128 * n + 128] = got[pl.ds(2 * n + k, 128, stride=8)].T

    def pick(code, here, there):
        return jnp.where(code > 1.5, here, jnp.where(code > 0.5, there, WALL))

    def arrived(from_, place):
        return from_[place // 8, place % 8 : place % 8 + 1]

    for k in range(2):
        for t in range(2):
            rows = pl.ds(8 * t, 8)
            fluid = c_solid[k, rows] == 0
            covered = c_cov[k, rows] == 1
            old = []
            for q in range(19):
                start = 16 * q + 8 * t
                old.append(jnp.where(covered, turned[k, start : start + 8], cp[q, k, rows]))
            post = collide(old, coarse)
            for q in range(19):
                value = jnp.where(fluid, post[q], old[q])
                source[q, k + 1, rows] = value
                walled[q, k + 1, rows] = jnp.where(fluid, value, WALL)
        prev_code = arrived(ru, 6 * k + 5) * has_prev
        next_code = arrived(rd, 6 * k + 5) * has_next
        for i in range(5):
            walled[YP[i], k + 1, 23:24] = pick(
                prev_code, turned[k, 304 + i : 305 + i], arrived(ru, 6 * k + i)
            )
            walled[YM[i], k + 1, 16:17] = pick(
                next_code, turned[k, 309 + i : 310 + i], arrived(rd, 6 * k + i)
            )
        values, from_, z, inside = ((ZP, rxu, 0, has_left), (ZM, rxd, 3, has_right))[k]
        prev_q, next_q = ((15, 18), (17, 16))[k]
        for t in range(2):
            code = from_[10 + t] * inside
            for i in range(5):
                start = 384 + 16 * i + 8 * t
                walled[values[i], z, 8 * t : 8 * t + 8] = pick(
                    code, turned[k, start : start + 8], from_[2 * i + t]
                )
        walled[prev_q, z, 23:24] = pick(
            from_[12, 2:3] * inside, turned[k, 464:465], from_[12, 0:1]
        )
        walled[next_q, z, 16:17] = pick(
            from_[12, 3:4] * inside, turned[k, 465:466], from_[12, 1:2]
        )

    lane = iota((16, 128), 1)
    for z in (1, 2):
        fluid = c_solid[z - 1] == 0
        for q in range(19):
            cx, cy, cz = VEL[q]
            value = walled[q, z - cz]
            if cy:
                value = pltpu.roll(value, cy % 24, 0)
            value = value[0:16]
            if cx:
                value = pltpu.roll(value, cx % 128, 1)
            open_ = value < WALL_TEST
            if cx:
                open_ = open_ & (lane != (0 if cx == 1 else 127))
            bounced = jnp.where(open_, value, source[OPP[q], z, 0:16])
            out[q, z - 1] = jnp.where(fluid, bounced, source[q, z, 0:16])


def shape(*dims):
    return jax.ShapeDtypeStruct(dims, F32)


def call(kernel, name, out_shape, n_vmem, scratch, smem=True):
    spec = pl.BlockSpec(memory_space=pltpu.VMEM)
    in_specs = ([pl.BlockSpec(memory_space=pltpu.SMEM)] if smem else []) + [spec] * n_vmem
    return pl.pallas_call(
        kernel,
        out_shape=out_shape,
        in_specs=in_specs,
        out_specs=[spec] * len(out_shape),
        scratch_shapes=[pltpu.VMEM(s, F32) for s in scratch],
        compiler_params=pltpu.CompilerParams(vmem_limit_bytes=56 * MIB),
        name=name,
    )


def ring(axis, step):
    count = lax.axis_size(axis)
    return [(i, (i + step) % count) for i in range(count)]


def shards(fine_pops, coarse_pops, fine_solid, coarse_solid, fine_active, coarse_covered, rates):
    factors = jnp.asarray([0.25] * 3 + [0.5] * 3 + [0.25] * 9, F32)
    both = jnp.concatenate([rates * factors, factors / (2.0 / rates - 0.5)])
    src, xu, xd, yu, yd, zu, zd = call(
        first_kernel,
        "collide_own",
        [
            shape(20, 8, 32, 128),
            shape(25, 32, 128),
            shape(25, 32, 128),
            shape(Y_TILES, 8, 128),
            shape(Y_TILES, 8, 128),
            shape(6, 16, 128),
            shape(6, 16, 128),
        ],
        6,
        [(2, 32, 128)],
    )(both, fine_pops, fine_solid, fine_active, coarse_pops, coarse_solid, coarse_covered)
    ru = lax.ppermute(yu, "quad", ring("quad", 1))
    rd = lax.ppermute(yd, "quad", ring("quad", -1))
    pu, pd = call(
        second_kernel,
        "pack_faces",
        [shape(X_TILES, 8, 128), shape(X_TILES, 8, 128)],
        6,
        [],
        smem=False,
    )(xu, xd, zu, zd, ru, rd)
    rxu = lax.ppermute(pu, "wide", ring("wide", 1))
    rxd = lax.ppermute(pd, "wide", ring("wide", -1))
    fine_out, send = call(
        third_kernel,
        "two_substeps",
        [shape(19, 8, 32, 128), shape(1024, 128)],
        5,
        [
            (20, 12, 40, 128),
            (19, 12, 40, 128),
            (19, 12, 40, 128),
            (19, 12, 40, 128),
            (19, 12, 40, 128),
            (4, 768, 128),
            (384, 128),
            (128, 128),
            (128, 128),
        ],
    )(both, src, ru, rd, rxu, rxd)
    got = lax.all_to_all(send, "wide", split_axis=0, concat_axis=0, tiled=True)
    (coarse_out,) = call(
        fourth_kernel,
        "coarse_step",
        [shape(19, 2, 16, 128)],
        8,
        [(2, 512, 128), (19, 4, 24, 128), (19, 4, 24, 128), (19, 4, 24, 128)],
    )(
        both,
        got,
        coarse_pops,
        coarse_solid,
        coarse_covered,
        ru[Y_FINE:],
        rd[Y_FINE:],
        rxu[X_FINE:],
        rxd[X_FINE:],
    )
    return (fine_out, coarse_out)


def solution(mesh):
    in_specs = (
        P(None, "wide", "quad", None),
        P(None, "wide", "quad", None),
        P("wide", "quad", None),
        P("wide", "quad", None),
        P("wide", "quad", None),
        P("wide", "quad", None),
        P(),
    )
    out_specs = (P(None, "wide", "quad", None), P(None, "wide", "quad", None))
    return jax.shard_map(shards, mesh=mesh, in_specs=in_specs, out_specs=out_specs, check_vma=False)
```

time: 215 us -> 69.2 us (0.32)
  the two profiles are of different devices: /device:TPU:18 before, /device:TPU:1 now
where the time goes in v1:
time: 69.2 us; the launch traced here: 68.8 us
  waiting for transfers between devices  23.3 us (34%)
  Pallas kernels  21 us (30%)
  starting transfers between devices  14.5 us (21%)
  local copies, waits for them, and re-layouts  7.91 us (11%)
  other arithmetic  1.3 us (2%)
    pallas_call x1, Pallas kernels, shards(): call(third_kernel, 'two_substeps', [shape(19, 8, 32, 128), shape(1024, 12...  10.8 us
    all_to_all x1, starting transfers between devices, shards(): got = lax.all_to_all(send, 'wide', split_axis=0, concat_axis=0, tiled=True)  8 us
    ppermute x1, waiting for transfers between devices, shards(): ru = lax.ppermute(yu, 'quad', ring('quad', 1))  7.59 us
    ppermute x1, waiting for transfers between devices, shards(): rxu = lax.ppermute(pu, 'wide', ring('wide', 1))  6.88 us
    all_to_all x1, waiting for transfers between devices, shards(): got = lax.all_to_all(send, 'wide', split_axis=0, concat_axis=0, tiled=True)  6.17 us
    pallas_call x1, Pallas kernels, shards(): call(first_kernel, 'collide_own', [shape(20, 8, 32, 128), shape(25, 32, 1...  5.56 us
    ppermute x1, starting transfers between devices, shards(): rxu = lax.ppermute(pu, 'wide', ring('wide', 1))  2.9 us
    ppermute x1, waiting for transfers between devices, shards(): rxd = lax.ppermute(pd, 'wide', ring('wide', -1))  2.67 us
  transfers between devices with their start and end apart: 5, of which 4 were waited for; matrix products, arithmetic and copies ran while one was open for 8% of the time, Pallas kernels for 0%

profile of v1, /device:TPU:1, one launch (start us, length us, event | category | flops | bytes accessed | tf_op | source)
XLA Modules:
  0.0 68.8 jit_solution(4437157116361785715)
XLA Ops:
  0.6 0.7 fusion
  1.3 0.6 pad_maximum_fusion.rates
  1.9 5.6 %collide_own.1 = (f32[20,8,32,128]{3,2,1,0:T(8,128)}, f32[25,32,128]{2,1,0:T(8,128)}, f32[25,32,128]{2,1,0:T(8,128)}, f32[82,8,128]{2,1,0:T(8,128)}, f32[82,8,12...) custom-call(f32[30]{0:T(128)} %pad_maximum_fusion.rates, f32[19,8,32,128]{3,2,1,0:T(8,128)} %f.1, ...), custom_call_target="tpu_custom_call" | custom-call | tf_op jit(solution)/shard_map/collide_own/pallas_call | solution.py:481
  7.5 2.1 %collective-permute-start = (f32[82,8,128]{2,1,0:T(8,128)}, f32[82,8,128]{2,1,0:T(8,128)S(1)}, u32[]{:S(2)}, u32[]{:S(2)}) collective-permute-start(f32[82,8,128]{2,1,0:T(8,128)} %get-tuple-element.14), channel_id=1, source_target_pairs={{0,1},{1,2},{2,3},{3,0},{4,5},{5,6},{6,7},{7,4},{8,9},{9,10},{10,1... | collective-permute-start | bytes 1007624 | tf_op jit(solution)/shard_map/ppermute | solution.py:496
  9.6 1.5 %collective-permute-start.1 = (f32[82,8,128]{2,1,0:T(8,128)}, f32[82,8,128]{2,1,0:T(8,128)S(1)}, u32[]{:S(2)}, u32[]{:S(2)}) collective-permute-start(f32[82,8,128]{2,1,0:T(8,128)} %get-tuple-element.15), channel_id=1, source_target_pairs={{0,3},{1,0},{2,1},{3,2},{4,7},{5,4},{6,5},{7,6},{8,11},{9,8},{10,9... | collective-permute-start | bytes 1007624 | tf_op jit(solution)/shard_map/ppermute | solution.py:497
  11.1 7.6 %collective-permute-done.ru = f32[82,8,128]{2,1,0:T(8,128)S(1)} collective-permute-done((f32[82,8,128]{2,1,0:T(8,128)}, f32[82,8,128]{2,1,0:T(8,128)S(1)}, u32[]{:S(2)}, u32[]{:S(2)}) %collective-permute-start) | collective-permute-done | bytes 335904 | tf_op jit(solution)/shard_map/ppermute | solution.py:496
  18.7 0.0 copy-start.1
  18.7 0.0 collective-permute-done.1.rd
  18.7 0.0 copy-start.2
  18.7 0.7 %copy-done.1 = f32[82,8,128]{2,1,0:T(8,128)} copy-done((f32[82,8,128]{2,1,0:T(8,128)}, f32[82,8,128]{2,1,0:T(8,128)S(1)}, u32[]{:S(2)}) %copy-start.1) | copy-done | bytes 335896
  19.5 0.1 copy-done.2
  19.6 2.4 %pack_faces.1 = (f32[138,8,128]{2,1,0:T(8,128)}, f32[138,8,128]{2,1,0:T(8,128)}) custom-call(f32[25,32,128]{2,1,0:T(8,128)} %get-tuple-element.16.xu, f32[25,32,128]{2,1,0:T(8,128)} %get-tuple-element.17.xd, f32[6,16,128]{2,1,0:T(8,128)} %get-tuple-element.18.zu, f32[6,16,128]{2,1,0:T(8,128)} %get-tuple-element.19.zd, f32[82,8,128]{2,1,0:T(8,128)} %copy-done.1, ...), custom_call_target="tpu_custom_call" | custom-call | tf_op jit(solution)/shard_map/pack_faces/pallas_call | solution.py:498
  22.0 2.9 %collective-permute-start.2 = (f32[138,8,128]{2,1,0:T(8,128)}, f32[138,8,128]{2,1,0:T(8,128)S(1)}, u32[]{:S(2)}, u32[]{:S(2)}) collective-permute-start(f32[138,8,128]{2,1,0:T(8,128)} %get-tuple-element.20), channel_id=1, source_target_pairs={{0,4},{4,8},{8,12},{12,16},{16,20},{20,24},{24,28},{28,32},{32,36}... | collective-permute-start | bytes 1695752 | tf_op jit(solution)/shard_map/ppermute | solution.py:506
  24.9 0.0 collective-permute-start.3
  24.9 6.9 %collective-permute-done.2.rxu = f32[138,8,128]{2,1,0:T(8,128)S(1)} collective-permute-done((f32[138,8,128]{2,1,0:T(8,128)}, f32[138,8,128]{2,1,0:T(8,128)S(1)}, u32[]{:S(2)}, u32[]{:S(2)}) %collective-permute-start.2) | collective-permute-done | bytes 565280 | tf_op jit(solution)/shard_map/ppermute | solution.py:506
  31.8 0.0 copy-start.3
  31.8 2.7 %collective-permute-done.3.rxd = f32[138,8,128]{2,1,0:T(8,128)S(1)} collective-permute-done((f32[138,8,128]{2,1,0:T(8,128)}, f32[138,8,128]{2,1,0:T(8,128)S(1)}, u32[]{:S(2)}, u32[]{:S(2)}) %collective-permute-start.3) | collective-permute-done | bytes 565280 | tf_op jit(solution)/shard_map/ppermute | solution.py:507
  34.5 0.0 copy-start.4
  34.5 0.0 copy-done.3
  34.5 0.8 %copy-done.4 = f32[138,8,128]{2,1,0:T(8,128)} copy-done((f32[138,8,128]{2,1,0:T(8,128)}, f32[138,8,128]{2,1,0:T(8,128)S(1)}, u32[]{:S(2)}) %copy-start.4) | copy-done | bytes 565272
  35.3 10.8 %two_substeps.1 = (f32[19,8,32,128]{3,2,1,0:T(8,128)}, f32[1024,128]{1,0:T(8,128)}) custom-call(f32[30]{0:T(128)} %pad_maximum_fusion.rates, f32[20,8,32,128]{3,2,1,0:T(8,128)} %get-tuple-element.13.src, f32[82,8,128]{2,1,0:T(8,128)} %copy-done.1, f32[82,8,128]{2,1,0:T(8,128)} %copy-done.2, f32[138,8,128]{2,1,0:T(8,128)} %copy-done.3, f32[138,8,128]{2,1,0:T(8,128)} %copy-done.4), custom_call_target="tpu_custom_call" | custom-call | tf_op jit(solution)/shard_map/two_substeps/pallas_call | solution.py:508
  46.1 8.0 %all-to-all-start = ((f32[32,32,128]{2,1,0:T(8,128)}), f32[32,32,128]{2,1,0:T(8,128)S(1)}, u32[]{:S(2)}, u32[]{:S(2)}) async-start(f32[32,32,128]{2,1,0:T(8,128)} %bitcast.3), calls=%async_computation | async-start | bytes 1048576 | tf_op jit(solution)/shard_map/all_to_all | solution.py:525
  54.1 1.3 %slice.16.ru = f32[2,8,128]{2,1,0:T(8,128)} slice(f32[82,8,128]{2,1,0:T(8,128)} %copy-done.1), slice={[80:82], [0:8], [0:128]} | slice | bytes 16384 | tf_op jit(solution)/shard_map/slice | solution.py:538
  55.4 1.3 %slice.17.rd = f32[2,8,128]{2,1,0:T(8,128)} slice(f32[82,8,128]{2,1,0:T(8,128)} %copy-done.2), slice={[80:82], [0:8], [0:128]} | slice | bytes 16384 | tf_op jit(solution)/shard_map/slice | solution.py:539
  56.6 1.4 %slice.18.rxu = f32[13,8,128]{2,1,0:T(8,128)} slice(f32[138,8,128]{2,1,0:T(8,128)} %copy-done.3), slice={[125:138], [0:8], [0:128]} | slice | bytes 106496 | tf_op jit(solution)/shard_map/slice | solution.py:540
  58.1 1.4 %slice.19.rxd = f32[13,8,128]{2,1,0:T(8,128)} slice(f32[138,8,128]{2,1,0:T(8,128)} %copy-done.4), slice={[125:138], [0:8], [0:128]} | slice | bytes 106496 | tf_op jit(solution)/shard_map/slice | solution.py:541
  59.5 6.2 %all-to-all-done = f32[32,32,128]{2,1,0:T(8,128)S(1)} async-done(((f32[32,32,128]{2,1,0:T(8,128)}), f32[32,32,128]{2,1,0:T(8,128)S(1)}, u32[]{:S(2)}, u32[]{:S(2)}) %all-to-all-start) | async-done | bytes 524320 | tf_op jit(solution)/shard_map/all_to_all | solution.py:525
  65.7 0.0 copy-start
  65.7 0.8 %copy-done = f32[32,32,128]{2,1,0:T(8,128)} copy-done((f32[32,32,128]{2,1,0:T(8,128)}, f32[32,32,128]{2,1,0:T(8,128)S(1)}, u32[]{:S(2)}) %copy-start) | copy-done | bytes 524312
  66.5 2.3 %coarse_step.1 = f32[19,2,16,128]{3,2,1,0:T(8,128)} custom-call(f32[30]{0:T(128)} %pad_maximum_fusion.rates, f32[1024,128]{1,0:T(8,128)} %bitcast.2, f32[19,2,16,128]{3,2,1,0:T(8,128)} %cp.3, s32[2,16,128]{2,1,0:T(8,128)} %c_solid.3, s32[2,16,128]{2,1,0:T(8,128)} %c_cov.3, f32[2,8,128]{2,1,0:T(8,128)} %slice.16.ru, f32[2,8,128]{2,1,0:T(8,128)} %slice.17.rd, ...), custom_call_target="tpu_custom_call" | custom-call | tf_op jit(solution)/shard_map/coarse_step/pallas_call | solution.py:526
Async XLA Ops:
  7.5 11.2 %collective-permute-start = (f32[82,8,128]{2,1,0:T(8,128)}, f32[82,8,128]{2,1,0:T(8,128)S(1)}, u32[]{:S(2)}, u32[]{:S(2)}) collective-permute-start(f32[82,8,128]{2,1,0:T(8,128)} %get-tuple-element.14), channel_id=1, source_target_pairs={{0,1},{1,2},{2,3},{3,0},{4,5},{5,6},{6,7},{7,4},{8,9},{9,10},{10,1... | collective-permute-start | bytes 1007624 | tf_op jit(solution)/shard_map/ppermute | solution.py:496
  9.6 9.1 %collective-permute-start.1 = (f32[82,8,128]{2,1,0:T(8,128)}, f32[82,8,128]{2,1,0:T(8,128)S(1)}, u32[]{:S(2)}, u32[]{:S(2)}) collective-permute-start(f32[82,8,128]{2,1,0:T(8,128)} %get-tuple-element.15), channel_id=1, source_target_pairs={{0,3},{1,0},{2,1},{3,2},{4,7},{5,4},{6,5},{7,6},{8,11},{9,8},{10,9... | collective-permute-start | bytes 1007624 | tf_op jit(solution)/shard_map/ppermute | solution.py:497
  18.7 0.7 %copy-start.1 = (f32[82,8,128]{2,1,0:T(8,128)}, f32[82,8,128]{2,1,0:T(8,128)S(1)}, u32[]{:S(2)}) copy-start(f32[82,8,128]{2,1,0:T(8,128)S(1)} %collective-permute-done.ru) | copy-start | bytes 1007620
  18.7 0.9 %copy-start.2 = (f32[82,8,128]{2,1,0:T(8,128)}, f32[82,8,128]{2,1,0:T(8,128)S(1)}, u32[]{:S(2)}) copy-start(f32[82,8,128]{2,1,0:T(8,128)S(1)} %collective-permute-done.1.rd) | copy-start | bytes 1007620
  22.0 9.8 %collective-permute-start.2 = (f32[138,8,128]{2,1,0:T(8,128)}, f32[138,8,128]{2,1,0:T(8,128)S(1)}, u32[]{:S(2)}, u32[]{:S(2)}) collective-permute-start(f32[138,8,128]{2,1,0:T(8,128)} %get-tuple-element.20), channel_id=1, source_target_pairs={{0,4},{4,8},{8,12},{12,16},{16,20},{20,24},{24,28},{28,32},{32,36}... | collective-permute-start | bytes 1695752 | tf_op jit(solution)/shard_map/ppermute | solution.py:506
  24.9 9.6 %collective-permute-start.3 = (f32[138,8,128]{2,1,0:T(8,128)}, f32[138,8,128]{2,1,0:T(8,128)S(1)}, u32[]{:S(2)}, u32[]{:S(2)}) collective-permute-start(f32[138,8,128]{2,1,0:T(8,128)} %get-tuple-element.21), channel_id=1, source_target_pairs={{0,124},{4,0},{8,4},{12,8},{16,12},{20,16},{24,20},{28,24},{32,28}... | collective-permute-start | bytes 1695752 | tf_op jit(solution)/shard_map/ppermute | solution.py:507
  31.8 2.7 %copy-start.3 = (f32[138,8,128]{2,1,0:T(8,128)}, f32[138,8,128]{2,1,0:T(8,128)S(1)}, u32[]{:S(2)}) copy-start(f32[138,8,128]{2,1,0:T(8,128)S(1)} %collective-permute-done.2.rxu) | copy-start | bytes 1695748
  34.5 0.8 %copy-start.4 = (f32[138,8,128]{2,1,0:T(8,128)}, f32[138,8,128]{2,1,0:T(8,128)S(1)}, u32[]{:S(2)}) copy-start(f32[138,8,128]{2,1,0:T(8,128)S(1)} %collective-permute-done.3.rxd) | copy-start | bytes 1695748
  46.1 19.6 %all-to-all-start = ((f32[32,32,128]{2,1,0:T(8,128)}), f32[32,32,128]{2,1,0:T(8,128)S(1)}, u32[]{:S(2)}, u32[]{:S(2)}) async-start(f32[32,32,128]{2,1,0:T(8,128)} %bitcast.3), calls=%async_computation | async-start | bytes 1048576 | tf_op jit(solution)/shard_map/all_to_all | solution.py:525
  65.7 0.8 %copy-start = (f32[32,32,128]{2,1,0:T(8,128)}, f32[32,32,128]{2,1,0:T(8,128)S(1)}, u32[]{:S(2)}) copy-start(f32[32,32,128]{2,1,0:T(8,128)S(1)} %all-to-all-done) | copy-start | bytes 1572868

commit v2 on v1

v2 whole, which is shorter than its diff:
```python
import jax
import jax.numpy as jnp
from jax import lax
from jax.experimental import pallas as pl
from jax.experimental.pallas import tpu as pltpu
from jax.sharding import PartitionSpec as P

VEL = [
    (0, 0, 0),
    (1, 0, 0),
    (-1, 0, 0),
    (0, 1, 0),
    (0, -1, 0),
    (0, 0, 1),
    (0, 0, -1),
    (1, 1, 0),
    (-1, -1, 0),
    (1, -1, 0),
    (-1, 1, 0),
    (1, 0, 1),
    (-1, 0, -1),
    (1, 0, -1),
    (-1, 0, 1),
    (0, 1, 1),
    (0, -1, -1),
    (0, 1, -1),
    (0, -1, 1),
]
OPP = [0, 2, 1, 4, 3, 6, 5, 8, 7, 10, 9, 12, 11, 14, 13, 16, 15, 18, 17]


def moving(axis, sign):
    return [q for q in range(19) if VEL[q][axis] == sign]


XP, XM = moving(0, 1), moving(0, -1)
YP, YM = moving(1, 1), moving(1, -1)
ZP, ZM = moving(2, 1), moving(2, -1)
WALL = 1e30
WALL_TEST = 1e29
F32 = jnp.float32
MIB = 1 << 20

Y_FOURTH = 480
Y_COARSE = 520
Y_ROWS = 536
X_TILES = 25
X_COARSE = 25
X_ALL = X_COARSE + 13

FACTOR = [0.25] * 3 + [0.5] * 3 + [0.25] * 9

def collide(f, rate):
    r_xy, r_xz, r_yz, r_xx, r_yy, r_zz = rate[:6]
    r_xyy, r_xzz, r_yxx, r_yzz, r_zxx, r_zyy, r_xxyy, r_xxzz, r_yyzz = rate[6:]
    sx, dx = f[1] + f[2], f[1] - f[2]
    sy, dy = f[3] + f[4], f[3] - f[4]
    sz, dz = f[5] + f[6], f[5] - f[6]

    def plane(i):
        a, b = f[i] + f[i + 1], f[i + 2] + f[i + 3]
        c, d = f[i] - f[i + 1], f[i + 2] - f[i + 3]
        return a + b, a - b, c + d, c - d

    m_xxyy, m_xy, m_xyy, m_yxx = plane(7)
    m_xxzz, m_xz, m_xzz, m_zxx = plane(11)
    m_yyzz, m_yz, m_yzz, m_zyy = plane(15)
    m_xx = sx + (m_xxyy + m_xxzz)
    m_yy = sy + (m_xxyy + m_yyzz)
    m_zz = sz + (m_xxzz + m_yyzz)
    jx = dx + (m_xyy + m_xzz)
    jy = dy + (m_yxx + m_yzz)
    jz = dz + (m_zxx + m_zyy)
    rho = (f[0] + sx) + (sy + sz) + ((m_xxyy + m_xxzz) + m_yyzz)
    inv = 1.0 / rho
    ux, uy, uz = jx * inv, jy * inv, jz * inv
    xx, yy, zz = jx * ux, jy * uy, jz * uz
    third = rho * (1.0 / 3.0)
    ninth = rho * (1.0 / 9.0)
    jx3, jy3, jz3 = jx * (1.0 / 3.0), jy * (1.0 / 3.0), jz * (1.0 / 3.0)
    xx3, yy3, zz3 = xx * (1.0 / 3.0), yy * (1.0 / 3.0), zz * (1.0 / 3.0)
    h_xx = (m_xx - third - xx) * r_xx
    h_yy = (m_yy - third - yy) * r_yy
    h_zz = (m_zz - third - zz) * r_zz
    post = [None] * 19

    def diagonal(i, fourth, cross, first, second):
        p, m = fourth + cross, fourth - cross
        s, d = first + second, first - second
        post[i] = f[i] - (p + s)
        post[i + 1] = f[i + 1] - (p - s)
        post[i + 2] = f[i + 2] - (m + d)
        post[i + 3] = f[i + 3] - (m - d)

    a_xy = (m_xxyy - ninth - (xx3 + yy3 - 0.5 * zz3)) * r_xxyy
    a_xz = (m_xxzz - ninth - (xx3 + zz3 - 0.5 * yy3)) * r_xxzz
    a_yz = (m_yyzz - ninth - (yy3 + zz3 - 0.5 * xx3)) * r_yyzz
    c_xyy, c_yxx = (m_xyy - jx3) * r_xyy, (m_yxx - jy3) * r_yxx
    c_xzz, c_zxx = (m_xzz - jx3) * r_xzz, (m_zxx - jz3) * r_zxx
    c_yzz, c_zyy = (m_yzz - jy3) * r_yzz, (m_zyy - jz3) * r_zyy
    diagonal(7, a_xy, (m_xy - jx * uy) * r_xy, c_xyy, c_yxx)
    diagonal(11, a_xz, (m_xz - jx * uz) * r_xz, c_xzz, c_zxx)
    diagonal(15, a_yz, (m_yz - jy * uz) * r_yz, c_yzz, c_zyy)

    def straight(i, h, a, c):
        p, n = h - 2.0 * a, 2.0 * c
        post[i] = f[i] - (p - n)
        post[i + 1] = f[i + 1] - (p + n)

    straight(1, h_xx, a_xy + a_xz, c_xyy + c_xzz)
    straight(3, h_yy, a_xy + a_yz, c_yxx + c_yzz)
    straight(5, h_zz, a_xz + a_yz, c_zxx + c_zyy)
    post[0] = f[0] + (2.0 * (h_xx + h_yy + h_zz) - 4.0 * (a_xy + a_xz + a_yz))
    return post


def iota(shape, axis):
    return lax.broadcasted_iota(jnp.int32, shape, axis)


def fine_rates(rates):
    return [rates[i] * FACTOR[i] for i in range(15)]


def coarse_rate(rates, i):
    rate = jnp.full((8, 128), rates[i], F32)
    return FACTOR[i] / (2.0 / rate - 0.5)


def wall_where(code, value):
    return jnp.where(code > 0.5, value, WALL)


def grown_blocks(active):
    grow = (iota((32, 128), 1) // 4 == iota((32, 128), 0)).astype(F32)
    return jnp.dot(active.astype(F32), grow, preferred_element_type=F32)


def edges():
    quad, wide = lax.axis_index("quad"), lax.axis_index("wide")
    return (
        (quad > 0).astype(F32),
        (quad < lax.axis_size("quad") - 1).astype(F32),
        (wide > 0).astype(F32),
        (wide < lax.axis_size("wide") - 1).astype(F32),
    )


def rows_kernel(
    rates_in, f, solid, active, cp, c_solid, c_cov, yu, yd, zu, zd,
    rates, low, high, solid_low, solid_high, act, cps, c_solids, c_covs, sems,
):
    small = [
        pltpu.make_async_copy(solid.at[:, 0:8], solid_low, sems.at[0]),
        pltpu.make_async_copy(solid.at[:, 24:32], solid_high, sems.at[1]),
        pltpu.make_async_copy(active, act, sems.at[2]),
        pltpu.make_async_copy(rates_in, rates, sems.at[22]),
        pltpu.make_async_copy(c_solid, c_solids, sems.at[3]),
        pltpu.make_async_copy(c_cov, c_covs, sems.at[4]),
        pltpu.make_async_copy(cp, cps, sems.at[5]),
    ]
    large = []
    for x in range(8):
        large.append(
            (
                pltpu.make_async_copy(f.at[:, x, 0:8], low.at[x], sems.at[6 + x]),
                pltpu.make_async_copy(f.at[:, x, 24:32], high.at[x], sems.at[14 + x]),
            )
        )
    for copy in small[:4]:
        copy.start()
    for pair in large:
        for copy in pair:
            copy.start()
    for copy in small[4:]:
        copy.start()
    for copy in small[:4]:
        copy.wait()
    fine = fine_rates(rates)
    upper = iota((8, 128), 0) < 4
    for x in range(8):
        if x % 4 == 0:
            grown = grown_blocks(act[x // 4])
            on = jnp.where(upper, grown[0:1], grown[7:8])
        for copy in large[x]:
            copy.wait()
        old = [jnp.where(upper, low[x, q], high[x, q]) for q in range(19)]
        fluid = jnp.where(upper, solid_low[x], solid_high[x]) == 0
        live = fluid & (on > 0.5)
        post = collide(old, fine)
        source = [jnp.where(live, post[q], old[q]) for q in range(19)]
        source.append(jnp.where(fluid, 1.0 + on, 0.0))
        for q in range(20):
            start = 60 * x + 3 * q
            yu[start : start + 3] = source[q][5:8]
            yd[start : start + 3] = source[q][0:3]
        for i in range(5):
            start = Y_FOURTH + 8 * i + x
            yu[start : start + 1] = jnp.where(fluid, source[YP[i]], WALL)[4:5]
            yd[start : start + 1] = jnp.where(fluid, source[YM[i]], WALL)[3:4]
    for copy in small[4:]:
        copy.wait()
    coarse = [coarse_rate(rates, i) for i in range(15)]
    for z in range(2):
        for t in range(2):
            rows = pl.ds(8 * t, 8)
            post = collide([cps[q, z, rows] for q in range(19)], coarse)
            code = jnp.where(c_solids[z, rows] == 0, 1.0 + c_covs[z, rows].astype(F32), 0.0)
            values, to = (ZP, zu) if z == 1 else (ZM, zd)
            for i in range(5):
                to[i, rows] = post[values[i]]
            to[5, rows] = code
            values, to, row = (YM, yd, 0) if t == 0 else (YP, yu, 7)
            for i in range(6):
                place = Y_COARSE + 6 * z + i
                value = code if i == 5 else post[values[i]]
                to[place : place + 1] = value[row : row + 1]


def cells_kernel(rates, f, solid, active, ext, crate, act):
    fine = fine_rates(rates)
    for i in range(15):
        crate[i] = coarse_rate(rates, i)
    grow_y = (iota((32, 8), 0) // 4 == iota((32, 8), 1)).astype(F32)
    for b in range(2):
        act[b] = jnp.dot(grow_y, grown_blocks(active[b]), preferred_element_type=F32)

    def plane(x, carry):
        for t in range(4):
            rows = pl.ds(8 * t, 8)
            old = [f[q, x, rows] for q in range(19)]
            fluid = solid[x, rows] == 0
            on = act[x // 4, rows]
            live = fluid & (on > 0.5)
            post = collide(old, fine)
            for q in range(19):
                ext[q, x, rows] = jnp.where(live, post[q], old[q])
            ext[19, x, rows] = jnp.where(fluid, 1.0 + on, 0.0)
        return carry

    lax.fori_loop(0, 8, plane, 0)


def fill_rows(q, x, ru, rd, to):
    start = 60 * x + 3 * q
    to[0:3] = rd[start : start + 3]
    to[5:8] = ru[start : start + 3]
    if q in YM:
        fourth = Y_FOURTH + 8 * YM.index(q) + x
        to[3:4] = rd[fourth : fourth + 1]
    if q in YP:
        fourth = Y_FOURTH + 8 * YP.index(q) + x
        to[4:5] = ru[fourth : fourth + 1]


def fill_code(x, ru, rd, to, has_prev, has_next):
    start = 60 * x + 57
    to[0:3] = rd[start : start + 3] * has_next
    to[5:8] = ru[start : start + 3] * has_prev
    to[3:4] = jnp.full((1, 128), has_next, F32)
    to[4:5] = jnp.full((1, 128), has_prev, F32)


def upwards():
    return lax.axis_index("quad") % 2 == 0


def put_both(first, second, place, up, down):
    goes_up = upwards()
    first[place] = jnp.where(goes_up, up, down)
    second[place] = jnp.where(goes_up, down, up)


def faces_kernel(ext, zu, zd, ru, rd, pa, pb, code, tile):
    has_prev, has_next, _, _ = edges()
    for n, x, values in ((0, 7, XP), (1, 0, XM)):
        fill_code(x, ru, rd, code.at[n], has_prev, has_next)
        for i in range(5):
            fill_rows(values[i], x, ru, rd, tile.at[n, i])
    for i in range(5):
        for t in range(4):
            rows = pl.ds(8 * t, 8)
            up = wall_where(ext[19, 7, rows], ext[XP[i], 7, rows])
            down = wall_where(ext[19, 0, rows], ext[XM[i], 0, rows])
            put_both(pa, pb, 5 * i + t, up, down)
        up, down = wall_where(code[0], tile[0, i]), wall_where(code[1], tile[1, i])
        put_both(pa, pb, 5 * i + 4, up, down)
    for i in range(6):
        for t in range(2):
            rows = pl.ds(8 * t, 8)
            put_both(pa, pb, X_COARSE + 2 * i + t, zu[i, rows], zd[i, rows])
    for n, z, up, down in ((0, 1, 15, 18), (1, 0, 17, 16)):

        def arrived(from_, place):
            return from_[Y_COARSE + place : Y_COARSE + place + 1]

        tile[n, 0] = jnp.zeros((8, 128), F32)
        tile[n, 0, 0:1] = arrived(ru, 6 * z + YP.index(up))
        tile[n, 0, 1:2] = arrived(rd, 6 * z + YM.index(down))
        tile[n, 0, 2:3] = arrived(ru, 6 * z + 5) * has_prev
        tile[n, 0, 3:4] = arrived(rd, 6 * z + 5) * has_next
    put_both(pa, pb, X_COARSE + 12, tile[0, 0], tile[1, 0])


def streamed(q, x, values, open_cells, live, lane, outer=None):
    cx, cy, cz = VEL[q]
    if q == 0:
        return values[0, x]
    if cx and outer is not None and outer[0] == cx:
        value = outer[1](q)
    else:
        value = jnp.where(open_cells[cx], values[q, x - cx], WALL)
    if cy:
        value = pltpu.roll(value, cy % 40, 0)
    if cz:
        value = pltpu.roll(value, cz % 128, 1)
    open_ = value < WALL_TEST
    if cz:
        open_ = open_ & (lane != (0 if cz == 1 else 127))
    return jnp.where(live, jnp.where(open_, value, values[OPP[q], x]), values[q, x])


def step_plane(x, ext, first, src2, fine, lane, outer=None):
    open_cells = {}
    for cx in (-1, 0, 1):
        if outer is None or outer[0] != cx:
            open_cells[cx] = ext[19, x - cx] > 0.5
    live = ext[19, x] > 1.5
    for q in range(19):
        first[q, x] = streamed(q, x, ext, open_cells, live, lane, outer)
    for t in range(5):
        rows = pl.ds(8 * t, 8)
        live_t = ext[19, x, rows] > 1.5
        old = [first[q, x, rows] for q in range(19)]
        post = collide(old, fine)
        for q in range(19):
            src2[q, x, rows] = jnp.where(live_t, post[q], old[q])


def inner_one_kernel(rates, ext_in, ru, rd, ext, first, src2):
    has_prev, has_next, _, _ = edges()
    fine = fine_rates(rates)
    lane = iota((40, 128), 1)

    def copy(x, carry):
        for q in range(20):
            ext[q, x, 0:32] = ext_in[q, x, 0:32]
        return carry

    lax.fori_loop(0, 8, copy, 0)
    for x in range(8):
        for q in range(19):
            fill_rows(q, x, ru, rd, ext.at[q, x, 32:40])
        fill_code(x, ru, rd, ext.at[19, x, 32:40], has_prev, has_next)

    def plane(x, carry):
        step_plane(x, ext, first, src2, fine, lane)
        return carry

    lax.fori_loop(1, 7, plane, 0)


def arrived_face(first, second, from_left, inside):
    values = XP if from_left else XM
    in_first = upwards() if from_left else jnp.logical_not(upwards())

    def get(q):
        rows = pl.ds(5 * values.index(q), 5)
        value = jnp.where(in_first, first[rows], second[rows]).reshape(40, 128)
        return jnp.where(inside > 0.5, value, WALL)

    return get


def outer_one_kernel(rates, ext, ra, rb, first_in, src2_in, first, src2, pa, pb):
    _, _, has_left, has_right = edges()
    fine = fine_rates(rates)
    lane = iota((40, 128), 1)
    step_plane(0, ext, first, src2, fine, lane, (1, arrived_face(ra, rb, True, has_left)))
    step_plane(7, ext, first, src2, fine, lane, (-1, arrived_face(ra, rb, False, has_right)))
    for i in range(5):
        for t in range(5):
            rows = pl.ds(8 * t, 8)
            up = wall_where(ext[19, 7, rows], src2[XP[i], 7, rows])
            down = wall_where(ext[19, 0, rows], src2[XM[i], 0, rows])
            put_both(pa, pb, 5 * i + t, up, down)


def second_plane(x, ext, first, src2, lane, emit, outer=None):
    open_cells = {}
    for cx in (-1, 0, 1):
        if outer is None or outer[0] != cx:
            open_cells[cx] = ext[19, x - cx] > 0.5
    live = ext[19, x] > 1.5
    for q in range(19):
        emit(q, streamed(q, x, src2, open_cells, live, lane, outer), first[q, x])


def destinations(sums, coarse, raw, up, down, send, b):
    def taken(k):
        return 2 * iota((32, 128), 0) + (k - 1)

    z_lane = iota((32, 128), 1)
    own_1 = jnp.where(z_lane // 2 == taken(1), 0.0625, 0.0)
    own_2 = jnp.where(z_lane // 2 == taken(2), 0.0625, 0.0)
    own_rows = jnp.concatenate([own_1, own_2], axis=0)
    before = (z_lane == 2 * taken(0)).astype(F32)
    after = (z_lane == 2 * taken(3)).astype(F32)
    even = iota((8, 128), 1) % 2 == 0
    dims = (((1,), (1,)), ((), ()))
    for t in range(3):
        cells = []
        for q in range(19):
            start = 40 * q + 16 * t
            value = sums[pl.ds(start, 8, stride=2)] + sums[pl.ds(start + 1, 8, stride=2)]
            if t < 2:
                raw[16 * q + 8 * t : 16 * q + 8 * t + 8] = value
            cells.append((value + pltpu.roll(value, 127, 1)) * 0.0625)
        post = collide(cells, coarse)
        if t < 2:
            for i in range(5):
                up[16 * i + 8 * t : 16 * i + 8 * t + 8] = post[ZP[i]]
                down[16 * i + 8 * t : 16 * i + 8 * t + 8] = post[ZM[i]]
        else:
            for i in range(5):
                prev = jnp.where(even, 16.0 * post[YP[i]], 0.0)
                next_ = jnp.where(even, 16.0 * post[YM[i]], 0.0)
                raw[304 + i : 305 + i] = prev[3:4]
                raw[309 + i : 310 + i] = next_[0:1]
            up[80:81] = post[15][3:4]
            up[81:82] = post[18][0:1]
            down[80:81] = post[17][3:4]
            down[81:82] = post[16][0:1]

    def picked(rows, cells):
        return lax.dot_general(
            rows, cells, dims, precision=lax.Precision.HIGHEST, preferred_element_type=F32
        )

    for n in range(3):
        got = picked(own_rows, raw[128 * n : 128 * n + 128])
        for k in range(2):
            send[pl.ds(8 * b + 2 * n + k, 32, stride=32)] = got[32 * k : 32 * k + 32]
    for k, (rows, ref) in enumerate(((before, up), (after, down))):
        send[pl.ds(8 * b + 6 + k, 32, stride=32)] = picked(rows, ref[...])


def clear(*refs):
    for ref in refs:
        ref[...] = jnp.zeros(ref.shape, F32)


def inner_two_kernel(
    ext, first, src2, crate, fine_out, sums, send, planes, raw, up, down, sem
):
    lane = iota((40, 128), 1)
    clear(raw, up, down)

    def out_copy(x):
        return pltpu.make_async_copy(planes.at[x - 1], fine_out.at[:, x], sem.at[x - 1])

    def plane(x, carry):
        def emit(q, value, before):
            planes[x - 1, q] = value[0:32]
            total = value + before
            place = (x // 2, pl.ds(40 * q, 40))
            fresh = (x % 2 == 0) | (x == 1)
            sums[place] = jnp.where(fresh, total, sums[place] + total)

        second_plane(x, ext, first, src2, lane, emit)
        out_copy(x).start()
        return carry

    lax.fori_loop(1, 7, plane, 0)
    coarse = [crate[i] for i in range(15)]

    def block(b, carry):
        destinations(sums.at[b], coarse, raw, up, down, send, b)
        return carry

    lax.fori_loop(1, 3, block, 0)
    for x in range(1, 7):
        out_copy(x).wait()


def outer_two_kernel(
    ext, first, src2, crate, ra, rb, sums_in, send_in, fine_in,
    send, fine_out, sums, planes, raw, up, down, sem,
):
    _, _, has_left, has_right = edges()
    lane = iota((40, 128), 1)
    clear(raw, up, down)
    sides = (
        (0, (1, arrived_face(ra, rb, True, has_left))),
        (7, (-1, arrived_face(ra, rb, False, has_right))),
    )
    copies = []
    for n, (x, outer) in enumerate(sides):

        def emit(q, value, before):
            planes[n, q] = value[0:32]
            rows = pl.ds(40 * q, 40)
            sums[n, rows] = value + before + sums_in[3 * n, rows]

        second_plane(x, ext, first, src2, lane, emit, outer)
        copy = pltpu.make_async_copy(planes.at[n], fine_out.at[:, x], sem.at[n])
        copy.start()
        copies.append(copy)
    coarse = [crate[i] for i in range(15)]
    for n in range(2):
        destinations(sums.at[n], coarse, raw, up, down, send, 3 * n)
    for copy in copies:
        copy.wait()


def coarse_kernel(
    got, crate, cp, c_solid, c_cov, ru, rd, ra, rb, out, turned, walled, source, message
):
    has_prev, has_next, has_left, has_right = edges()
    coarse = [crate[i] for i in range(15)]
    for k in range(2):
        for n in range(4):
            turned[k, 128 * n : 128 * n + 128] = got[pl.ds(2 * n + k, 128, stride=8)].T

    goes_up = upwards()
    for i in range(13):
        first, second = ra[X_COARSE + i], rb[X_COARSE + i]
        message[0, i] = jnp.where(goes_up, first, second)
        message[1, i] = jnp.where(goes_up, second, first)

    def pick(code, here, there):
        return jnp.where(code > 1.5, here, jnp.where(code > 0.5, there, WALL))

    def arrived(from_, place):
        return from_[Y_COARSE + place : Y_COARSE + place + 1]

    for k in range(2):
        for t in range(2):
            rows = pl.ds(8 * t, 8)
            fluid = c_solid[k, rows] == 0
            covered = c_cov[k, rows] == 1
            old = []
            for q in range(19):
                start = 16 * q + 8 * t
                old.append(jnp.where(covered, turned[k, start : start + 8], cp[q, k, rows]))
            post = collide(old, coarse)
            for q in range(19):
                value = jnp.where(fluid, post[q], old[q])
                source[q, k + 1, rows] = value
                walled[q, k + 1, rows] = jnp.where(fluid, value, WALL)
        prev_code = arrived(ru, 6 * k + 5) * has_prev
        next_code = arrived(rd, 6 * k + 5) * has_next
        for i in range(5):
            walled[YP[i], k + 1, 23:24] = pick(
                prev_code, turned[k, 304 + i : 305 + i], arrived(ru, 6 * k + i)
            )
            walled[YM[i], k + 1, 16:17] = pick(
                next_code, turned[k, 309 + i : 310 + i], arrived(rd, 6 * k + i)
            )
        values, from_, z, inside = ((ZP, message.at[0], 0, has_left), (ZM, message.at[1], 3, has_right))[k]
        prev_q, next_q = ((15, 18), (17, 16))[k]
        for t in range(2):
            code = from_[10 + t] * inside
            for i in range(5):
                start = 384 + 16 * i + 8 * t
                walled[values[i], z, 8 * t : 8 * t + 8] = pick(
                    code, turned[k, start : start + 8], from_[2 * i + t]
                )
        walled[prev_q, z, 23:24] = pick(
            from_[12, 2:3] * inside, turned[k, 464:465], from_[12, 0:1]
        )
        walled[next_q, z, 16:17] = pick(
            from_[12, 3:4] * inside, turned[k, 465:466], from_[12, 1:2]
        )

    lane = iota((16, 128), 1)
    for z in (1, 2):
        fluid = c_solid[z - 1] == 0
        for q in range(19):
            cx, cy, cz = VEL[q]
            value = walled[q, z - cz]
            if cy:
                value = pltpu.roll(value, cy % 24, 0)
            value = value[0:16]
            if cx:
                value = pltpu.roll(value, cx % 128, 1)
            open_ = value < WALL_TEST
            if cx:
                open_ = open_ & (lane != (0 if cx == 1 else 127))
            bounced = jnp.where(open_, value, source[OPP[q], z, 0:16])
            out[q, z - 1] = jnp.where(fluid, bounced, source[q, z, 0:16])


def shape(*dims):
    return jax.ShapeDtypeStruct(dims, F32)


SMEM = pl.BlockSpec(memory_space=pltpu.SMEM)
VMEM = pl.BlockSpec(memory_space=pltpu.VMEM)
HBM = pl.BlockSpec(memory_space=pltpu.HBM)


def call(kernel, name, ins, outs, scratch=(), aliases=None, cells=0):
    return pl.pallas_call(
        kernel,
        out_shape=[shape(*dims) for dims, _ in outs],
        in_specs=ins,
        out_specs=[place for _, place in outs],
        scratch_shapes=[s if not isinstance(s, tuple) else pltpu.VMEM(s, F32) for s in scratch],
        input_output_aliases=aliases or {},
        compiler_params=pltpu.CompilerParams(vmem_limit_bytes=24 * MIB),
        cost_estimate=pl.CostEstimate(
            flops=300 * cells, bytes_accessed=160 * cells, transcendentals=cells
        ),
        name=name,
    )


def over_quad(up, down):
    count = lax.axis_size("quad")
    ring = [(i, (i + 1) % count) for i in range(count)]
    return lax.ppermute(up, "quad", ring), lax.ppermute(down, "quad", [(j, i) for i, j in ring])


def over_wide(first, second):
    wide, quad = lax.axis_size("wide"), lax.axis_size("quad")
    path = []
    for q in range(0, quad, 2):
        line = [(w, q) for w in range(wide)] + [(w, q + 1) for w in reversed(range(wide))]
        path += list(zip(line, line[1:] + line[:1]))
    path = [(a[0] * quad + a[1], b[0] * quad + b[1]) for a, b in path]
    axes = ("wide", "quad")
    return (
        lax.ppermute(first, axes, path),
        lax.ppermute(second, axes, [(j, i) for i, j in path]),
    )


def shards(fine_pops, coarse_pops, fine_solid, coarse_solid, fine_active, coarse_covered, rates):
    i32 = jnp.int32
    dma = pltpu.SemaphoreType.DMA
    ext_shape, pops_shape = (20, 8, 40, 128), (19, 8, 40, 128)
    yu, yd, zu, zd = call(
        rows_kernel,
        "collide_rows",
        [HBM] * 7,
        [((Y_ROWS, 128), VMEM)] * 2 + [((6, 16, 128), VMEM)] * 2,
        [
            pltpu.SMEM((15,), F32),
            (8, 19, 8, 128),
            (8, 19, 8, 128),
            pltpu.VMEM((8, 8, 128), i32),
            pltpu.VMEM((8, 8, 128), i32),
            pltpu.VMEM((2, 8, 32), i32),
            (19, 2, 16, 128),
            pltpu.VMEM((2, 16, 128), i32),
            pltpu.VMEM((2, 16, 128), i32),
            dma((23,)),
        ],
    )(
        *[
            pltpu.with_memory_space_constraint(a, pltpu.HBM)
            for a in (
                rates, fine_pops, fine_solid, fine_active, coarse_pops, coarse_solid, coarse_covered
            )
        ]
    )
    ru, rd = over_quad(yu, yd)
    ext, crate = call(
        cells_kernel,
        "collide_cells",
        [SMEM] + [VMEM] * 3,
        [(ext_shape, VMEM), ((15, 8, 128), VMEM)],
        [(2, 32, 128)],
        cells=32768,
    )(rates, fine_pops, fine_solid, fine_active)
    pa, pb = call(
        faces_kernel,
        "pack_faces",
        [VMEM] * 5,
        [((X_ALL, 8, 128), VMEM)] * 2,
        [(2, 8, 128), (2, 5, 8, 128)],
    )(ext, zu, zd, ru, rd)
    ra, rb = over_wide(pa, pb)
    ext, first, src2 = call(
        inner_one_kernel,
        "substep_one_inner",
        [SMEM] + [VMEM] * 3,
        [(ext_shape, VMEM), (pops_shape, VMEM), (pops_shape, VMEM)],
        cells=24576,
    )(rates, ext, ru, rd)
    first, src2, pa, pb = call(
        outer_one_kernel,
        "substep_one_faces",
        [SMEM] + [VMEM] * 5,
        [(pops_shape, VMEM)] * 2 + [((X_TILES, 8, 128), VMEM)] * 2,
        aliases={4: 0, 5: 1},
    )(rates, ext, ra, rb, first, src2)
    ra2, rb2 = over_wide(pa, pb)
    work = [(384, 128), (128, 128), (128, 128)]
    fine_out, sums, send = call(
        inner_two_kernel,
        "substep_two_inner",
        [VMEM] * 4,
        [((19, 8, 32, 128), HBM), ((4, 768, 128), VMEM), ((1024, 128), VMEM)],
        [(6, 19, 32, 128)] + work + [dma((6,))],
        cells=24576,
    )(ext, first, src2, crate)
    send, fine_out = call(
        outer_two_kernel,
        "substep_two_faces",
        [VMEM] * 8 + [HBM],
        [((1024, 128), VMEM), ((19, 8, 32, 128), HBM)],
        [(2, 768, 128), (2, 19, 32, 128)] + work + [dma((2,))],
        aliases={7: 0, 8: 1},
    )(ext, first, src2, crate, ra2, rb2, sums, send, fine_out)
    got = lax.all_to_all(send, "wide", split_axis=0, concat_axis=0, tiled=True)
    (coarse_out,) = call(
        coarse_kernel,
        "coarse_step",
        [VMEM] * 9,
        [((19, 2, 16, 128), VMEM)],
        [(2, 512, 128), (19, 4, 24, 128), (19, 4, 24, 128), (2, 13, 8, 128)],
    )(got, crate, coarse_pops, coarse_solid, coarse_covered, ru, rd, ra, rb)
    return (fine_out, coarse_out)


def solution(mesh):
    in_specs = (
        P(None, "wide", "quad", None),
        P(None, "wide", "quad", None),
        P("wide", "quad", None),
        P("wide", "quad", None),
        P("wide", "quad", None),
        P("wide", "quad", None),
        P(),
    )
    out_specs = (P(None, "wide", "quad", None), P(None, "wide", "quad", None))
    return jax.shard_map(shards, mesh=mesh, in_specs=in_specs, out_specs=out_specs, check_vma=False)
```

time: 69.2 us -> 50 us (0.72)
  blocking collectives: 0 us -> 21.4 us
  waiting for transfers between devices: 23.3 us -> 5.1 us
  Pallas kernels: 21 us -> 13 us
  starting transfers between devices: 14.5 us -> 7.29 us
  local copies, waits for them, and re-layouts: 7.91 us -> 2.27 us
  other arithmetic: 1.3 us -> 0 us
    all_to_all x0 -> x1, blocking collectives: none -> 21.4 us  [shards(): got = lax.all_to_all(send, 'wide', split_axis=0, concat_axis=0, tiled=True)]
    ppermute x4 -> x6, waiting for transfers between devices: 17.1 us -> 5.1 us  [the longest x2 3.3 us: over_wide(): lax.ppermute(second, axes, [(j, i) for i, j in path])]
    pallas_call x4 -> x8, Pallas kernels: 21 us -> 13 us  [the longest x1 2.6 us: shards(): call(inner_two_kernel, 'substep_two_inner', [VMEM] * 4, [((19, 8, 32, 128...]
    all_to_all x1 -> x0, starting transfers between devices: 8 us -> none  [shards(): got = lax.all_to_all(send, 'wide', split_axis=0, concat_axis=0, tiled=True)]
    all_to_all x1 -> x0, waiting for transfers between devices: 6.17 us -> none  [shards(): got = lax.all_to_all(send, 'wide', split_axis=0, concat_axis=0, tiled=True)]
    slice x4 -> x0, local copies, waits for them, and re-layouts: 5.45 us -> none  [the longest x1 1.44 us: shards(): rxd[X_FINE:]]
    ppermute x4 -> x6, starting transfers between devices: 6.55 us -> 7.29 us  [the longest x2 3.07 us: over_wide(): lax.ppermute(first, axes, path)]
    unnamed x10 -> x16, local copies, waits for them, and re-layouts: 2.46 us -> 2.27 us
  transfers between devices with their start and end apart: 5 -> 6, of which waited for: 4 -> 3; matrix products, arithmetic and copies ran while one was open for 8% -> 0% of each run, Pallas kernels for 0% -> 14%
where the time goes in v2:
time: 50 us; the launch traced here: 49.8 us
  blocking collectives  21.4 us (43%)
  Pallas kernels  13 us (26%)
  starting transfers between devices  7.29 us (15%)
  waiting for transfers between devices  5.1 us (10%)
  local copies, waits for them, and re-layouts  2.27 us (5%)
  between operations  0.72 us (1%)
    all_to_all x1, blocking collectives, shards(): got = lax.all_to_all(send, 'wide', split_axis=0, concat_axis=0, tiled=True)  21.4 us
    ppermute x2, waiting for transfers between devices, over_wide(): lax.ppermute(second, axes, [(j, i) for i, j in path])  3.3 us
    ppermute x2, starting transfers between devices, over_wide(): lax.ppermute(first, axes, path)  3.07 us
    pallas_call x1, Pallas kernels, shards(): call(inner_two_kernel, 'substep_two_inner', [VMEM] * 4, [((19, 8, 32, 128...  2.6 us
    pallas_call x1, Pallas kernels, shards(): call(inner_one_kernel, 'substep_one_inner', [SMEM] + [VMEM] * 3, [(ext_sh...  2.58 us
    unnamed x16, local copies, waits for them, and re-layouts  2.27 us
    ppermute x1, starting transfers between devices, over_quad(): lax.ppermute(up, 'quad', ring)  2.19 us
    pallas_call x1, Pallas kernels, shards(): call(cells_kernel, 'collide_cells', [SMEM] + [VMEM] * 3, [(ext_shape, VME...  1.99 us
  transfers between devices with their start and end apart: 6, of which 3 were waited for; matrix products, arithmetic and copies ran while one was open for 0% of the time, Pallas kernels for 14%

profile of v2, /device:TPU:1, one launch (start us, length us, event | category | flops | bytes accessed | tf_op | source)
XLA Modules:
  0.0 49.8 jit_solution(10542327448733370101)
XLA Ops:
  0.6 0.0 copy-start
  0.6 2.0 %collide_rows.1 = (f32[536,128]{1,0:T(8,128)S(1)}, f32[536,128]{1,0:T(8,128)S(1)}, f32[6,16,128]{2,1,0:T(8,128)S(1)}, f32[6,16,128]{2,1,0:T(8,128)S(1)}) custom-call(f32[15]{0:T(128)} %rates.5, f32[19,8,32,128]{3,2,1,0:T(8,128)} %f.3, s32[8,32,128]{2,1,0:T(8,128)} %solid.3, s32[2,8,32]{2,1,0:T(8,128)} %active.3, f32[19,2,16,128]{3,2,1,0:T(8,128)} %cp.3, ...), custom_call_target="tpu_custom_call" | custom-call | tf_op jit(solution)/shard_map/collide_rows/pallas_call | solution.py:643
  2.6 2.2 %collective-permute-start = (f32[536,128]{1,0:T(8,128)S(1)}, f32[536,128]{1,0:T(8,128)S(1)}, u32[]{:S(2)}, u32[]{:S(2)}) collective-permute-start(f32[536,128]{1,0:T(8,128)S(1)} %get-tuple-element.23), channel_id=1, source_target_pairs={{0,1},{1,2},{2,3},{3,0},{4,5},{5,6},{6,7},{7,4},{8,9},{9,10},{10,1... | collective-permute-start | bytes 823304 | tf_op jit(solution)/shard_map/ppermute | solution.py:622
  4.8 1.5 %collective-permute-start.1 = (f32[536,128]{1,0:T(8,128)S(1)}, f32[536,128]{1,0:T(8,128)S(1)}, u32[]{:S(2)}, u32[]{:S(2)}) collective-permute-start(f32[536,128]{1,0:T(8,128)S(1)} %get-tuple-element.24), channel_id=1, source_target_pairs={{1,0},{2,1},{3,2},{0,3},{5,4},{6,5},{7,6},{4,7},{9,8},{10,9},{11,1... | collective-permute-start | bytes 823304 | tf_op jit(solution)/shard_map/ppermute | solution.py:622
  6.3 0.0 copy-done
  6.3 0.0 copy-start.2
  6.3 0.9 %copy-done.2 = s32[8,32,128]{2,1,0:T(8,128)S(1)} copy-done((s32[8,32,128]{2,1,0:T(8,128)S(1)}, s32[8,32,128]{2,1,0:T(8,128)}, u32[]{:S(2)}) %copy-start.2) | copy-done | bytes 131096
  7.2 0.0 copy-start.5
  7.2 0.7 %copy-done.5 = s32[2,8,32]{2,1,0:T(8,128)S(1)} copy-done((s32[2,8,32]{2,1,0:T(8,128)S(1)}, s32[2,8,32]{2,1,0:T(8,128)}, u32[]{:S(2)}) %copy-start.5) | copy-done | bytes 2072
  7.9 0.0 copy-start.6
  7.9 0.7 %copy-done.6 = f32[15]{0:T(128)S(1)} copy-done((f32[15]{0:T(128)S(1)}, f32[15]{0:T(128)}, u32[]{:S(2)}) %copy-start.6) | copy-done | bytes 84
  8.6 0.0 copy-start.7
  8.6 2.0 %collide_cells.1 = (f32[20,8,40,128]{3,2,1,0:T(8,128)S(1)}, f32[15,8,128]{2,1,0:T(8,128)S(1)}) custom-call(f32[15]{0:T(128)S(1)} %copy-done.6, f32[19,8,32,128]{3,2,1,0:T(8,128)S(1)} %copy-done, s32[8,32,128]{2,1,0:T(8,128)S(1)} %copy-done.2, s32[2,8,32]{2,1,0:T(8,128)S(1)} %copy-done.5), custom_call_target="tpu_custom_call" | custom-call | flops 9830400 | bytes 5242880 | tf_op jit(solution)/shard_map/collide_cells/pallas_call | solution.py:669
  10.6 1.8 %collective-permute-done.ru = f32[536,128]{1,0:T(8,128)S(1)} collective-permute-done((f32[536,128]{1,0:T(8,128)S(1)}, f32[536,128]{1,0:T(8,128)S(1)}, u32[]{:S(2)}, u32[]{:S(2)}) %collective-permute-start) | collective-permute-done | bytes 274464 | tf_op jit(solution)/shard_map/ppermute | solution.py:622
  12.4 0.0 collective-permute-done.1.rd
  12.4 0.1 pack_faces.1
  12.5 3.0 %collective-permute-start.2 = (f32[38,8,128]{2,1,0:T(8,128)S(1)}, f32[38,8,128]{2,1,0:T(8,128)S(1)}, u32[]{:S(2)}, u32[]{:S(2)}) collective-permute-start(f32[38,8,128]{2,1,0:T(8,128)S(1)} %get-tuple-element.28), channel_id=1, source_target_pairs={{0,4},{4,8},{8,12},{12,16},{16,20},{20,24},{24,28},{28,32},{32,36}... | collective-permute-start | bytes 466952 | tf_op jit(solution)/shard_map/ppermute | solution.py:634
  15.4 0.0 collective-permute-start.3
  15.4 0.0 copy-done.7
  15.5 2.6 %substep_one_inner.1 = (f32[20,8,40,128]{3,2,1,0:T(8,128)S(1)}, f32[19,8,40,128]{3,2,1,0:T(8,128)S(1)}, f32[19,8,40,128]{3,2,1,0:T(8,128)S(1)}) custom-call(f32[15]{0:T(128)S(1)} %copy-done.7, f32[20,8,40,128]{3,2,1,0:T(8,128)S(1)} %get-tuple-element.22.ext_in.ext, f32[536,128]{1,0:T(8,128)S(1)} %collective-permute-done.ru, ...), custom_call_target="tpu_custom_call" | custom-call | flops 7372800 | bytes 3932160 | tf_op jit(solution)/shard_map/substep_one_inner/pallas_call | solution.py:685
  18.0 0.0 collective-permute-done.2.ra
  18.0 2.1 %collective-permute-done.3.rb = f32[38,8,128]{2,1,0:T(8,128)S(1)} collective-permute-done((f32[38,8,128]{2,1,0:T(8,128)S(1)}, f32[38,8,128]{2,1,0:T(8,128)S(1)}, u32[]{:S(2)}, u32[]{:S(2)}) %collective-permute-start.3) | collective-permute-done | bytes 155680 | tf_op jit(solution)/shard_map/ppermute | solution.py:635
  20.1 1.1 %substep_one_faces.1 = (f32[19,8,40,128]{3,2,1,0:T(8,128)S(1)}, f32[19,8,40,128]{3,2,1,0:T(8,128)S(1)}, f32[25,8,128]{2,1,0:T(8,128)S(1)}, f32[25,8,128]{2,1,0:T(8,128)S(1)}) custom-call(f32[15]{0:T(128)S(1)} %copy-done.7, f32[20,8,40,128]{3,2,1,0:T(8,128)S(1)} %get-tuple-element.25.ext, ...), custom_call_target="tpu_custom_call", output_to_operand_aliasing={{0}: (4, {}), {1}: (5, {})} | custom-call | tf_op jit(solution)/shard_map/substep_one_faces/pallas_call | solution.py:692
  21.2 0.1 collective-permute-start.4
  21.3 0.5 collective-permute-start.5
  21.8 2.6 %substep_two_inner.1 = (f32[19,8,32,128]{3,2,1,0:T(8,128)}, f32[4,768,128]{2,1,0:T(8,128)S(1)}, f32[1024,128]{1,0:T(8,128)S(1)}) custom-call(f32[20,8,40,128]{3,2,1,0:T(8,128)S(1)} %get-tuple-element.25.ext, f32[19,8,40,128]{3,2,1,0:T(8,128)S(1)} %get-tuple-element.32.first, f32[19,8,40,128]{3,2,1,0:T(8,128)S(1)} %get-tuple-element.33.src2, ...), custom_call_target="tpu_custom_call" | custom-call | flops 7372800 | bytes 3932160 | tf_op jit(solution)/shard_map/substep_two_inner/pallas_call | solution.py:701
  24.4 0.0 collective-permute-done.4.ra
  24.4 1.2 %collective-permute-done.5.rb = f32[25,8,128]{2,1,0:T(8,128)S(1)} collective-permute-done((f32[25,8,128]{2,1,0:T(8,128)S(1)}, f32[25,8,128]{2,1,0:T(8,128)S(1)}, u32[]{:S(2)}, u32[]{:S(2)}) %collective-permute-start.5) | collective-permute-done | bytes 102432 | tf_op jit(solution)/shard_map/ppermute | solution.py:635
  25.6 0.0 copy-start.1
  25.6 0.0 copy-start.3
  25.6 0.0 copy-start.4
  25.6 1.6 %substep_two_faces.1 = (f32[1024,128]{1,0:T(8,128)S(1)}, f32[19,8,32,128]{3,2,1,0:T(8,128)}) custom-call(f32[20,8,40,128]{3,2,1,0:T(8,128)S(1)} %get-tuple-element.25.ext, f32[19,8,40,128]{3,2,1,0:T(8,128)S(1)} %get-tuple-element.32.first, f32[19,8,40,128]{3,2,1,0:T(8,128)S(1)} %get-tuple-element.33.src2, ...), custom_call_target="tpu_custom_call", output_to_operand_aliasing={{0}: (7, {}), {1}: (8, {})} | custom-call | tf_op jit(solution)/shard_map/substep_two_faces/pallas_call | solution.py:709
  27.2 21.4 %all_to_all.11 = f32[32,32,128]{2,1,0:T(8,128)S(1)} all-to-all(f32[32,32,128]{2,1,0:T(8,128)S(1)} %bitcast.3), channel_id=1, replica_groups=mesh['wide'=32,'quad'=4] {'wide'}, dimensions={0} | all-to-all | bytes 1048576 | tf_op jit(solution)/shard_map/all_to_all | solution.py:717
  48.6 0.0 copy-done.1
  48.6 0.0 copy-done.3
  48.6 0.0 copy-done.4
  48.6 1.1 %coarse_step.1 = f32[19,2,16,128]{3,2,1,0:T(8,128)} custom-call(f32[1024,128]{1,0:T(8,128)S(1)} %bitcast.2, f32[15,8,128]{2,1,0:T(8,128)S(1)} %get-tuple-element.34.crate, f32[19,2,16,128]{3,2,1,0:T(8,128)S(1)} %copy-done.1, s32[2,16,128]{2,1,0:T(8,128)S(1)} %copy-done.3, s32[2,16,128]{2,1,0:T(8,128)S(1)} %copy-done.4, ...), custom_call_target="tpu_custom_call" | custom-call | tf_op jit(solution)/shard_map/coarse_step/pallas_call | solution.py:718
Async XLA Ops:
  0.6 5.7 %copy-start = (f32[19,8,32,128]{3,2,1,0:T(8,128)S(1)}, f32[19,8,32,128]{3,2,1,0:T(8,128)}, u32[]{:S(2)}) copy-start(f32[19,8,32,128]{3,2,1,0:T(8,128)} %f.3) | copy-start | bytes 7471108
  2.6 9.8 %collective-permute-start = (f32[536,128]{1,0:T(8,128)S(1)}, f32[536,128]{1,0:T(8,128)S(1)}, u32[]{:S(2)}, u32[]{:S(2)}) collective-permute-start(f32[536,128]{1,0:T(8,128)S(1)} %get-tuple-element.23), channel_id=1, source_target_pairs={{0,1},{1,2},{2,3},{3,0},{4,5},{5,6},{6,7},{7,4},{8,9},{9,10},{10,1... | collective-permute-start | bytes 823304 | tf_op jit(solution)/shard_map/ppermute | solution.py:622
  4.8 7.6 %collective-permute-start.1 = (f32[536,128]{1,0:T(8,128)S(1)}, f32[536,128]{1,0:T(8,128)S(1)}, u32[]{:S(2)}, u32[]{:S(2)}) collective-permute-start(f32[536,128]{1,0:T(8,128)S(1)} %get-tuple-element.24), channel_id=1, source_target_pairs={{1,0},{2,1},{3,2},{0,3},{5,4},{6,5},{7,6},{4,7},{9,8},{10,9},{11,1... | collective-permute-start | bytes 823304 | tf_op jit(solution)/shard_map/ppermute | solution.py:622
  6.3 0.9 %copy-start.2 = (s32[8,32,128]{2,1,0:T(8,128)S(1)}, s32[8,32,128]{2,1,0:T(8,128)}, u32[]{:S(2)}) copy-start(s32[8,32,128]{2,1,0:T(8,128)} %solid.3) | copy-start | bytes 393220
  7.2 0.7 %copy-start.5 = (s32[2,8,32]{2,1,0:T(8,128)S(1)}, s32[2,8,32]{2,1,0:T(8,128)}, u32[]{:S(2)}) copy-start(s32[2,8,32]{2,1,0:T(8,128)} %active.3) | copy-start | bytes 6148
  7.9 0.7 %copy-start.6 = (f32[15]{0:T(128)S(1)}, f32[15]{0:T(128)}, u32[]{:S(2)}) copy-start(f32[15]{0:T(128)} %rates.5) | copy-start | bytes 184
  8.6 6.9 %copy-start.7 = (f32[15]{0:T(128)S(1)}, f32[15]{0:T(128)}, u32[]{:S(2)}) copy-start(f32[15]{0:T(128)} %rates.5) | copy-start | bytes 184
  12.5 5.6 %collective-permute-start.2 = (f32[38,8,128]{2,1,0:T(8,128)S(1)}, f32[38,8,128]{2,1,0:T(8,128)S(1)}, u32[]{:S(2)}, u32[]{:S(2)}) collective-permute-start(f32[38,8,128]{2,1,0:T(8,128)S(1)} %get-tuple-element.28), channel_id=1, source_target_pairs={{0,4},{4,8},{8,12},{12,16},{16,20},{20,24},{24,28},{28,32},{32,36}... | collective-permute-start | bytes 466952 | tf_op jit(solution)/shard_map/ppermute | solution.py:634
  15.4 4.7 %collective-permute-start.3 = (f32[38,8,128]{2,1,0:T(8,128)S(1)}, f32[38,8,128]{2,1,0:T(8,128)S(1)}, u32[]{:S(2)}, u32[]{:S(2)}) collective-permute-start(f32[38,8,128]{2,1,0:T(8,128)S(1)} %get-tuple-element.29), channel_id=1, source_target_pairs={{4,0},{8,4},{12,8},{16,12},{20,16},{24,20},{28,24},{32,28},{36,32}... | collective-permute-start | bytes 466952 | tf_op jit(solution)/shard_map/ppermute | solution.py:635
  21.2 3.2 %collective-permute-start.4 = (f32[25,8,128]{2,1,0:T(8,128)S(1)}, f32[25,8,128]{2,1,0:T(8,128)S(1)}, u32[]{:S(2)}, u32[]{:S(2)}) collective-permute-start(f32[25,8,128]{2,1,0:T(8,128)S(1)} %get-tuple-element.35), channel_id=1, source_target_pairs={{0,4},{4,8},{8,12},{12,16},{16,20},{20,24},{24,28},{28,32},{32,36}... | collective-permute-start | bytes 307208 | tf_op jit(solution)/shard_map/ppermute | solution.py:634
  21.3 4.4 %collective-permute-start.5 = (f32[25,8,128]{2,1,0:T(8,128)S(1)}, f32[25,8,128]{2,1,0:T(8,128)S(1)}, u32[]{:S(2)}, u32[]{:S(2)}) collective-permute-start(f32[25,8,128]{2,1,0:T(8,128)S(1)} %get-tuple-element.36), channel_id=1, source_target_pairs={{4,0},{8,4},{12,8},{16,12},{20,16},{24,20},{28,24},{32,28},{36,32}... | collective-permute-start | bytes 307208 | tf_op jit(solution)/shard_map/ppermute | solution.py:635
  25.6 23.0 %copy-start.1 = (f32[19,2,16,128]{3,2,1,0:T(8,128)S(1)}, f32[19,2,16,128]{3,2,1,0:T(8,128)}, u32[]{:S(2)}) copy-start(f32[19,2,16,128]{3,2,1,0:T(8,128)} %cp.3) | copy-start | bytes 933892
  25.6 23.0 %copy-start.3 = (s32[2,16,128]{2,1,0:T(8,128)S(1)}, s32[2,16,128]{2,1,0:T(8,128)}, u32[]{:S(2)}) copy-start(s32[2,16,128]{2,1,0:T(8,128)} %c_solid.3) | copy-start | bytes 49156
  25.6 23.0 %copy-start.4 = (s32[2,16,128]{2,1,0:T(8,128)S(1)}, s32[2,16,128]{2,1,0:T(8,128)}, u32[]{:S(2)}) copy-start(s32[2,16,128]{2,1,0:T(8,128)} %c_cov.3) | copy-start | bytes 49156

commit v3 on v2

v3 whole, which is shorter than its diff:
```python
import functools

import jax
import jax.numpy as jnp
from jax import lax
from jax.experimental import pallas as pl
from jax.experimental.pallas import tpu as pltpu
from jax.sharding import PartitionSpec as P

VEL = [
    (0, 0, 0),
    (1, 0, 0),
    (-1, 0, 0),
    (0, 1, 0),
    (0, -1, 0),
    (0, 0, 1),
    (0, 0, -1),
    (1, 1, 0),
    (-1, -1, 0),
    (1, -1, 0),
    (-1, 1, 0),
    (1, 0, 1),
    (-1, 0, -1),
    (1, 0, -1),
    (-1, 0, 1),
    (0, 1, 1),
    (0, -1, -1),
    (0, 1, -1),
    (0, -1, 1),
]
OPP = [0, 2, 1, 4, 3, 6, 5, 8, 7, 10, 9, 12, 11, 14, 13, 16, 15, 18, 17]


def moving(axis, sign):
    return [q for q in range(19) if VEL[q][axis] == sign]


XP, XM = moving(0, 1), moving(0, -1)
YP, YM = moving(1, 1), moving(1, -1)
ZP, ZM = moving(2, 1), moving(2, -1)
WALL = 1e30
WALL_TEST = 1e29
F32 = jnp.float32
MIB = 1 << 20

FACES = (0, 7)
INNER = (1, 2, 3, 4, 5, 6)
NEXT = ((1, XM), (6, XP))
ACROSS = [q for q in range(19) if VEL[q][0] == 0]
Y_COARSE = 130
Y_NEXT = 142
Y_FACES = 176
Y_INNER = 392
X_COARSE = 100
X_ALL = X_COARSE + 13
CHUNK = 25

FACTOR = [0.25] * 3 + [0.5] * 3 + [0.25] * 9

def collide(f, rate):
    r_xy, r_xz, r_yz, r_xx, r_yy, r_zz = rate[:6]
    r_xyy, r_xzz, r_yxx, r_yzz, r_zxx, r_zyy, r_xxyy, r_xxzz, r_yyzz = rate[6:]
    sx, dx = f[1] + f[2], f[1] - f[2]
    sy, dy = f[3] + f[4], f[3] - f[4]
    sz, dz = f[5] + f[6], f[5] - f[6]

    def plane(i):
        a, b = f[i] + f[i + 1], f[i + 2] + f[i + 3]
        c, d = f[i] - f[i + 1], f[i + 2] - f[i + 3]
        return a + b, a - b, c + d, c - d

    m_xxyy, m_xy, m_xyy, m_yxx = plane(7)
    m_xxzz, m_xz, m_xzz, m_zxx = plane(11)
    m_yyzz, m_yz, m_yzz, m_zyy = plane(15)
    m_xx = sx + (m_xxyy + m_xxzz)
    m_yy = sy + (m_xxyy + m_yyzz)
    m_zz = sz + (m_xxzz + m_yyzz)
    jx = dx + (m_xyy + m_xzz)
    jy = dy + (m_yxx + m_yzz)
    jz = dz + (m_zxx + m_zyy)
    rho = (f[0] + sx) + (sy + sz) + ((m_xxyy + m_xxzz) + m_yyzz)
    inv = 1.0 / rho
    ux, uy, uz = jx * inv, jy * inv, jz * inv
    xx, yy, zz = jx * ux, jy * uy, jz * uz
    third = rho * (1.0 / 3.0)
    ninth = rho * (1.0 / 9.0)
    jx3, jy3, jz3 = jx * (1.0 / 3.0), jy * (1.0 / 3.0), jz * (1.0 / 3.0)
    xx3, yy3, zz3 = xx * (1.0 / 3.0), yy * (1.0 / 3.0), zz * (1.0 / 3.0)
    h_xx = (m_xx - third - xx) * r_xx
    h_yy = (m_yy - third - yy) * r_yy
    h_zz = (m_zz - third - zz) * r_zz
    post = [None] * 19

    def diagonal(i, fourth, cross, first, second):
        p, m = fourth + cross, fourth - cross
        s, d = first + second, first - second
        post[i] = f[i] - (p + s)
        post[i + 1] = f[i + 1] - (p - s)
        post[i + 2] = f[i + 2] - (m + d)
        post[i + 3] = f[i + 3] - (m - d)

    a_xy = (m_xxyy - ninth - (xx3 + yy3 - 0.5 * zz3)) * r_xxyy
    a_xz = (m_xxzz - ninth - (xx3 + zz3 - 0.5 * yy3)) * r_xxzz
    a_yz = (m_yyzz - ninth - (yy3 + zz3 - 0.5 * xx3)) * r_yyzz
    c_xyy, c_yxx = (m_xyy - jx3) * r_xyy, (m_yxx - jy3) * r_yxx
    c_xzz, c_zxx = (m_xzz - jx3) * r_xzz, (m_zxx - jz3) * r_zxx
    c_yzz, c_zyy = (m_yzz - jy3) * r_yzz, (m_zyy - jz3) * r_zyy
    diagonal(7, a_xy, (m_xy - jx * uy) * r_xy, c_xyy, c_yxx)
    diagonal(11, a_xz, (m_xz - jx * uz) * r_xz, c_xzz, c_zxx)
    diagonal(15, a_yz, (m_yz - jy * uz) * r_yz, c_yzz, c_zyy)

    def straight(i, h, a, c):
        p, n = h - 2.0 * a, 2.0 * c
        post[i] = f[i] - (p - n)
        post[i + 1] = f[i + 1] - (p + n)

    straight(1, h_xx, a_xy + a_xz, c_xyy + c_xzz)
    straight(3, h_yy, a_xy + a_yz, c_yxx + c_yzz)
    straight(5, h_zz, a_xz + a_yz, c_zxx + c_zyy)
    post[0] = f[0] + (2.0 * (h_xx + h_yy + h_zz) - 4.0 * (a_xy + a_xz + a_yz))
    return post


def iota(shape, axis):
    return lax.broadcasted_iota(jnp.int32, shape, axis)


def write_rates(rates, fine, coarse):
    for i in range(15):
        rate = jnp.full((8, 128), rates[i], F32)
        fine[i] = rate * FACTOR[i]
        coarse[i] = FACTOR[i] / (2.0 / rate - 0.5)


def read_rates(ref):
    return [ref[i] for i in range(15)]


def wall_where(code, value):
    return jnp.where(code > 0.5, value, WALL)


def grown_blocks(active):
    grow = (iota((32, 128), 1) // 4 == iota((32, 128), 0)).astype(F32)
    return jnp.dot(active.astype(F32), grow, preferred_element_type=F32)


def edges():
    quad, wide = lax.axis_index("quad"), lax.axis_index("wide")
    return (
        (quad > 0).astype(F32),
        (quad < lax.axis_size("quad") - 1).astype(F32),
        (wide > 0).astype(F32),
        (wide < lax.axis_size("wide") - 1).astype(F32),
    )


def collide_plane(x, f, solid, on, fine, ext):
    for t in range(4):
        rows = pl.ds(8 * t, 8)
        old = [f[q, rows] for q in range(19)]
        fluid = solid[x, rows] == 0
        live = fluid & (on[x // 4, rows] > 0.5)
        post = collide(old, fine)
        for q in range(19):
            ext[q, x, rows] = jnp.where(live, post[q], old[q])
        ext[19, x, rows] = jnp.where(fluid, 1.0 + on[x // 4, rows], 0.0)


def grow(active, on):
    grow_y = (iota((32, 8), 0) // 4 == iota((32, 8), 1)).astype(F32)
    for b in range(2):
        on[b] = jnp.dot(grow_y, grown_blocks(active[b]), preferred_element_type=F32)


def pack_rows(planes, ext, yu, yd):
    fourth = 60 * len(planes)
    for n, x in enumerate(planes):
        for q in range(20):
            start = 60 * n + 3 * q
            yu[start : start + 3] = ext[q, x, 24:32][5:8]
            yd[start : start + 3] = ext[q, x, 0:8][0:3]
        for i in range(5):
            start = fourth + len(planes) * i + n
            yu[start : start + 1] = wall_where(ext[19, x, 24:32], ext[YP[i], x, 24:32])[4:5]
            yd[start : start + 1] = wall_where(ext[19, x, 0:8], ext[YM[i], x, 0:8])[3:4]


def faces_first_kernel(
    rates_in, f, solid_in, active_in, cp, c_solid, c_cov,
    ext, yu, yd, zu, zd, solid, on, frate, crate,
    rates, held, active, cps, c_solids, c_covs, sems,
):
    small = [
        pltpu.make_async_copy(rates_in, rates, sems.at[0]),
        pltpu.make_async_copy(solid_in, solid, sems.at[1]),
        pltpu.make_async_copy(active_in, active, sems.at[2]),
    ]
    coarse_copies = [
        pltpu.make_async_copy(cp, cps, sems.at[3]),
        pltpu.make_async_copy(c_solid, c_solids, sems.at[4]),
        pltpu.make_async_copy(c_cov, c_covs, sems.at[5]),
    ]
    planes = [
        pltpu.make_async_copy(f.at[:, x], held.at[n], sems.at[6 + n])
        for n, x in enumerate((0, 7, 1, 6))
    ]
    for copy in small + planes + coarse_copies:
        copy.start()
    for copy in small:
        copy.wait()
    write_rates(rates, frate, crate)
    fine = read_rates(frate)
    grow(active, on)
    for n, x in enumerate((0, 7, 1, 6)):
        planes[n].wait()
        collide_plane(x, held.at[n], solid, on, fine, ext)
    pack_rows(FACES, ext, yu, yd)
    for e, (x, values) in enumerate(NEXT):
        for i, q in enumerate(values):
            start = Y_NEXT + 15 * e + 3 * i
            high = wall_where(ext[19, x, 24:32], ext[q, x, 24:32])
            low = wall_where(ext[19, x, 0:8], ext[q, x, 0:8])
            yu[start : start + 3] = high[5:8]
            yd[start : start + 3] = low[0:3]
            fourth = Y_NEXT + 30 + e
            if q in YP:
                yu[fourth : fourth + 1] = high[4:5]
            if q in YM:
                yd[fourth : fourth + 1] = low[3:4]
    for copy in coarse_copies:
        copy.wait()
    coarse = read_rates(crate)
    for z in range(2):
        for t in range(2):
            rows = pl.ds(8 * t, 8)
            post = collide([cps[q, z, rows] for q in range(19)], coarse)
            code = jnp.where(c_solids[z, rows] == 0, 1.0 + c_covs[z, rows].astype(F32), 0.0)
            values, to = (ZP, zu) if z == 1 else (ZM, zd)
            for i in range(5):
                to[i, rows] = post[values[i]]
            to[5, rows] = code
            values, to, row = (YM, yd, 0) if t == 0 else (YP, yu, 7)
            for i in range(6):
                place = Y_COARSE + 6 * z + i
                value = code if i == 5 else post[values[i]]
                to[place : place + 1] = value[row : row + 1]


def inner_first_kernel(frate, f, solid, on, ext_in, ext, yu, yd):
    fine = read_rates(frate)

    def plane(x, carry):
        collide_plane(x, f.at[:, x], solid, on, fine, ext)
        return carry

    lax.fori_loop(2, 6, plane, 0)
    pack_rows(INNER, ext, yu, yd)


def fill_rows(q, planes, n, ru, rd, to):
    start = 60 * n + 3 * q
    to[0:3] = rd[start : start + 3]
    to[5:8] = ru[start : start + 3]
    fourth = 60 * len(planes) + n
    if q in YM:
        place = fourth + len(planes) * YM.index(q)
        to[3:4] = rd[place : place + 1]
    if q in YP:
        place = fourth + len(planes) * YP.index(q)
        to[4:5] = ru[place : place + 1]


def fill_code(n, ru, rd, to, has_prev, has_next):
    start = 60 * n + 57
    to[0:3] = rd[start : start + 3] * has_next
    to[5:8] = ru[start : start + 3] * has_prev
    to[3:4] = jnp.full((1, 128), has_next, F32)
    to[4:5] = jnp.full((1, 128), has_prev, F32)


def upwards():
    return lax.axis_index("wide") % 2 == 0


def face_planes_kernel(ext, held):
    for face, x in enumerate(FACES):
        for q in range(20):
            held[q, face, 0:32] = ext[q, x, 0:32]
        near, values = NEXT[face]
        for i, q in enumerate(values):
            held[20 + i, face, 0:32] = wall_where(ext[19, near, 0:32], ext[q, near, 0:32])


def faces_kernel(planes, zu, zd, ru, rd, pa, pb, held, beyond, tile, both):
    has_prev, has_next, _, _ = edges()
    lane = iota((40, 128), 1)
    inside = jnp.where(iota((8, 128), 0) < 4, has_next, has_prev) > 0.5
    for face, x in enumerate(FACES):
        place = jnp.where(upwards() == (x == 7), 0, 1)
        for q in range(19):
            held[q, 0, 0:32] = planes[q, face, 0:32]
            fill_rows(q, FACES, face, ru, rd, held.at[q, 0, 32:40])
        held[19, 0, 0:32] = planes[19, face, 0:32]
        fill_code(face, ru, rd, held.at[19, 0, 32:40], has_prev, has_next)
        values = NEXT[face][1]
        for i, q in enumerate(values):
            beyond[i, 0:32] = planes[20 + i, face, 0:32]
            start = Y_NEXT + 15 * face + 3 * i
            fourth = Y_NEXT + 30 + face
            tile[0:3] = rd[start : start + 3]
            tile[5:8] = ru[start : start + 3]
            if q in YM:
                tile[3:4] = rd[fourth : fourth + 1]
            if q in YP:
                tile[4:5] = ru[fourth : fourth + 1]
            beyond[i, 32:40] = jnp.where(inside, tile[...], WALL)
        code = held[19, 0]
        live, open_cells = code > 1.5, {0: code > 0.5}
        outer = (VEL[values[0]][0], lambda q: beyond[values.index(q)])
        for i in range(20):
            if i < 14:
                q = (ACROSS + values)[i]
                part = streamed(q, 0, held, open_cells, live, lane, outer)
            elif i < 19:
                part = wall_where(code, held[values[i - 14], 0])
            else:
                part = code
            for t in range(5):
                both[place, 5 * i + t] = part[8 * t : 8 * t + 8]
        z, arriving, leaving, from_ = ((0, 17, 16, zd), (1, 15, 18, zu))[face]
        for i in range(6):
            for t in range(2):
                both[place, X_COARSE + 2 * i + t] = from_[i, 8 * t : 8 * t + 8]

        def arrived(rows, i):
            row = Y_COARSE + 6 * z + i
            return rows[row : row + 1]

        tile[0:1] = arrived(ru, YP.index(arriving))
        tile[1:2] = arrived(rd, YM.index(leaving))
        tile[2:3] = arrived(ru, 5) * has_prev
        tile[3:4] = arrived(rd, 5) * has_next
        both[place, X_COARSE + 12] = tile[...]
    pa[...] = both[0]
    pb[...] = both[1]


def streamed(q, x, values, open_cells, live, lane, outer=None):
    cx, cy, cz = VEL[q]
    if q == 0:
        return values[0, x]
    if cx and outer is not None and outer[0] == cx:
        value = outer[1](q)
    else:
        value = jnp.where(open_cells[cx], values[q, x - cx], WALL)
    if cy:
        value = pltpu.roll(value, cy % 40, 0)
    if cz:
        value = pltpu.roll(value, cz % 128, 1)
    open_ = value < WALL_TEST
    if cz:
        open_ = open_ & (lane != (0 if cz == 1 else 127))
    return jnp.where(live, jnp.where(open_, value, values[OPP[q], x]), values[q, x])


def step_plane(x, ext, first, src2, fine, lane, outer=None):
    open_cells = {}
    for cx in (-1, 0, 1):
        if outer is None or outer[0] != cx:
            open_cells[cx] = ext[19, x - cx] > 0.5
    live = ext[19, x] > 1.5
    for q in range(19):
        first[q, x] = streamed(q, x, ext, open_cells, live, lane, outer)
    for t in range(5):
        rows = pl.ds(8 * t, 8)
        live_t = ext[19, x, rows] > 1.5
        old = [first[q, x, rows] for q in range(19)]
        post = collide(old, fine)
        for q in range(19):
            src2[q, x, rows] = jnp.where(live_t, post[q], old[q])


def fill_kernel(ext_in, ru, rd, ru2, rd2, ext):
    has_prev, has_next, _, _ = edges()
    for planes, up, down in ((FACES, ru, rd), (INNER, ru2, rd2)):
        for n, x in enumerate(planes):
            for q in range(19):
                fill_rows(q, planes, n, up, down, ext.at[q, x, 32:40])
            fill_code(n, up, down, ext.at[19, x, 32:40], has_prev, has_next)


def second_plane(x, ext, first, src2, lane, emit, outer=None):
    open_cells = {}
    for cx in (-1, 0, 1):
        if outer is None or outer[0] != cx:
            open_cells[cx] = ext[19, x - cx] > 0.5
    live = ext[19, x] > 1.5
    for q in range(19):
        emit(q, streamed(q, x, src2, open_cells, live, lane, outer), first[q, x])


def own_planes():
    z_pair = iota((32, 128), 1) // 2
    plane = 2 * iota((32, 128), 0)
    return [jnp.where(z_pair == plane + k, 0.0625, 0.0) for k in range(2)]


def picked(rows, cells):
    return lax.dot_general(
        rows,
        cells,
        (((1,), (1,)), ((), ())),
        precision=lax.Precision.HIGHEST,
        preferred_element_type=F32,
    )


def destinations(sums, coarse, raw, mixed, rest, send, b):
    even = iota((8, 128), 1) % 2 == 0

    def alone(value, shift):
        value = jnp.where(even, 16.0 * value, 0.0)
        return pltpu.roll(value, 2 * shift % 128, 1) if shift else value

    for t in range(3):
        cells = []
        for q in range(19):
            start = 40 * q + 16 * t
            value = sums[pl.ds(start, 8, stride=2)] + sums[pl.ds(start + 1, 8, stride=2)]
            if t < 2:
                place = 16 * q + 8 * t
                if q < 16:
                    raw[place : place + 8] = value
                else:
                    mixed[0, place - 256 : place - 248] = value
                    mixed[1, place - 256 : place - 248] = value
            cells.append((value + pltpu.roll(value, 127, 1)) * 0.0625)
        post = collide(cells, coarse)
        if t < 2:
            for i in range(5):
                place = 48 + 16 * i + 8 * t
                mixed[0, place : place + 8] = alone(post[ZP[i]], 1)
                mixed[1, place : place + 8] = alone(post[ZM[i]], -1)
        else:
            last = [alone(post[q], 0)[3:4] for q in YP] + [alone(post[q], 0)[0:1] for q in YM]
            for k in range(2):
                corners = ((15, 18), (17, 16))[k]
                shift = (1, -1)[k]
                here = last + [alone(post[corners[0]], shift)[3:4], alone(post[corners[1]], shift)[0:1]]
                for i in range(12):
                    rest[pl.ds(64 * k + 12 * b + i, 1)] = here[i]
    planes = own_planes()
    both = jnp.concatenate(planes, axis=0)
    for n in range(2):
        got = picked(both, raw[128 * n : 128 * n + 128])
        for k in range(2):
            send[pl.ds(6 * b + 2 * k + n, 32, stride=CHUNK)] = got[32 * k : 32 * k + 32]
    for k in range(2):
        send[pl.ds(6 * b + 4 + k, 32, stride=CHUNK)] = picked(planes[k], mixed[k])


def inner_kernel(
    frate, ext, crate, first, src2, fine_out, send, rest, planes, sums, raw, mixed, sem
):
    fine = read_rates(frate)
    lane = iota((40, 128), 1)
    rest[...] = jnp.zeros(rest.shape, F32)

    def substep_one(x, carry):
        step_plane(x, ext, first, src2, fine, lane)
        return carry

    lax.fori_loop(1, 7, substep_one, 0)

    def out_copy(x):
        return pltpu.make_async_copy(planes.at[x - 2], fine_out.at[:, x], sem.at[x - 2])

    def pair(b, carry):
        for e in range(2):
            x = 2 * b + e

            def emit(q, value, before):
                planes[x - 2, q] = value[0:32]
                rows = pl.ds(40 * q, 40)
                total = value + before
                sums[b - 1, rows] = total if e == 0 else sums[b - 1, rows] + total

            second_plane(x, ext, first, src2, lane, emit)
            out_copy(x).start()
        return carry

    lax.fori_loop(1, 3, pair, 0)
    coarse = read_rates(crate)
    for b in (1, 2):
        destinations(sums.at[b - 1], coarse, raw, mixed, rest, send, b)
    for x in range(2, 6):
        out_copy(x).wait()


def side(
    left, message, inside, frate, ext, crate, first, src2, send, rest, fine_out,
    planes, sums, raw, mixed, before, outside, sem,
):
    fine = read_rates(frate)
    lane = iota((40, 128), 1)
    entering, leaving = (XP, XM) if left else (XM, XP)
    cx = 1 if left else -1
    x, near, b = (0, 1, 0) if left else (7, 6, 3)

    def arrived(i):
        return message[5 * i : 5 * i + 5].reshape(40, 128)

    def part(i):
        return jnp.where(inside > 0.5, arrived(i), WALL)

    code = arrived(19)
    for i, q in enumerate(ACROSS + entering):
        before[q] = arrived(i)
    open_cells = ext[19, x] > 0.5
    for q in leaving:
        _, cy, cz = VEL[q]
        value = jnp.where(open_cells, ext[q, x], WALL)
        if cy:
            value = pltpu.roll(value, cy % 40, 0)
        if cz:
            value = pltpu.roll(value, cz % 128, 1)
        open_ = value < WALL_TEST
        if cz:
            open_ = open_ & (lane != (0 if cz == 1 else 127))
        before[q] = jnp.where(open_, value, arrived(14 + entering.index(OPP[q])))
    for t in range(5):
        rows = pl.ds(8 * t, 8)
        code_t = message[95 + t] * inside
        old = [before[q, rows] for q in range(19)]
        post = collide(old, fine)
        for i, q in enumerate(entering):
            value = jnp.where(code_t > 1.5, post[q], old[q])
            outside[i, rows] = wall_where(code_t, value)
    step_plane(
        x, ext, first, src2, fine, lane, (cx, lambda q: part(14 + entering.index(q)))
    )
    copies = []
    for e, (plane, outer) in enumerate(
        ((x, (cx, lambda q: outside[entering.index(q)])), (near, None))
    ):

        def emit(q, value, earlier):
            planes[e, q] = value[0:32]
            rows = pl.ds(40 * q, 40)
            total = value + earlier
            sums[rows] = total if e == 0 else sums[rows] + total

        second_plane(plane, ext, first, src2, lane, emit, outer)
        copy = pltpu.make_async_copy(planes.at[e], fine_out.at[:, plane], sem.at[e])
        copy.start()
        copies.append(copy)
    destinations(sums, read_rates(crate), raw, mixed, rest, send, b)
    for copy in copies:
        copy.wait()


def side_kernel(
    second, frate, ext, crate, message, first_in, src2_in, send_in, rest_in, fine_in,
    first, src2, send, rest, fine_out, planes, sums, raw, mixed, before, outside, sem,
):
    _, _, has_left, has_right = edges()
    on_left = upwards() if second else jnp.logical_not(upwards())
    refs = (
        frate, ext, crate, first, src2, send, rest, fine_out,
        planes, sums, raw, mixed, before, outside, sem,
    )

    @pl.when(on_left)
    def _():
        side(True, message, has_left, *refs)

    @pl.when(jnp.logical_not(on_left))
    def _():
        side(False, message, has_right, *refs)

    if second:
        of_first, of_second = (picked(plane, rest[...]) for plane in own_planes())
        send[pl.ds(CHUNK - 1, 32, stride=CHUNK)] = jnp.where(
            iota((32, 128), 1) < 64, of_first, of_second
        )


def coarse_kernel(
    got, crate, cp, c_solid, c_cov, ru, rd, ra, rb, out, mesh, turned, rest, walled, source, message
):
    has_prev, has_next, has_left, has_right = edges()
    coarse = read_rates(crate)
    for m in range(6):
        for b in range(4):
            mesh[m, pl.ds(b, 32, stride=4)] = got[pl.ds(6 * b + m, 32, stride=CHUNK)]
    left = got[pl.ds(CHUNK - 1, 32, stride=CHUNK)]
    for b in range(4):
        mesh[6, pl.ds(b, 32, stride=4)] = pltpu.roll(left, -12 * b % 128, 1) if b else left
    for k in range(2):
        for n, m in enumerate((2 * k, 2 * k + 1, 4 + k)):
            turned[k, 128 * n : 128 * n + 128] = mesh[m].T
    rest[...] = mesh[6].T

    goes_up = upwards()
    for i in range(13):
        first, second = ra[X_COARSE + i], rb[X_COARSE + i]
        message[0, i] = jnp.where(goes_up, second, first)
        message[1, i] = jnp.where(goes_up, first, second)

    def pick(code, here, there):
        return jnp.where(code > 1.5, here, jnp.where(code > 0.5, there, WALL))

    def arrived(from_, place):
        return from_[Y_COARSE + place : Y_COARSE + place + 1]

    for k in range(2):
        for t in range(2):
            rows = pl.ds(8 * t, 8)
            fluid = c_solid[k, rows] == 0
            covered = c_cov[k, rows] == 1
            old = []
            for q in range(19):
                start = 16 * q + 8 * t
                old.append(jnp.where(covered, turned[k, start : start + 8], cp[q, k, rows]))
            post = collide(old, coarse)
            for q in range(19):
                value = jnp.where(fluid, post[q], old[q])
                source[q, k + 1, rows] = value
                walled[q, k + 1, rows] = jnp.where(fluid, value, WALL)
        prev_code = arrived(ru, 6 * k + 5) * has_prev
        next_code = arrived(rd, 6 * k + 5) * has_next
        for i in range(5):
            walled[YP[i], k + 1, 23:24] = pick(
                prev_code, rest[64 * k + i : 64 * k + i + 1], arrived(ru, 6 * k + i)
            )
            walled[YM[i], k + 1, 16:17] = pick(
                next_code, rest[64 * k + 5 + i : 64 * k + 6 + i], arrived(rd, 6 * k + i)
            )
        values, from_, z, inside = ((ZP, message.at[0], 0, has_left), (ZM, message.at[1], 3, has_right))[k]
        prev_q, next_q = ((15, 18), (17, 16))[k]
        for t in range(2):
            code = from_[10 + t] * inside
            for i in range(5):
                start = 304 + 16 * i + 8 * t
                walled[values[i], z, 8 * t : 8 * t + 8] = pick(
                    code, turned[k, start : start + 8], from_[2 * i + t]
                )
        walled[prev_q, z, 23:24] = pick(
            from_[12, 2:3] * inside, rest[64 * k + 10 : 64 * k + 11], from_[12, 0:1]
        )
        walled[next_q, z, 16:17] = pick(
            from_[12, 3:4] * inside, rest[64 * k + 11 : 64 * k + 12], from_[12, 1:2]
        )

    lane = iota((16, 128), 1)
    for z in (1, 2):
        fluid = c_solid[z - 1] == 0
        for q in range(19):
            cx, cy, cz = VEL[q]
            value = walled[q, z - cz]
            if cy:
                value = pltpu.roll(value, cy % 24, 0)
            value = value[0:16]
            if cx:
                value = pltpu.roll(value, cx % 128, 1)
            open_ = value < WALL_TEST
            if cx:
                open_ = open_ & (lane != (0 if cx == 1 else 127))
            bounced = jnp.where(open_, value, source[OPP[q], z, 0:16])
            out[q, z - 1] = jnp.where(fluid, bounced, source[q, z, 0:16])


VMEM = pl.BlockSpec(memory_space=pltpu.VMEM)
HBM = pl.BlockSpec(memory_space=pltpu.HBM)


def call(kernel, name, ins, outs, scratch=(), aliases=None, weight=1):
    return pl.pallas_call(
        kernel,
        out_shape=[jax.ShapeDtypeStruct(out[0], (out + (F32,))[2]) for out in outs],
        in_specs=ins,
        out_specs=[out[1] for out in outs],
        scratch_shapes=[s if not isinstance(s, tuple) else pltpu.VMEM(s, F32) for s in scratch],
        input_output_aliases=aliases or {},
        compiler_params=pltpu.CompilerParams(vmem_limit_bytes=24 * MIB),
        cost_estimate=pl.CostEstimate(
            flops=weight * 1_000_000_000, bytes_accessed=0, transcendentals=0
        ),
        name=name,
    )


def over_quad(up, down):
    count = lax.axis_size("quad")
    ring = [(i, (i + 1) % count) for i in range(count)]
    return lax.ppermute(up, "quad", ring), lax.ppermute(down, "quad", [(j, i) for i, j in ring])


def over_wide(first, second):
    wide, quad = lax.axis_size("wide"), lax.axis_size("quad")
    near, far = [], []
    for w in range(wide):
        for q in range(quad):
            near.append((w * quad + q, (w ^ 1) * quad + q))
            if w in (0, wide - 1):
                far.append((w * quad + q, w * quad + (q ^ 1)))
            else:
                far.append((w * quad + q, (w + 1 if w % 2 else w - 1) * quad + q))
    axes = ("wide", "quad")
    return lax.ppermute(first, axes, near), lax.ppermute(second, axes, far)


def shards(fine_pops, coarse_pops, fine_solid, coarse_solid, fine_active, coarse_covered, rates):
    i32 = jnp.int32
    dma = pltpu.SemaphoreType.DMA
    ext_shape, pops_shape = (20, 8, 40, 128), (19, 8, 40, 128)
    def in_hbm(*arrays):
        return [pltpu.with_memory_space_constraint(a, pltpu.HBM) for a in arrays]

    ext, yu, yd, zu, zd, solid, on, frate, crate = call(
        faces_first_kernel,
        "collide_faces",
        [HBM] * 7,
        [(ext_shape, VMEM)]
        + [((Y_FACES, 128), VMEM)] * 2
        + [((6, 16, 128), VMEM)] * 2
        + [((8, 32, 128), VMEM, i32), ((2, 32, 128), VMEM)]
        + [((15, 8, 128), VMEM)] * 2,
        [
            pltpu.SMEM((15,), F32),
            (4, 19, 32, 128),
            pltpu.VMEM((2, 8, 32), i32),
            (19, 2, 16, 128),
            pltpu.VMEM((2, 16, 128), i32),
            pltpu.VMEM((2, 16, 128), i32),
            dma((10,)),
        ],
    )(
        *in_hbm(
            rates, fine_pops, fine_solid, fine_active, coarse_pops, coarse_solid, coarse_covered
        )
    )
    ru, rd = over_quad(yu, yd)
    ext, yu, yd = call(
        inner_first_kernel,
        "collide_inner",
        [VMEM] * 5,
        [(ext_shape, VMEM)] + [((Y_INNER, 128), VMEM)] * 2,
        aliases={4: 0},
        weight=2,
    )(frate, fine_pops, solid, on, ext)
    ru2, rd2 = over_quad(yu, yd)
    (face_planes,) = call(
        face_planes_kernel,
        "copy_faces",
        [VMEM],
        [((25, 2, 32, 128), VMEM)],
        weight=20,
    )(ext)
    pa, pb = call(
        faces_kernel,
        "substep_one_faces",
        [VMEM] * 5,
        [((X_ALL, 8, 128), VMEM)] * 2,
        [(20, 1, 40, 128), (5, 40, 128), (8, 128), (2, X_ALL, 8, 128)],
    )(face_planes, zu, zd, ru, rd)
    ra, rb = over_wide(pa, pb)
    (ext,) = call(
        fill_kernel,
        "fill_rows",
        [VMEM] * 5,
        [(ext_shape, VMEM)],
        aliases={0: 0},
    )(ext, ru, rd, ru2, rd2)
    kept = [(pops_shape, VMEM)] * 2
    sent = [((32 * CHUNK, 128), VMEM), ((128, 128), VMEM)]
    out_shape = ((19, 8, 32, 128), HBM)
    work = [(256, 128), (2, 128, 128)]
    first, src2, fine_out, send, rest = call(
        inner_kernel,
        "substeps_inner",
        [VMEM] * 3,
        kept + [out_shape] + sent,
        [(4, 19, 32, 128), (2, 768, 128)] + work + [dma((4,))],
        weight=50,
    )(frate, ext, crate)
    for second, message in ((False, ra), (True, rb)):
        first, src2, send, rest, fine_out = call(
            functools.partial(side_kernel, second),
            "substeps_second_side" if second else "substeps_first_side",
            [VMEM] * 8 + [HBM],
            kept + sent + [out_shape],
            [(2, 19, 32, 128), (768, 128)]
            + work
            + [(19, 40, 128), (5, 40, 128), dma((2,))],
            aliases={4: 0, 5: 1, 6: 2, 7: 3, 8: 4},
            weight=2,
        )(frate, ext, crate, message, first, src2, send, rest, fine_out)
    count = lax.axis_size("wide")
    got = lax.all_to_all(
        send.reshape(count, 1, CHUNK * 128), "wide", split_axis=0, concat_axis=0, tiled=True
    ).reshape(count * CHUNK, 128)
    (coarse_out,) = call(
        coarse_kernel,
        "coarse_step",
        [VMEM] * 9,
        [((19, 2, 16, 128), VMEM)],
        [(7, 128, 128), (2, 384, 128), (128, 128), (19, 4, 24, 128), (19, 4, 24, 128), (2, 13, 8, 128)],
    )(got, crate, coarse_pops, coarse_solid, coarse_covered, ru, rd, ra, rb)
    return (fine_out, coarse_out)


def solution(mesh):
    in_specs = (
        P(None, "wide", "quad", None),
        P(None, "wide", "quad", None),
        P("wide", "quad", None),
        P("wide", "quad", None),
        P("wide", "quad", None),
        P("wide", "quad", None),
        P(),
    )
    out_specs = (P(None, "wide", "quad", None), P(None, "wide", "quad", None))
    return jax.shard_map(shards, mesh=mesh, in_specs=in_specs, out_specs=out_specs, check_vma=False)
```

time: 50 us -> 42.4 us (0.85)
  waiting for transfers between devices: 5.1 us -> 1.3 us
  starting transfers between devices: 7.29 us -> 9.71 us
  local copies, waits for them, and re-layouts: 2.27 us -> 0.02 us
  blocking collectives: 21.4 us -> 19.2 us
  Pallas kernels: 13 us -> 11.3 us
    ppermute x1 -> x2, starting transfers between devices: 1.52 us -> 4.18 us  [over_quad(): lax.ppermute(down, 'quad', [(j, i) for i, j in ring])]
    ppermute x4 -> x2, waiting for transfers between devices: 3.31 us -> 1.02 us  [over_wide(): return (lax.ppermute(first, axes, near), lax.ppermute(second, axes, far))]
    unnamed x16 -> x8, local copies, waits for them, and re-layouts: 2.27 us -> 0.02 us
    all_to_all x1, blocking collectives: 21.4 us -> 19.2 us  [shards(): lax.all_to_all(send.reshape(count, 1, CHUNK * 128), 'wide', split_axis=0,...]
    pallas_call x7 -> x8, Pallas kernels: 11.8 us -> 10.2 us  [the longest x2 3.44 us: shards(): call(functools.partial(side_kernel, second), 'substeps_second_side' if se...]
    ppermute x1 -> x2, waiting for transfers between devices: 1.8 us -> 0.28 us  [over_quad(): lax.ppermute(up, 'quad', ring)]
    ppermute x4 -> x2, starting transfers between devices: 3.57 us -> 3.26 us  [over_wide(): return (lax.ppermute(first, axes, near), lax.ppermute(second, axes, far))]
    ppermute x1 -> x2, starting transfers between devices: 2.19 us -> 2.27 us  [over_quad(): lax.ppermute(up, 'quad', ring)]
  transfers between devices with their start and end apart: 6 -> 6, of which waited for: 3 -> 2; matrix products, arithmetic and copies ran while one was open for 0% -> 0% of each run, Pallas kernels for 14% -> 15%
where the time goes in v3:
time: 42.4 us; the launch traced here: 42.3 us
  blocking collectives  19.2 us (45%)
  Pallas kernels  11.3 us (27%)
  starting transfers between devices  9.71 us (23%)
  waiting for transfers between devices  1.3 us (3%)
  between operations  0.73 us (2%)
    all_to_all x1, blocking collectives, shards(): lax.all_to_all(send.reshape(count, 1, CHUNK * 128), 'wide', split_axis=0,...  19.2 us
    ppermute x2, starting transfers between devices, over_quad(): lax.ppermute(down, 'quad', [(j, i) for i, j in ring])  4.18 us
    pallas_call x2, Pallas kernels, shards(): call(functools.partial(side_kernel, second), 'substeps_second_side' if se...  3.44 us
    pallas_call x1, Pallas kernels, shards(): call(inner_kernel, 'substeps_inner', [VMEM] * 3, kept + [out_shape] + sen...  3.34 us
    ppermute x2, starting transfers between devices, over_wide(): return (lax.ppermute(first, axes, near), lax.ppermute(second, axes, far))  3.26 us
    ppermute x2, starting transfers between devices, over_quad(): lax.ppermute(up, 'quad', ring)  2.27 us
    pallas_call x1, Pallas kernels, shards(): call(faces_first_kernel, 'collide_faces', [HBM] * 7, [(ext_shape, VMEM)]...  2.19 us
    pallas_call x1, Pallas kernels, shards(): call(coarse_kernel, 'coarse_step', [VMEM] * 9, [((19, 2, 16, 128), VMEM)]...  1.15 us
  transfers between devices with their start and end apart: 6, of which 2 were waited for; matrix products, arithmetic and copies ran while one was open for 0% of the time, Pallas kernels for 15%

profile of v3, /device:TPU:1, one launch (start us, length us, event | category | flops | bytes accessed | tf_op | source)
XLA Modules:
  0.0 42.3 jit_solution(12987397785102300939)
XLA Ops:
  0.6 0.0 copy-start
  0.6 2.2 %collide_faces.1 = (f32[20,8,40,128]{3,2,1,0:T(8,128)S(1)}, f32[176,128]{1,0:T(8,128)S(1)}, f32[176,128]{1,0:T(8,128)S(1)}, f32[6,16,128]{2,1,0:T(8,128)S(1)}, f...) custom-call(f32[15]{0:T(128)} %rates_in.1, ...), custom_call_target="tpu_custom_call" | custom-call | flops 1000000000 | tf_op jit(solution)/shard_map/collide_faces/pallas_call | solution.py:721
  2.8 2.2 %collective-permute-start = (f32[176,128]{1,0:T(8,128)S(1)}, f32[176,128]{1,0:T(8,128)S(1)}, u32[]{:S(2)}, u32[]{:S(2)}) collective-permute-start(f32[176,128]{1,0:T(8,128)S(1)} %get-tuple-element.33), channel_id=1, source_target_pairs={{0,1},{1,2},{2,3},{3,0},{4,5},{5,6},{6,7},{7,4},{8,9},{9,10},{10,1... | collective-permute-start | bytes 270344 | tf_op jit(solution)/shard_map/ppermute | solution.py:697
  5.0 1.5 %collective-permute-start.1 = (f32[176,128]{1,0:T(8,128)S(1)}, f32[176,128]{1,0:T(8,128)S(1)}, u32[]{:S(2)}, u32[]{:S(2)}) collective-permute-start(f32[176,128]{1,0:T(8,128)S(1)} %get-tuple-element.34), channel_id=1, source_target_pairs={{1,0},{2,1},{3,2},{0,3},{5,4},{6,5},{7,6},{4,7},{9,8},{10,9},{11,1... | collective-permute-start | bytes 270344 | tf_op jit(solution)/shard_map/ppermute | solution.py:697
  6.6 0.0 copy-done
  6.6 0.6 %collide_inner.1 = (f32[20,8,40,128]{3,2,1,0:T(8,128)S(1)}, f32[392,128]{1,0:T(8,128)S(1)}, f32[392,128]{1,0:T(8,128)S(1)}) custom-call(f32[15,8,128]{2,1,0:T(8,128)S(1)} %get-tuple-element.28.frate, f32[19,8,32,128]{3,2,1,0:T(8,128)S(1)} %copy-done, s32[8,32,128]{2,1,0:T(8,128)S(1)} %get-tuple-element.29.solid, ...), custom_call_target="tpu_custom_call", output_to_operand_aliasing={{0}: (4, {})} | custom-call | flops 2000000000 | tf_op jit(solution)/shard_map/collide_inner/pallas_call | solution.py:745
  7.2 0.1 collective-permute-start.2
  7.3 2.7 %collective-permute-start.3 = (f32[392,128]{1,0:T(8,128)S(1)}, f32[392,128]{1,0:T(8,128)S(1)}, u32[]{:S(2)}, u32[]{:S(2)}) collective-permute-start(f32[392,128]{1,0:T(8,128)S(1)} %get-tuple-element.36), channel_id=1, source_target_pairs={{1,0},{2,1},{3,2},{0,3},{5,4},{6,5},{7,6},{4,7},{9,8},{10,9},{11,1... | collective-permute-start | bytes 602120 | tf_op jit(solution)/shard_map/ppermute | solution.py:697
  9.9 0.1 copy_faces.1.planes
  10.0 0.0 collective-permute-done.ru
  10.0 0.0 collective-permute-done.1.rd
  10.0 0.4 substep_one_faces.1
  10.4 3.3 %collective-permute-start.4 = (f32[113,8,128]{2,1,0:T(8,128)S(1)}, f32[113,8,128]{2,1,0:T(8,128)S(1)}, u32[]{:S(2)}, u32[]{:S(2)}) collective-permute-start(f32[113,8,128]{2,1,0:T(8,128)S(1)} %get-tuple-element.40), channel_id=1, source_target_pairs={{0,1},{1,0},{2,3},{3,2},{4,8},{5,9},{6,10},{7,11},{8,4},{9,5},{10,... | collective-permute-start | bytes 1388552 | tf_op jit(solution)/shard_map/ppermute | solution.py:711
  13.7 0.0 collective-permute-start.5
  13.7 0.3 collective-permute-done.2.ru2
  13.9 0.0 collective-permute-done.3.rd2
  14.0 0.1 fill_rows.1.ext
  14.1 3.3 %substeps_inner.1 = (f32[19,8,40,128]{3,2,1,0:T(8,128)S(1)}, f32[19,8,40,128]{3,2,1,0:T(8,128)S(1)}, f32[19,8,32,128]{3,2,1,0:T(8,128)}, f32[800,128]{1,0:T(8,128)S(1)}, f32[128,128]{1,0:T(8,128)S(1)}) custom-call(f32[15,8,128]{2,1,0:T(8,128)S(1)} %get-tuple-element.28.frate, f32[20,8,40,128]{3,2,1,0:T(8,128)S(1)} %fill_rows.1.ext, ...), custom_call_target="tpu_custom_call" | custom-call | flops 49999998976 | tf_op jit(solution)/shard_map/substeps_inner/pallas_call | solution.py:780
  17.5 0.0 collective-permute-done.5.message.ra
  17.5 1.7 %substeps_first_side.1 = (f32[19,8,40,128]{3,2,1,0:T(8,128)S(1)}, f32[19,8,40,128]{3,2,1,0:T(8,128)S(1)}, f32[800,128]{1,0:T(8,128)S(1)}, f32[128,128]{1,0:T(8,128)S(1)}, f32[19,8,32,128]{3,2,1,0:T(8,128)}) custom-call(f32[15,8,128]{2,1,0:T(8,128)S(1)} %get-tuple-element.28.frate, ...), custom_call_target="tpu_custom_call", output_to_operand_aliasing={{0}: (4, {}), {1}: (5, {}), {2}: (6, {}), {3}: (7, {}), {4}... | custom-call | flops 2000000000 | tf_op jit(solution)/shard_map/substeps_first_side/pallas_call | solution.py:789
  19.2 1.0 %collective-permute-done.4.message.rb = f32[113,8,128]{2,1,0:T(8,128)S(1)} collective-permute-done((f32[113,8,128]{2,1,0:T(8,128)S(1)}, f32[113,8,128]{2,1,0:T(8,128)S(1)}, u32[]{:S(2)}, u32[]{:S(2)}) %collective-permute-start.4) | collective-permute-done | bytes 462880 | tf_op jit(solution)/shard_map/ppermute | solution.py:711
  20.2 0.0 copy-start.1
  20.2 0.0 copy-start.2
  20.2 0.0 copy-start.3
  20.2 1.8 %substeps_second_side.1 = (f32[19,8,40,128]{3,2,1,0:T(8,128)S(1)}, f32[19,8,40,128]{3,2,1,0:T(8,128)S(1)}, f32[800,128]{1,0:T(8,128)S(1)}, f32[128,128]{1,0:T(8,128)S(1)}, f32[19,8,32,128]{3,2,1,0:T(8,128)}) custom-call(f32[15,8,128]{2,1,0:T(8,128)S(1)} %get-tuple-element.28.frate, ...), custom_call_target="tpu_custom_call", output_to_operand_aliasing={{0}: (4, {}), {1}: (5, {}), {2}: (6, {}), {3}: (7, {}), {4}... | custom-call | flops 2000000000 | tf_op jit(solution)/shard_map/substeps_second_side/pallas_call | solution.py:789
  21.9 19.2 %all_to_all.5 = f32[32,1,3200]{2,1,0:T(1,128)S(1)} all-to-all(f32[32,1,3200]{2,1,0:T(1,128)S(1)} %bitcast.2), channel_id=1, replica_groups=mesh['wide'=32,'quad'=4] {'wide'}, dimensions={0} | all-to-all | bytes 819200 | tf_op jit(solution)/shard_map/all_to_all | solution.py:801
  41.1 0.0 copy-done.1
  41.1 0.0 copy-done.2
  41.1 0.0 copy-done.3
  41.1 1.1 %coarse_step.1 = f32[19,2,16,128]{3,2,1,0:T(8,128)} custom-call(f32[800,128]{1,0:T(8,128)S(1)} %bitcast.3, f32[15,8,128]{2,1,0:T(8,128)S(1)} %get-tuple-element.37.crate, f32[19,2,16,128]{3,2,1,0:T(8,128)S(1)} %copy-done.1, s32[2,16,128]{2,1,0:T(8,128)S(1)} %copy-done.2, s32[2,16,128]{2,1,0:T(8,128)S(1)} %copy-done.3, ...), custom_call_target="tpu_custom_call" | custom-call | flops 1000000000 | tf_op jit(solution)/shard_map/coarse_step/pallas_call | solution.py:804
Async XLA Ops:
  0.6 5.9 %copy-start = (f32[19,8,32,128]{3,2,1,0:T(8,128)S(1)}, f32[19,8,32,128]{3,2,1,0:T(8,128)}, u32[]{:S(2)}) copy-start(f32[19,8,32,128]{3,2,1,0:T(8,128)} %f.3) | copy-start | bytes 7471108
  2.8 7.2 %collective-permute-start = (f32[176,128]{1,0:T(8,128)S(1)}, f32[176,128]{1,0:T(8,128)S(1)}, u32[]{:S(2)}, u32[]{:S(2)}) collective-permute-start(f32[176,128]{1,0:T(8,128)S(1)} %get-tuple-element.33), channel_id=1, source_target_pairs={{0,1},{1,2},{2,3},{3,0},{4,5},{5,6},{6,7},{7,4},{8,9},{9,10},{10,1... | collective-permute-start | bytes 270344 | tf_op jit(solution)/shard_map/ppermute | solution.py:697
  5.0 5.0 %collective-permute-start.1 = (f32[176,128]{1,0:T(8,128)S(1)}, f32[176,128]{1,0:T(8,128)S(1)}, u32[]{:S(2)}, u32[]{:S(2)}) collective-permute-start(f32[176,128]{1,0:T(8,128)S(1)} %get-tuple-element.34), channel_id=1, source_target_pairs={{1,0},{2,1},{3,2},{0,3},{5,4},{6,5},{7,6},{4,7},{9,8},{10,9},{11,1... | collective-permute-start | bytes 270344 | tf_op jit(solution)/shard_map/ppermute | solution.py:697
  7.2 6.7 %collective-permute-start.2 = (f32[392,128]{1,0:T(8,128)S(1)}, f32[392,128]{1,0:T(8,128)S(1)}, u32[]{:S(2)}, u32[]{:S(2)}) collective-permute-start(f32[392,128]{1,0:T(8,128)S(1)} %get-tuple-element.35), channel_id=1, source_target_pairs={{0,1},{1,2},{2,3},{3,0},{4,5},{5,6},{6,7},{7,4},{8,9},{9,10},{10,1... | collective-permute-start | bytes 602120 | tf_op jit(solution)/shard_map/ppermute | solution.py:697
  7.3 6.7 %collective-permute-start.3 = (f32[392,128]{1,0:T(8,128)S(1)}, f32[392,128]{1,0:T(8,128)S(1)}, u32[]{:S(2)}, u32[]{:S(2)}) collective-permute-start(f32[392,128]{1,0:T(8,128)S(1)} %get-tuple-element.36), channel_id=1, source_target_pairs={{1,0},{2,1},{3,2},{0,3},{5,4},{6,5},{7,6},{4,7},{9,8},{10,9},{11,1... | collective-permute-start | bytes 602120 | tf_op jit(solution)/shard_map/ppermute | solution.py:697
  10.4 9.8 %collective-permute-start.4 = (f32[113,8,128]{2,1,0:T(8,128)S(1)}, f32[113,8,128]{2,1,0:T(8,128)S(1)}, u32[]{:S(2)}, u32[]{:S(2)}) collective-permute-start(f32[113,8,128]{2,1,0:T(8,128)S(1)} %get-tuple-element.40), channel_id=1, source_target_pairs={{0,1},{1,0},{2,3},{3,2},{4,8},{5,9},{6,10},{7,11},{8,4},{9,5},{10,... | collective-permute-start | bytes 1388552 | tf_op jit(solution)/shard_map/ppermute | solution.py:711
  13.7 3.8 %collective-permute-start.5 = (f32[113,8,128]{2,1,0:T(8,128)S(1)}, f32[113,8,128]{2,1,0:T(8,128)S(1)}, u32[]{:S(2)}, u32[]{:S(2)}) collective-permute-start(f32[113,8,128]{2,1,0:T(8,128)S(1)} %get-tuple-element.41), channel_id=1, source_target_pairs={{0,4},{1,5},{2,6},{3,7},{4,0},{5,1},{6,2},{7,3},{8,12},{9,13},{10,... | collective-permute-start | bytes 1388552 | tf_op jit(solution)/shard_map/ppermute | solution.py:711
  20.2 21.0 %copy-start.1 = (f32[19,2,16,128]{3,2,1,0:T(8,128)S(1)}, f32[19,2,16,128]{3,2,1,0:T(8,128)}, u32[]{:S(2)}) copy-start(f32[19,2,16,128]{3,2,1,0:T(8,128)} %cp.3) | copy-start | bytes 933892
  20.2 21.0 %copy-start.2 = (s32[2,16,128]{2,1,0:T(8,128)S(1)}, s32[2,16,128]{2,1,0:T(8,128)}, u32[]{:S(2)}) copy-start(s32[2,16,128]{2,1,0:T(8,128)} %c_solid.3) | copy-start | bytes 49156
  20.2 21.0 %copy-start.3 = (s32[2,16,128]{2,1,0:T(8,128)S(1)}, s32[2,16,128]{2,1,0:T(8,128)}, u32[]{:S(2)}) copy-start(s32[2,16,128]{2,1,0:T(8,128)} %c_cov.3) | copy-start | bytes 49156

commit v4 on v3

--- a/solution.py
+++ b/solution.py
@@ -51,7 +51,7 @@
 Y_NEXT = 142
 Y_FACES = 176
 Y_INNER = 392
-X_COARSE = 100
+X_COARSE = 70
 X_ALL = X_COARSE + 13
 CHUNK = 25
 
@@ -186,10 +186,19 @@
             yd[start : start + 1] = wall_where(ext[19, x, 0:8], ext[YM[i], x, 0:8])[3:4]
 
 
+def even_quad():
+    return lax.axis_index("quad") % 2 == 0
+
+
+def order_rows(up, down, first, second):
+    first[...] = jnp.where(even_quad(), up[...], down[...])
+    second[...] = jnp.where(even_quad(), down[...], up[...])
+
+
 def faces_first_kernel(
     rates_in, f, solid_in, active_in, cp, c_solid, c_cov,
-    ext, yu, yd, zu, zd, solid, on, frate, crate,
-    rates, held, active, cps, c_solids, c_covs, sems,
+    ext, ya, yb, zu, zd, solid, on, frate, crate,
+    rates, held, active, cps, c_solids, c_covs, yu, yd, sems,
 ):
     small = [
         pltpu.make_async_copy(rates_in, rates, sems.at[0]),
@@ -245,17 +254,19 @@
                 place = Y_COARSE + 6 * z + i
                 value = code if i == 5 else post[values[i]]
                 to[place : place + 1] = value[row : row + 1]
-
-
-def inner_first_kernel(frate, f, solid, on, ext_in, ext, yu, yd):
+    order_rows(yu, yd, ya, yb)
+
+
+def inner_first_kernel(frate, f, solid, on, ext_in, ext, ya, yb, yu, yd):
     fine = read_rates(frate)
 
     def plane(x, carry):
-        collide_plane(x, f.at[:, x], solid, on, fine, ext)
+        collide_plane(x, f.at[:, x - 2], solid, on, fine, ext)
         return carry
 
     lax.fori_loop(2, 6, plane, 0)
     pack_rows(INNER, ext, yu, yd)
+    order_rows(yu, yd, ya, yb)
 
 
 def fill_rows(q, planes, n, ru, rd, to):
@@ -292,8 +303,9 @@
             held[20 + i, face, 0:32] = wall_where(ext[19, near, 0:32], ext[q, near, 0:32])
 
 
-def faces_kernel(planes, zu, zd, ru, rd, pa, pb, held, beyond, tile, both):
+def faces_kernel(planes, zu, zd, qa, qb, pa, pb, ru, rd, held, beyond, tile, both):
     has_prev, has_next, _, _ = edges()
+    order_rows(qb, qa, ru, rd)
     lane = iota((40, 128), 1)
     inside = jnp.where(iota((8, 128), 0) < 4, has_next, has_prev) > 0.5
     for face, x in enumerate(FACES):
@@ -318,12 +330,19 @@
         code = held[19, 0]
         live, open_cells = code > 1.5, {0: code > 0.5}
         outer = (VEL[values[0]][0], lambda q: beyond[values.index(q)])
-        for i in range(20):
-            if i < 14:
-                q = (ACROSS + values)[i]
-                part = streamed(q, 0, held, open_cells, live, lane, outer)
-            elif i < 19:
-                part = wall_where(code, held[values[i - 14], 0])
+        staying = {q: streamed(q, 0, held, open_cells, live, lane, outer) for q in ACROSS}
+        total = None
+        for q, part in staying.items():
+            total = part if total is None else total + part
+        along_y = (staying[3] - staying[4]) + (staying[15] - staying[16]) + (staying[17] - staying[18])
+        along_z = (staying[5] - staying[6]) + (staying[15] - staying[16]) - (staying[17] - staying[18])
+        for i in range(14):
+            if i < 3:
+                part = (total, along_y, along_z)[i]
+            elif i < 8:
+                part = streamed(values[i - 3], 0, held, open_cells, live, lane, outer)
+            elif i < 13:
+                part = wall_where(code, held[values[i - 8], 0])
             else:
                 part = code
             for t in range(5):
@@ -381,8 +400,9 @@
             src2[q, x, rows] = jnp.where(live_t, post[q], old[q])
 
 
-def fill_kernel(ext_in, ru, rd, ru2, rd2, ext):
+def fill_kernel(ext_in, ru, rd, qa, qb, ext, ru2, rd2):
     has_prev, has_next, _, _ = edges()
+    order_rows(qb, qa, ru2, rd2)
     for planes, up, down in ((FACES, ru, rd), (INNER, ru2, rd2)):
         for n, x in enumerate(planes):
             for q in range(19):
@@ -461,7 +481,7 @@
 
 
 def inner_kernel(
-    frate, ext, crate, first, src2, fine_out, send, rest, planes, sums, raw, mixed, sem
+    frate, ext, crate, first, src2, planes, send, rest, sums, raw, mixed
 ):
     fine = read_rates(frate)
     lane = iota((40, 128), 1)
@@ -473,34 +493,28 @@
 
     lax.fori_loop(1, 7, substep_one, 0)
 
-    def out_copy(x):
-        return pltpu.make_async_copy(planes.at[x - 2], fine_out.at[:, x], sem.at[x - 2])
-
     def pair(b, carry):
         for e in range(2):
             x = 2 * b + e
 
             def emit(q, value, before):
-                planes[x - 2, q] = value[0:32]
+                planes[q, x - 2] = value[0:32]
                 rows = pl.ds(40 * q, 40)
                 total = value + before
                 sums[b - 1, rows] = total if e == 0 else sums[b - 1, rows] + total
 
             second_plane(x, ext, first, src2, lane, emit)
-            out_copy(x).start()
         return carry
 
     lax.fori_loop(1, 3, pair, 0)
     coarse = read_rates(crate)
     for b in (1, 2):
         destinations(sums.at[b - 1], coarse, raw, mixed, rest, send, b)
-    for x in range(2, 6):
-        out_copy(x).wait()
 
 
 def side(
-    left, message, inside, frate, ext, crate, first, src2, send, rest, fine_out,
-    planes, sums, raw, mixed, before, outside, sem,
+    left, message, inside, frate, ext, crate, first, src2, send, rest, planes,
+    sums, raw, mixed, before, outside,
 ):
     fine = read_rates(frate)
     lane = iota((40, 128), 1)
@@ -514,9 +528,8 @@
     def part(i):
         return jnp.where(inside > 0.5, arrived(i), WALL)
 
-    code = arrived(19)
-    for i, q in enumerate(ACROSS + entering):
-        before[q] = arrived(i)
+    for i, q in enumerate(entering):
+        before[q] = arrived(3 + i)
     open_cells = ext[19, x] > 0.5
     for q in leaving:
         _, cy, cz = VEL[q]
@@ -528,48 +541,43 @@
         open_ = value < WALL_TEST
         if cz:
             open_ = open_ & (lane != (0 if cz == 1 else 127))
-        before[q] = jnp.where(open_, value, arrived(14 + entering.index(OPP[q])))
+        before[q] = jnp.where(open_, value, arrived(8 + entering.index(OPP[q])))
     for t in range(5):
         rows = pl.ds(8 * t, 8)
-        code_t = message[95 + t] * inside
-        old = [before[q, rows] for q in range(19)]
+        code_t = message[65 + t] * inside
+        old = [before[q, rows] if VEL[q][0] else None for q in range(19)]
+        total, along_y, along_z = message[t], message[5 + t], message[10 + t]
+        for q in ACROSS:
+            old[q] = jnp.zeros((8, 128), F32)
+        old[0], old[3], old[5] = total - along_y - along_z, along_y, along_z
         post = collide(old, fine)
         for i, q in enumerate(entering):
             value = jnp.where(code_t > 1.5, post[q], old[q])
             outside[i, rows] = wall_where(code_t, value)
     step_plane(
-        x, ext, first, src2, fine, lane, (cx, lambda q: part(14 + entering.index(q)))
+        x, ext, first, src2, fine, lane, (cx, lambda q: part(8 + entering.index(q)))
     )
-    copies = []
     for e, (plane, outer) in enumerate(
         ((x, (cx, lambda q: outside[entering.index(q)])), (near, None))
     ):
 
         def emit(q, value, earlier):
-            planes[e, q] = value[0:32]
+            planes[q, plane % 2] = value[0:32]
             rows = pl.ds(40 * q, 40)
             total = value + earlier
             sums[rows] = total if e == 0 else sums[rows] + total
 
         second_plane(plane, ext, first, src2, lane, emit, outer)
-        copy = pltpu.make_async_copy(planes.at[e], fine_out.at[:, plane], sem.at[e])
-        copy.start()
-        copies.append(copy)
     destinations(sums, read_rates(crate), raw, mixed, rest, send, b)
-    for copy in copies:
-        copy.wait()
-
-
-def side_kernel(
-    second, frate, ext, crate, message, first_in, src2_in, send_in, rest_in, fine_in,
-    first, src2, send, rest, fine_out, planes, sums, raw, mixed, before, outside, sem,
-):
+
+
+def first_plane(second):
+    return jnp.where(upwards() == second, 0, 6)
+
+
+def sides(second, message, *refs):
     _, _, has_left, has_right = edges()
-    on_left = upwards() if second else jnp.logical_not(upwards())
-    refs = (
-        frate, ext, crate, first, src2, send, rest, fine_out,
-        planes, sums, raw, mixed, before, outside, sem,
-    )
+    on_left = upwards() == second
 
     @pl.when(on_left)
     def _():
@@ -579,16 +587,43 @@
     def _():
         side(False, message, has_right, *refs)
 
-    if second:
-        of_first, of_second = (picked(plane, rest[...]) for plane in own_planes())
-        send[pl.ds(CHUNK - 1, 32, stride=CHUNK)] = jnp.where(
-            iota((32, 128), 1) < 64, of_first, of_second
-        )
+
+def first_side_kernel(
+    done, frate, ext, crate, message, first_in, src2_in, send_in, rest_in,
+    first, src2, send, rest, fine_out, planes, sums, raw, mixed, before, outside, sem,
+):
+    copy = pltpu.make_async_copy(done, fine_out.at[:, 2:6], sem)
+    copy.start()
+    sides(
+        False, message, frate, ext, crate, first, src2, send, rest, planes,
+        sums, raw, mixed, before, outside,
+    )
+    copy.wait()
+
+
+def second_side_kernel(
+    done, fine_in, frate, ext, crate, message, first_in, src2_in, send_in, rest_in,
+    first, src2, send, rest, fine_out, planes, sums, raw, mixed, before, outside, sem,
+):
+    copy = pltpu.make_async_copy(done, fine_out.at[:, pl.ds(first_plane(False), 2)], sem)
+    copy.start()
+    sides(
+        True, message, frate, ext, crate, first, src2, send, rest, planes,
+        sums, raw, mixed, before, outside,
+    )
+    of_first, of_second = (picked(plane, rest[...]) for plane in own_planes())
+    send[pl.ds(CHUNK - 1, 32, stride=CHUNK)] = jnp.where(
+        iota((32, 128), 1) < 64, of_first, of_second
+    )
+    copy.wait()
 
 
 def coarse_kernel(
-    got, crate, cp, c_solid, c_cov, ru, rd, ra, rb, out, mesh, turned, rest, walled, source, message
+    done, fine_in, got, crate, cp, c_solid, c_cov, ru, rd, ra, rb, out, fine_out,
+    mesh, turned, rest, walled, source, message, result, sems,
 ):
+    copy = pltpu.make_async_copy(done, fine_out.at[:, pl.ds(first_plane(True), 2)], sems.at[0])
+    copy.start()
     has_prev, has_next, has_left, has_right = edges()
     coarse = read_rates(crate)
     for m in range(6):
@@ -654,6 +689,7 @@
         )
 
     lane = iota((16, 128), 1)
+    copies = [copy]
     for z in (1, 2):
         fluid = c_solid[z - 1] == 0
         for q in range(19):
@@ -668,7 +704,11 @@
             if cx:
                 open_ = open_ & (lane != (0 if cx == 1 else 127))
             bounced = jnp.where(open_, value, source[OPP[q], z, 0:16])
-            out[q, z - 1] = jnp.where(fluid, bounced, source[q, z, 0:16])
+            result[q, z - 1] = jnp.where(fluid, bounced, source[q, z, 0:16])
+        copies.append(pltpu.make_async_copy(result.at[:, z - 1], out.at[:, z - 1], sems.at[z]))
+        copies[-1].start()
+    for copy in copies:
+        copy.wait()
 
 
 VMEM = pl.BlockSpec(memory_space=pltpu.VMEM)
@@ -691,10 +731,18 @@
     )
 
 
-def over_quad(up, down):
-    count = lax.axis_size("quad")
-    ring = [(i, (i + 1) % count) for i in range(count)]
-    return lax.ppermute(up, "quad", ring), lax.ppermute(down, "quad", [(j, i) for i, j in ring])
+def over_quad(first, second):
+    wide, quad = lax.axis_size("wide"), lax.axis_size("quad")
+    near, far = [], []
+    for w in range(wide):
+        for q in range(quad):
+            near.append((w * quad + q, w * quad + (q ^ 1)))
+            if q in (0, quad - 1):
+                far.append((w * quad + q, (w ^ 1) * quad + q))
+            else:
+                far.append((w * quad + q, w * quad + (q + 1 if q % 2 else q - 1)))
+    axes = ("wide", "quad")
+    return lax.ppermute(first, axes, near), lax.ppermute(second, axes, far)
 
 
 def over_wide(first, second):
@@ -708,7 +756,8 @@
             else:
                 far.append((w * quad + q, (w + 1 if w % 2 else w - 1) * quad + q))
     axes = ("wide", "quad")
-    return lax.ppermute(first, axes, near), lax.ppermute(second, axes, far)
+    second = lax.ppermute(second, axes, far)
+    return lax.ppermute(first, axes, near), second
 
 
 def shards(fine_pops, coarse_pops, fine_solid, coarse_solid, fine_active, coarse_covered, rates):
@@ -718,7 +767,7 @@
     def in_hbm(*arrays):
         return [pltpu.with_memory_space_constraint(a, pltpu.HBM) for a in arrays]
 
-    ext, yu, yd, zu, zd, solid, on, frate, crate = call(
+    ext, ya, yb, zu, zd, solid, on, frate, crate = call(
         faces_first_kernel,
         "collide_faces",
         [HBM] * 7,
@@ -734,6 +783,8 @@
             (19, 2, 16, 128),
             pltpu.VMEM((2, 16, 128), i32),
             pltpu.VMEM((2, 16, 128), i32),
+            (Y_FACES, 128),
+            (Y_FACES, 128),
             dma((10,)),
         ],
     )(
@@ -741,16 +792,17 @@
             rates, fine_pops, fine_solid, fine_active, coarse_pops, coarse_solid, coarse_covered
         )
     )
-    ru, rd = over_quad(yu, yd)
-    ext, yu, yd = call(
+    qa, qb = over_quad(ya, yb)
+    ext, ya, yb = call(
         inner_first_kernel,
         "collide_inner",
         [VMEM] * 5,
         [(ext_shape, VMEM)] + [((Y_INNER, 128), VMEM)] * 2,
+        [(Y_INNER, 128)] * 2,
         aliases={4: 0},
         weight=2,
-    )(frate, fine_pops, solid, on, ext)
-    ru2, rd2 = over_quad(yu, yd)
+    )(frate, lax.slice_in_dim(fine_pops, 2, 6, axis=1), solid, on, ext)
+    qa2, qb2 = over_quad(ya, yb)
     (face_planes,) = call(
         face_planes_kernel,
         "copy_faces",
@@ -758,56 +810,66 @@
         [((25, 2, 32, 128), VMEM)],
         weight=20,
     )(ext)
-    pa, pb = call(
+    pa, pb, ru, rd = call(
         faces_kernel,
         "substep_one_faces",
         [VMEM] * 5,
-        [((X_ALL, 8, 128), VMEM)] * 2,
+        [((X_ALL, 8, 128), VMEM)] * 2 + [((Y_FACES, 128), VMEM)] * 2,
         [(20, 1, 40, 128), (5, 40, 128), (8, 128), (2, X_ALL, 8, 128)],
-    )(face_planes, zu, zd, ru, rd)
+    )(face_planes, zu, zd, qa, qb)
     ra, rb = over_wide(pa, pb)
     (ext,) = call(
         fill_kernel,
         "fill_rows",
         [VMEM] * 5,
         [(ext_shape, VMEM)],
+        [(Y_INNER, 128)] * 2,
         aliases={0: 0},
-    )(ext, ru, rd, ru2, rd2)
+    )(ext, ru, rd, qa2, qb2)
     kept = [(pops_shape, VMEM)] * 2
     sent = [((32 * CHUNK, 128), VMEM), ((128, 128), VMEM)]
     out_shape = ((19, 8, 32, 128), HBM)
+    two_planes = ((19, 2, 32, 128), VMEM)
     work = [(256, 128), (2, 128, 128)]
-    first, src2, fine_out, send, rest = call(
+    side_work = [(768, 128)] + work + [(19, 40, 128), (5, 40, 128), dma]
+    first, src2, done, send, rest = call(
         inner_kernel,
         "substeps_inner",
         [VMEM] * 3,
-        kept + [out_shape] + sent,
-        [(4, 19, 32, 128), (2, 768, 128)] + work + [dma((4,))],
+        kept + [((19, 4, 32, 128), VMEM)] + sent,
+        [(2, 768, 128)] + work,
         weight=50,
     )(frate, ext, crate)
-    for second, message in ((False, ra), (True, rb)):
-        first, src2, send, rest, fine_out = call(
-            functools.partial(side_kernel, second),
-            "substeps_second_side" if second else "substeps_first_side",
-            [VMEM] * 8 + [HBM],
-            kept + sent + [out_shape],
-            [(2, 19, 32, 128), (768, 128)]
-            + work
-            + [(19, 40, 128), (5, 40, 128), dma((2,))],
-            aliases={4: 0, 5: 1, 6: 2, 7: 3, 8: 4},
-            weight=2,
-        )(frate, ext, crate, message, first, src2, send, rest, fine_out)
+    first, src2, send, rest, fine_out, done = call(
+        first_side_kernel,
+        "substeps_first_side",
+        [VMEM] * 9,
+        kept + sent + [out_shape, two_planes],
+        side_work,
+        aliases={5: 0, 6: 1, 7: 2, 8: 3},
+        weight=2,
+    )(done, frate, ext, crate, ra, first, src2, send, rest)
+    first, src2, send, rest, fine_out, done = call(
+        second_side_kernel,
+        "substeps_second_side",
+        [VMEM, HBM] + [VMEM] * 8,
+        kept + sent + [out_shape, two_planes],
+        side_work,
+        aliases={1: 4, 6: 0, 7: 1, 8: 2, 9: 3},
+        weight=2,
+    )(done, fine_out, frate, ext, crate, rb, first, src2, send, rest)
     count = lax.axis_size("wide")
     got = lax.all_to_all(
         send.reshape(count, 1, CHUNK * 128), "wide", split_axis=0, concat_axis=0, tiled=True
     ).reshape(count * CHUNK, 128)
-    (coarse_out,) = call(
+    coarse_out, fine_out = call(
         coarse_kernel,
         "coarse_step",
-        [VMEM] * 9,
-        [((19, 2, 16, 128), VMEM)],
-        [(7, 128, 128), (2, 384, 128), (128, 128), (19, 4, 24, 128), (19, 4, 24, 128), (2, 13, 8, 128)],
-    )(got, crate, coarse_pops, coarse_solid, coarse_covered, ru, rd, ra, rb)
+        [VMEM, HBM] + [VMEM] * 9,
+        [((19, 2, 16, 128), HBM), out_shape],
+        [(7, 128, 128), (2, 384, 128), (128, 128), (19, 4, 24, 128), (19, 4, 24, 128), (2, 13, 8, 128), (19, 2, 16, 128), dma((3,))],
+        aliases={1: 1},
+    )(done, fine_out, got, crate, coarse_pops, coarse_solid, coarse_covered, ru, rd, ra, rb)
     return (fine_out, coarse_out)
 
 

time: 42.4 us -> 40.7 us (0.960)
  starting transfers between devices: 9.71 us -> 8.2 us
  blocking collectives: 19.2 us -> 20.3 us
  waiting for transfers between devices: 1.3 us -> 0.54 us
  Pallas kernels: 11.3 us -> 10.7 us
    ppermute x6, starting transfers between devices: 9.71 us -> 8.2 us  [the longest x4 6.1 us: over_quad(): return (lax.ppermute(first, axes, near), lax.ppermute(second, axes, far))]
    all_to_all x1, blocking collectives: 19.2 us -> 20.3 us  [shards(): lax.all_to_all(send.reshape(count, 1, CHUNK * 128), 'wide', split_axis=0,...]
    ppermute x6, waiting for transfers between devices: 1.3 us -> 0.54 us  [the longest x4 0.29 us: over_quad(): return (lax.ppermute(first, axes, near), lax.ppermute(second, axes, far))]
    pallas_call x5, Pallas kernels: 8.08 us -> 7.36 us  [the longest x1 3.28 us: shards(): call(inner_kernel, 'substeps_inner', [VMEM] * 3, kept + [((19, 4, 32, 128...]
  transfers between devices with their start and end apart: 6 -> 6, of which waited for: 2 -> 2; matrix products, arithmetic and copies ran while one was open for 0% -> 0% of each run, Pallas kernels for 15% -> 14%
where the time goes in v4:
time: 40.7 us; the launch traced here: 40.5 us
  blocking collectives  20.3 us (50%)
  Pallas kernels  10.7 us (26%)
  starting transfers between devices  8.2 us (20%)
  between operations  0.72 us (2%)
  waiting for transfers between devices  0.54 us (1%)
    all_to_all x1, blocking collectives, shards(): lax.all_to_all(send.reshape(count, 1, CHUNK * 128), 'wide', split_axis=0,...  20.3 us
    ppermute x4, starting transfers between devices, over_quad(): return (lax.ppermute(first, axes, near), lax.ppermute(second, axes, far))  6.1 us
    pallas_call x1, Pallas kernels, shards(): call(inner_kernel, 'substeps_inner', [VMEM] * 3, kept + [((19, 4, 32, 128...  3.28 us
    pallas_call x1, Pallas kernels, shards(): call(faces_first_kernel, 'collide_faces', [HBM] * 7, [(ext_shape, VMEM)]...  2.2 us
    ppermute x1, starting transfers between devices, over_wide(): second = lax.ppermute(second, axes, far)  2.02 us
    pallas_call x1, Pallas kernels, shards(): call(second_side_kernel, 'substeps_second_side', [VMEM, HBM] + [VMEM] * 8...  1.46 us
    pallas_call x1, Pallas kernels, shards(): call(coarse_kernel, 'coarse_step', [VMEM, HBM] + [VMEM] * 9, [((19, 2, 16...  1.27 us
    pallas_call x1, Pallas kernels, shards(): call(first_side_kernel, 'substeps_first_side', [VMEM] * 9, kept + sent +...  1.15 us
  transfers between devices with their start and end apart: 6, of which 2 were waited for; matrix products, arithmetic and copies ran while one was open for 0% of the time, Pallas kernels for 14%

profile of v4, /device:TPU:1, one launch (start us, length us, event | category | flops | bytes accessed | tf_op | source)
XLA Modules:
  0.0 40.5 jit_solution(12458777632531085274)
XLA Ops:
  0.6 0.0 copy-start.3
  0.6 2.2 %collide_faces.1 = (f32[20,8,40,128]{3,2,1,0:T(8,128)S(1)}, f32[176,128]{1,0:T(8,128)S(1)}, f32[176,128]{1,0:T(8,128)S(1)}, f32[6,16,128]{2,1,0:T(8,128)S(1)}, f...) custom-call(f32[15]{0:T(128)} %rates_in.1, ...), custom_call_target="tpu_custom_call" | custom-call | flops 1000000000 | tf_op jit(solution)/shard_map/collide_faces/pallas_call | solution.py:770
  2.9 2.2 %collective-permute-start = (f32[176,128]{1,0:T(8,128)S(1)}, f32[176,128]{1,0:T(8,128)S(1)}, u32[]{:S(2)}, u32[]{:S(2)}) collective-permute-start(f32[176,128]{1,0:T(8,128)S(1)} %get-tuple-element.41), channel_id=1, source_target_pairs={{0,1},{1,0},{2,3},{3,2},{4,5},{5,4},{6,7},{7,6},{8,9},{9,8},{10,11... | collective-permute-start | bytes 270344 | tf_op jit(solution)/shard_map/ppermute | solution.py:745
  5.1 1.0 %collective-permute-start.1 = (f32[176,128]{1,0:T(8,128)S(1)}, f32[176,128]{1,0:T(8,128)S(1)}, u32[]{:S(2)}, u32[]{:S(2)}) collective-permute-start(f32[176,128]{1,0:T(8,128)S(1)} %get-tuple-element.42), channel_id=1, source_target_pairs={{0,4},{1,2},{2,1},{3,7},{4,0},{5,6},{6,5},{7,3},{8,12},{9,10},{10,... | collective-permute-start | bytes 270344 | tf_op jit(solution)/shard_map/ppermute | solution.py:745
  6.0 0.0 copy-done.3
  6.0 0.1 slice.3.f
  6.1 0.7 %collide_inner.1 = (f32[20,8,40,128]{3,2,1,0:T(8,128)S(1)}, f32[392,128]{1,0:T(8,128)S(1)}, f32[392,128]{1,0:T(8,128)S(1)}) custom-call(f32[15,8,128]{2,1,0:T(8,128)S(1)} %get-tuple-element.34.frate, f32[19,4,32,128]{3,2,1,0:T(8,128)S(1)} %slice.3.f, s32[8,32,128]{2,1,0:T(8,128)S(1)} %get-tuple-element.35.solid, ...), custom_call_target="tpu_custom_call", output_to_operand_aliasing={{0}: (4, {})} | custom-call | flops 2000000000 | tf_op jit(solution)/shard_map/collide_inner/pallas_call | solution.py:796
  6.8 1.4 %collective-permute-start.2 = (f32[392,128]{1,0:T(8,128)S(1)}, f32[392,128]{1,0:T(8,128)S(1)}, u32[]{:S(2)}, u32[]{:S(2)}) collective-permute-start(f32[392,128]{1,0:T(8,128)S(1)} %get-tuple-element.45), channel_id=1, source_target_pairs={{0,1},{1,0},{2,3},{3,2},{4,5},{5,4},{6,7},{7,6},{8,9},{9,8},{10,11... | collective-permute-start | bytes 602120 | tf_op jit(solution)/shard_map/ppermute | solution.py:745
  8.3 1.5 %collective-permute-start.3 = (f32[392,128]{1,0:T(8,128)S(1)}, f32[392,128]{1,0:T(8,128)S(1)}, u32[]{:S(2)}, u32[]{:S(2)}) collective-permute-start(f32[392,128]{1,0:T(8,128)S(1)} %get-tuple-element.46), channel_id=1, source_target_pairs={{0,4},{1,2},{2,1},{3,7},{4,0},{5,6},{6,5},{7,3},{8,12},{9,10},{10,... | collective-permute-start | bytes 602120 | tf_op jit(solution)/shard_map/ppermute | solution.py:745
  9.8 0.1 copy_faces.1.planes
  9.9 0.0 collective-permute-done.qa
  9.9 0.0 collective-permute-done.1.qb
  9.9 0.3 substep_one_faces.1
  10.2 0.1 collective-permute-start.4
  10.3 2.0 %collective-permute-start.5 = (f32[83,8,128]{2,1,0:T(8,128)S(1)}, f32[83,8,128]{2,1,0:T(8,128)S(1)}, u32[]{:S(2)}, u32[]{:S(2)}) collective-permute-start(f32[83,8,128]{2,1,0:T(8,128)S(1)} %get-tuple-element.56), channel_id=1, source_target_pairs={{0,1},{1,0},{2,3},{3,2},{4,8},{5,9},{6,10},{7,11},{8,4},{9,5},{10,... | collective-permute-start | bytes 1019912 | tf_op jit(solution)/shard_map/ppermute | solution.py:759
  12.3 0.3 collective-permute-done.2.qa
  12.6 0.0 collective-permute-done.3.qb
  12.6 0.2 fill_rows.1.ext
  12.8 3.3 %substeps_inner.1 = (f32[19,8,40,128]{3,2,1,0:T(8,128)S(1)}, f32[19,8,40,128]{3,2,1,0:T(8,128)S(1)}, f32[19,4,32,128]{3,2,1,0:T(8,128)S(1)}, f32[800,128]{1,0:T(8,128)S(1)}, f32[128,128]{1,0:T(8,128)S(1)}) custom-call(f32[15,8,128]{2,1,0:T(8,128)S(1)} %get-tuple-element.34.frate, f32[20,8,40,128]{3,2,1,0:T(8,128)S(1)} %fill_rows.1.ext, ...), custom_call_target="tpu_custom_call" | custom-call | flops 49999998976 | tf_op jit(solution)/shard_map/substeps_inner/pallas_call | solution.py:835
  16.1 0.0 collective-permute-done.4.message.ra
  16.1 1.2 %substeps_first_side.1 = (f32[19,8,40,128]{3,2,1,0:T(8,128)S(1)}, f32[19,8,40,128]{3,2,1,0:T(8,128)S(1)}, f32[800,128]{1,0:T(8,128)S(1)}, f32[128,128]{1,0:T(8,1...) custom-call(f32[19,4,32,128]{3,2,1,0:T(8,128)S(1)} %get-tuple-elemen, ...), custom_call_target="tpu_custom_call", output_to_operand_aliasing={{0}: (5, {}), {1}: (6, {}), {2}: (7, {}), {3}: (8, {})} | custom-call | flops 2000000000 | tf_op jit(solution)/shard_map/substeps_first_side/pallas_call | solution.py:843
  17.2 0.2 collective-permute-done.5.message.rb
  17.5 0.0 copy-start
  17.5 0.0 copy-start.1
  17.5 0.0 copy-start.2
  17.5 1.5 %substeps_second_side.1 = (f32[19,8,40,128]{3,2,1,0:T(8,128)S(1)}, f32[19,8,40,128]{3,2,1,0:T(8,128)S(1)}, f32[800,128]{1,0:T(8,128)S(1)}, f32[128,128]{1,0:T(8,...) custom-call(f32[19,2,32,128]{3,2,1,0:T(8,128)S(1)} %get-tuple-elemen, ...), custom_call_target="tpu_custom_call", output_to_operand_aliasing={{4}: (1, {}), {0}: (6, {}), {1}: (7, {}), {2}: (8, {}), {3}... | custom-call | flops 2000000000 | tf_op jit(solution)/shard_map/substeps_second_side/pallas_call | solution.py:852
  19.0 20.3 %all_to_all.5 = f32[32,1,3200]{2,1,0:T(1,128)S(1)} all-to-all(f32[32,1,3200]{2,1,0:T(1,128)S(1)} %bitcast.2), channel_id=1, replica_groups=mesh['wide'=32,'quad'=4] {'wide'}, dimensions={0} | all-to-all | bytes 819200 | tf_op jit(solution)/shard_map/all_to_all | solution.py:862
  39.2 0.0 copy-done
  39.2 0.0 copy-done.1
  39.2 0.0 copy-done.2
  39.2 1.3 %coarse_step.1 = (f32[19,2,16,128]{3,2,1,0:T(8,128)}, f32[19,8,32,128]{3,2,1,0:T(8,128)}) custom-call(f32[19,2,32,128]{3,2,1,0:T(8,128)S(1)} %get-tuple-element.61.done, f32[19,8,32,128]{3,2,1,0:T(8,128)} %get-tuple-element.62.fine_in, f32[800,128]{1,0:T(8,128)S(1)} %bitcast.3, ...), custom_call_target="tpu_custom_call", output_to_operand_aliasing={{1}: (1, {})} | custom-call | flops 1000000000 | tf_op jit(solution)/shard_map/coarse_step/pallas_call | solution.py:865
Async XLA Ops:
  0.6 5.4 %copy-start.3 = (f32[19,8,32,128]{3,2,1,0:T(8,128)S(1)}, f32[19,8,32,128]{3,2,1,0:T(8,128)}, u32[]{:S(2)}) copy-start(f32[19,8,32,128]{3,2,1,0:T(8,128)} %f.1) | copy-start | bytes 7471108
  2.9 7.0 %collective-permute-start = (f32[176,128]{1,0:T(8,128)S(1)}, f32[176,128]{1,0:T(8,128)S(1)}, u32[]{:S(2)}, u32[]{:S(2)}) collective-permute-start(f32[176,128]{1,0:T(8,128)S(1)} %get-tuple-element.41), channel_id=1, source_target_pairs={{0,1},{1,0},{2,3},{3,2},{4,5},{5,4},{6,7},{7,6},{8,9},{9,8},{10,11... | collective-permute-start | bytes 270344 | tf_op jit(solution)/shard_map/ppermute | solution.py:745
  5.1 4.8 %collective-permute-start.1 = (f32[176,128]{1,0:T(8,128)S(1)}, f32[176,128]{1,0:T(8,128)S(1)}, u32[]{:S(2)}, u32[]{:S(2)}) collective-permute-start(f32[176,128]{1,0:T(8,128)S(1)} %get-tuple-element.42), channel_id=1, source_target_pairs={{0,4},{1,2},{2,1},{3,7},{4,0},{5,6},{6,5},{7,3},{8,12},{9,10},{10,... | collective-permute-start | bytes 270344 | tf_op jit(solution)/shard_map/ppermute | solution.py:745
  6.8 5.8 %collective-permute-start.2 = (f32[392,128]{1,0:T(8,128)S(1)}, f32[392,128]{1,0:T(8,128)S(1)}, u32[]{:S(2)}, u32[]{:S(2)}) collective-permute-start(f32[392,128]{1,0:T(8,128)S(1)} %get-tuple-element.45), channel_id=1, source_target_pairs={{0,1},{1,0},{2,3},{3,2},{4,5},{5,4},{6,7},{7,6},{8,9},{9,8},{10,11... | collective-permute-start | bytes 602120 | tf_op jit(solution)/shard_map/ppermute | solution.py:745
  8.3 4.3 %collective-permute-start.3 = (f32[392,128]{1,0:T(8,128)S(1)}, f32[392,128]{1,0:T(8,128)S(1)}, u32[]{:S(2)}, u32[]{:S(2)}) collective-permute-start(f32[392,128]{1,0:T(8,128)S(1)} %get-tuple-element.46), channel_id=1, source_target_pairs={{0,4},{1,2},{2,1},{3,7},{4,0},{5,6},{6,5},{7,3},{8,12},{9,10},{10,... | collective-permute-start | bytes 602120 | tf_op jit(solution)/shard_map/ppermute | solution.py:745
  10.2 5.9 %collective-permute-start.4 = (f32[83,8,128]{2,1,0:T(8,128)S(1)}, f32[83,8,128]{2,1,0:T(8,128)S(1)}, u32[]{:S(2)}, u32[]{:S(2)}) collective-permute-start(f32[83,8,128]{2,1,0:T(8,128)S(1)} %get-tuple-element.49), channel_id=1, source_target_pairs={{0,4},{1,5},{2,6},{3,7},{4,0},{5,1},{6,2},{7,3},{8,12},{9,13},{10,... | collective-permute-start | bytes 1019912 | tf_op jit(solution)/shard_map/ppermute | solution.py:760
  10.3 7.2 %collective-permute-start.5 = (f32[83,8,128]{2,1,0:T(8,128)S(1)}, f32[83,8,128]{2,1,0:T(8,128)S(1)}, u32[]{:S(2)}, u32[]{:S(2)}) collective-permute-start(f32[83,8,128]{2,1,0:T(8,128)S(1)} %get-tuple-element.56), channel_id=1, source_target_pairs={{0,1},{1,0},{2,3},{3,2},{4,8},{5,9},{6,10},{7,11},{8,4},{9,5},{10,... | collective-permute-start | bytes 1019912 | tf_op jit(solution)/shard_map/ppermute | solution.py:759
  17.5 21.7 %copy-start = (f32[19,2,16,128]{3,2,1,0:T(8,128)S(1)}, f32[19,2,16,128]{3,2,1,0:T(8,128)}, u32[]{:S(2)}) copy-start(f32[19,2,16,128]{3,2,1,0:T(8,128)} %cp.3) | copy-start | bytes 933892
  17.5 21.7 %copy-start.1 = (s32[2,16,128]{2,1,0:T(8,128)S(1)}, s32[2,16,128]{2,1,0:T(8,128)}, u32[]{:S(2)}) copy-start(s32[2,16,128]{2,1,0:T(8,128)} %c_solid.3) | copy-start | bytes 49156
  17.5 21.7 %copy-start.2 = (s32[2,16,128]{2,1,0:T(8,128)S(1)}, s32[2,16,128]{2,1,0:T(8,128)}, u32[]{:S(2)}) copy-start(s32[2,16,128]{2,1,0:T(8,128)} %c_cov.3) | copy-start | bytes 49156

commit v5 on v4

--- a/solution.py
+++ b/solution.py
@@ -51,8 +51,8 @@
 Y_NEXT = 142
 Y_FACES = 176
 Y_INNER = 392
-X_COARSE = 70
-X_ALL = X_COARSE + 13
+X_COARSE = 65
+X_ALL = X_COARSE + 11
 CHUNK = 25
 
 FACTOR = [0.25] * 3 + [0.5] * 3 + [0.25] * 9
@@ -195,10 +195,10 @@
     second[...] = jnp.where(even_quad(), down[...], up[...])
 
 
-def faces_first_kernel(
+def rows_first_kernel(
     rates_in, f, solid_in, active_in, cp, c_solid, c_cov,
-    ext, ya, yb, zu, zd, solid, on, frate, crate,
-    rates, held, active, cps, c_solids, c_covs, yu, yd, sems,
+    ya, yb, solid, on, frate, crate,
+    rates, low, high, active, cps, c_solids, c_covs, yu, yd, sems,
 ):
     small = [
         pltpu.make_async_copy(rates_in, rates, sems.at[0]),
@@ -211,62 +211,92 @@
         pltpu.make_async_copy(c_cov, c_covs, sems.at[5]),
     ]
     planes = [
-        pltpu.make_async_copy(f.at[:, x], held.at[n], sems.at[6 + n])
+        (
+            pltpu.make_async_copy(f.at[:, x, 0:8], low.at[n], sems.at[6 + 2 * n]),
+            pltpu.make_async_copy(f.at[:, x, 24:32], high.at[n], sems.at[7 + 2 * n]),
+        )
         for n, x in enumerate((0, 7, 1, 6))
     ]
-    for copy in small + planes + coarse_copies:
+    for copy in small:
+        copy.start()
+    for pair in planes:
+        for copy in pair:
+            copy.start()
+    for copy in coarse_copies:
         copy.start()
     for copy in small:
         copy.wait()
     write_rates(rates, frate, crate)
     fine = read_rates(frate)
     grow(active, on)
+    upper = iota((8, 128), 0) < 4
     for n, x in enumerate((0, 7, 1, 6)):
-        planes[n].wait()
-        collide_plane(x, held.at[n], solid, on, fine, ext)
-    pack_rows(FACES, ext, yu, yd)
-    for e, (x, values) in enumerate(NEXT):
-        for i, q in enumerate(values):
-            start = Y_NEXT + 15 * e + 3 * i
-            high = wall_where(ext[19, x, 24:32], ext[q, x, 24:32])
-            low = wall_where(ext[19, x, 0:8], ext[q, x, 0:8])
-            yu[start : start + 3] = high[5:8]
-            yd[start : start + 3] = low[0:3]
-            fourth = Y_NEXT + 30 + e
-            if q in YP:
-                yu[fourth : fourth + 1] = high[4:5]
-            if q in YM:
-                yd[fourth : fourth + 1] = low[3:4]
+        for copy in planes[n]:
+            copy.wait()
+        old = [jnp.where(upper, low[n, q], high[n, q]) for q in range(19)]
+        fluid = jnp.where(upper, solid[x, 0:8], solid[x, 24:32]) == 0
+        here = jnp.where(upper, on[x // 4, 0:8], on[x // 4, 24:32])
+        live = fluid & (here > 0.5)
+        post = collide(old, fine)
+        source = [jnp.where(live, post[q], old[q]) for q in range(19)]
+        source.append(jnp.where(fluid, 1.0 + here, 0.0))
+        walled = [jnp.where(fluid, value, WALL) for value in source[:19]]
+        if n < 2:
+            for q in range(20):
+                start = 60 * n + 3 * q
+                yu[start : start + 3] = source[q][5:8]
+                yd[start : start + 3] = source[q][0:3]
+            for i in range(5):
+                start = 120 + 2 * i + n
+                yu[start : start + 1] = walled[YP[i]][4:5]
+                yd[start : start + 1] = walled[YM[i]][3:4]
+        else:
+            e = n - 2
+            for i, q in enumerate(NEXT[e][1]):
+                start = Y_NEXT + 15 * e + 3 * i
+                fourth = Y_NEXT + 30 + e
+                yu[start : start + 3] = walled[q][5:8]
+                yd[start : start + 3] = walled[q][0:3]
+                if q in YP:
+                    yu[fourth : fourth + 1] = walled[q][4:5]
+                if q in YM:
+                    yd[fourth : fourth + 1] = walled[q][3:4]
     for copy in coarse_copies:
         copy.wait()
     coarse = read_rates(crate)
     for z in range(2):
+        old = [jnp.where(upper, cps[q, z, 0:8], cps[q, z, 8:16]) for q in range(19)]
+        post = collide(old, coarse)
+        fluid = jnp.where(upper, c_solids[z, 0:8], c_solids[z, 8:16]) == 0
+        covered = jnp.where(upper, c_covs[z, 0:8], c_covs[z, 8:16]).astype(F32)
+        code = jnp.where(fluid, 1.0 + covered, 0.0)
+        for i in range(6):
+            place = Y_COARSE + 6 * z + i
+            yu[place : place + 1] = (code if i == 5 else post[YP[i]])[7:8]
+            yd[place : place + 1] = (code if i == 5 else post[YM[i]])[0:1]
+    order_rows(yu, yd, ya, yb)
+
+
+def cells_first_kernel(
+    frate, crate, f, solid, on, cp, c_solid, c_cov, ext, ya, yb, zu, zd, yu, yd
+):
+    fine = read_rates(frate)
+
+    def plane(x, carry):
+        collide_plane(x, f.at[:, x], solid, on, fine, ext)
+        return carry
+
+    lax.fori_loop(0, 8, plane, 0)
+    pack_rows(INNER, ext, yu, yd)
+    order_rows(yu, yd, ya, yb)
+    coarse = read_rates(crate)
+    for z, values, to in ((1, ZP, zu), (0, ZM, zd)):
         for t in range(2):
             rows = pl.ds(8 * t, 8)
-            post = collide([cps[q, z, rows] for q in range(19)], coarse)
-            code = jnp.where(c_solids[z, rows] == 0, 1.0 + c_covs[z, rows].astype(F32), 0.0)
-            values, to = (ZP, zu) if z == 1 else (ZM, zd)
+            post = collide([cp[q, z, rows] for q in range(19)], coarse)
             for i in range(5):
                 to[i, rows] = post[values[i]]
-            to[5, rows] = code
-            values, to, row = (YM, yd, 0) if t == 0 else (YP, yu, 7)
-            for i in range(6):
-                place = Y_COARSE + 6 * z + i
-                value = code if i == 5 else post[values[i]]
-                to[place : place + 1] = value[row : row + 1]
-    order_rows(yu, yd, ya, yb)
-
-
-def inner_first_kernel(frate, f, solid, on, ext_in, ext, ya, yb, yu, yd):
-    fine = read_rates(frate)
-
-    def plane(x, carry):
-        collide_plane(x, f.at[:, x - 2], solid, on, fine, ext)
-        return carry
-
-    lax.fori_loop(2, 6, plane, 0)
-    pack_rows(INNER, ext, yu, yd)
-    order_rows(yu, yd, ya, yb)
+            to[5, rows] = jnp.where(c_solid[z, rows] == 0, 1.0 + c_cov[z, rows].astype(F32), 0.0)
 
 
 def fill_rows(q, planes, n, ru, rd, to):
@@ -301,6 +331,10 @@
         near, values = NEXT[face]
         for i, q in enumerate(values):
             held[20 + i, face, 0:32] = wall_where(ext[19, near, 0:32], ext[q, near, 0:32])
+
+
+def copy_kernel(from_, to):
+    to[...] = from_[...]
 
 
 def faces_kernel(planes, zu, zd, qa, qb, pa, pb, ru, rd, held, beyond, tile, both):
@@ -336,31 +370,32 @@
             total = part if total is None else total + part
         along_y = (staying[3] - staying[4]) + (staying[15] - staying[16]) + (staying[17] - staying[18])
         along_z = (staying[5] - staying[6]) + (staying[15] - staying[16]) - (staying[17] - staying[18])
-        for i in range(14):
+        for i in range(13):
             if i < 3:
-                part = (total, along_y, along_z)[i]
+                part = (jnp.where(live, total, WALL), along_y, along_z)[i]
             elif i < 8:
                 part = streamed(values[i - 3], 0, held, open_cells, live, lane, outer)
-            elif i < 13:
+            else:
                 part = wall_where(code, held[values[i - 8], 0])
-            else:
-                part = code
             for t in range(5):
                 both[place, 5 * i + t] = part[8 * t : 8 * t + 8]
         z, arriving, leaving, from_ = ((0, 17, 16, zd), (1, 15, 18, zu))[face]
-        for i in range(6):
-            for t in range(2):
-                both[place, X_COARSE + 2 * i + t] = from_[i, 8 * t : 8 * t + 8]
+
+        def marked(cells, value):
+            return wall_where(cells, jnp.where(cells > 1.5, -WALL, value))
+
+        for t in range(2):
+            rows = pl.ds(8 * t, 8)
+            for i in range(5):
+                both[place, X_COARSE + 2 * i + t] = marked(from_[5, rows], from_[i, rows])
 
         def arrived(rows, i):
             row = Y_COARSE + 6 * z + i
             return rows[row : row + 1]
 
-        tile[0:1] = arrived(ru, YP.index(arriving))
-        tile[1:2] = arrived(rd, YM.index(leaving))
-        tile[2:3] = arrived(ru, 5) * has_prev
-        tile[3:4] = arrived(rd, 5) * has_next
-        both[place, X_COARSE + 12] = tile[...]
+        tile[0:1] = marked(arrived(ru, 5) * has_prev, arrived(ru, YP.index(arriving)))
+        tile[1:2] = marked(arrived(rd, 5) * has_next, arrived(rd, YM.index(leaving)))
+        both[place, X_COARSE + 10] = tile[...]
     pa[...] = both[0]
     pb[...] = both[1]
 
@@ -421,17 +456,19 @@
 
 
 def own_planes():
-    z_pair = iota((32, 128), 1) // 2
-    plane = 2 * iota((32, 128), 0)
-    return [jnp.where(z_pair == plane + k, 0.0625, 0.0) for k in range(2)]
+    z_pair = iota((64, 256), 1) % 128 // 2
+    row = iota((64, 256), 0)
+    plane = 2 * (row % 32) + row // 32
+    return jnp.where(z_pair == plane, 0.0625, 0.0).astype(jnp.bfloat16)
 
 
 def picked(rows, cells):
+    high = cells.astype(jnp.bfloat16)
+    low = (cells - high.astype(F32)).astype(jnp.bfloat16)
     return lax.dot_general(
         rows,
-        cells,
+        jnp.concatenate([high, low], axis=1),
         (((1,), (1,)), ((), ())),
-        precision=lax.Precision.HIGHEST,
         preferred_element_type=F32,
     )
 
@@ -471,13 +508,17 @@
                 for i in range(12):
                     rest[pl.ds(64 * k + 12 * b + i, 1)] = here[i]
     planes = own_planes()
-    both = jnp.concatenate(planes, axis=0)
+    got = picked(planes, raw[...])
     for n in range(2):
-        got = picked(both, raw[128 * n : 128 * n + 128])
         for k in range(2):
-            send[pl.ds(6 * b + 2 * k + n, 32, stride=CHUNK)] = got[32 * k : 32 * k + 32]
+            send[pl.ds(6 * b + 2 * k + n, 32, stride=CHUNK)] = got[
+                32 * k : 32 * k + 32, 128 * n : 128 * n + 128
+            ]
+    got = picked(planes, mixed[...].reshape(256, 128))
     for k in range(2):
-        send[pl.ds(6 * b + 4 + k, 32, stride=CHUNK)] = picked(planes[k], mixed[k])
+        send[pl.ds(6 * b + 4 + k, 32, stride=CHUNK)] = got[
+            32 * k : 32 * k + 32, 128 * k : 128 * k + 128
+        ]
 
 
 def inner_kernel(
@@ -544,7 +585,6 @@
         before[q] = jnp.where(open_, value, arrived(8 + entering.index(OPP[q])))
     for t in range(5):
         rows = pl.ds(8 * t, 8)
-        code_t = message[65 + t] * inside
         old = [before[q, rows] if VEL[q][0] else None for q in range(19)]
         total, along_y, along_z = message[t], message[5 + t], message[10 + t]
         for q in ACROSS:
@@ -552,8 +592,9 @@
         old[0], old[3], old[5] = total - along_y - along_z, along_y, along_z
         post = collide(old, fine)
         for i, q in enumerate(entering):
-            value = jnp.where(code_t > 1.5, post[q], old[q])
-            outside[i, rows] = wall_where(code_t, value)
+            value = jnp.where(total < WALL_TEST, post[q], old[q])
+            fluid = message[40 + 5 * i + t] < WALL_TEST
+            outside[i, rows] = jnp.where(fluid & (inside > 0.5), value, WALL)
     step_plane(
         x, ext, first, src2, fine, lane, (cx, lambda q: part(8 + entering.index(q)))
     )
@@ -611,9 +652,9 @@
         True, message, frate, ext, crate, first, src2, send, rest, planes,
         sums, raw, mixed, before, outside,
     )
-    of_first, of_second = (picked(plane, rest[...]) for plane in own_planes())
+    got = picked(own_planes(), rest[...])
     send[pl.ds(CHUNK - 1, 32, stride=CHUNK)] = jnp.where(
-        iota((32, 128), 1) < 64, of_first, of_second
+        iota((32, 128), 1) < 64, got[0:32], got[32:64]
     )
     copy.wait()
 
@@ -638,7 +679,7 @@
     rest[...] = mesh[6].T
 
     goes_up = upwards()
-    for i in range(13):
+    for i in range(11):
         first, second = ra[X_COARSE + i], rb[X_COARSE + i]
         message[0, i] = jnp.where(goes_up, second, first)
         message[1, i] = jnp.where(goes_up, first, second)
@@ -674,18 +715,21 @@
             )
         values, from_, z, inside = ((ZP, message.at[0], 0, has_left), (ZM, message.at[1], 3, has_right))[k]
         prev_q, next_q = ((15, 18), (17, 16))[k]
+
+        def from_beyond(value, here):
+            return jnp.where(inside > 0.5, jnp.where(value < -WALL_TEST, here, value), WALL)
+
         for t in range(2):
-            code = from_[10 + t] * inside
             for i in range(5):
                 start = 304 + 16 * i + 8 * t
-                walled[values[i], z, 8 * t : 8 * t + 8] = pick(
-                    code, turned[k, start : start + 8], from_[2 * i + t]
+                walled[values[i], z, 8 * t : 8 * t + 8] = from_beyond(
+                    from_[2 * i + t], turned[k, start : start + 8]
                 )
-        walled[prev_q, z, 23:24] = pick(
-            from_[12, 2:3] * inside, rest[64 * k + 10 : 64 * k + 11], from_[12, 0:1]
+        walled[prev_q, z, 23:24] = from_beyond(
+            from_[10, 0:1], rest[64 * k + 10 : 64 * k + 11]
         )
-        walled[next_q, z, 16:17] = pick(
-            from_[12, 3:4] * inside, rest[64 * k + 11 : 64 * k + 12], from_[12, 1:2]
+        walled[next_q, z, 16:17] = from_beyond(
+            from_[10, 1:2], rest[64 * k + 11 : 64 * k + 12]
         )
 
     lane = iota((16, 128), 1)
@@ -767,25 +811,24 @@
     def in_hbm(*arrays):
         return [pltpu.with_memory_space_constraint(a, pltpu.HBM) for a in arrays]
 
-    ext, ya, yb, zu, zd, solid, on, frate, crate = call(
-        faces_first_kernel,
-        "collide_faces",
+    ya, yb, solid, on, frate, crate = call(
+        rows_first_kernel,
+        "collide_rows",
         [HBM] * 7,
-        [(ext_shape, VMEM)]
-        + [((Y_FACES, 128), VMEM)] * 2
-        + [((6, 16, 128), VMEM)] * 2
+        [((Y_FACES, 128), VMEM)] * 2
         + [((8, 32, 128), VMEM, i32), ((2, 32, 128), VMEM)]
         + [((15, 8, 128), VMEM)] * 2,
         [
             pltpu.SMEM((15,), F32),
-            (4, 19, 32, 128),
+            (4, 19, 8, 128),
+            (4, 19, 8, 128),
             pltpu.VMEM((2, 8, 32), i32),
             (19, 2, 16, 128),
             pltpu.VMEM((2, 16, 128), i32),
             pltpu.VMEM((2, 16, 128), i32),
             (Y_FACES, 128),
             (Y_FACES, 128),
-            dma((10,)),
+            dma((14,)),
         ],
     )(
         *in_hbm(
@@ -793,15 +836,14 @@
         )
     )
     qa, qb = over_quad(ya, yb)
-    ext, ya, yb = call(
-        inner_first_kernel,
-        "collide_inner",
-        [VMEM] * 5,
-        [(ext_shape, VMEM)] + [((Y_INNER, 128), VMEM)] * 2,
+    ext, ya, yb, zu, zd = call(
+        cells_first_kernel,
+        "collide_cells",
+        [VMEM] * 8,
+        [(ext_shape, VMEM)] + [((Y_INNER, 128), VMEM)] * 2 + [((6, 16, 128), VMEM)] * 2,
         [(Y_INNER, 128)] * 2,
-        aliases={4: 0},
         weight=2,
-    )(frate, lax.slice_in_dim(fine_pops, 2, 6, axis=1), solid, on, ext)
+    )(frate, crate, fine_pops, solid, on, coarse_pops, coarse_solid, coarse_covered)
     qa2, qb2 = over_quad(ya, yb)
     (face_planes,) = call(
         face_planes_kernel,
@@ -817,6 +859,9 @@
         [((X_ALL, 8, 128), VMEM)] * 2 + [((Y_FACES, 128), VMEM)] * 2,
         [(20, 1, 40, 128), (5, 40, 128), (8, 128), (2, X_ALL, 8, 128)],
     )(face_planes, zu, zd, qa, qb)
+    (pb,) = call(
+        copy_kernel, "copy_message", [VMEM], [((X_ALL, 8, 128), VMEM)], weight=20
+    )(pb)
     ra, rb = over_wide(pa, pb)
     (ext,) = call(
         fill_kernel,
@@ -867,7 +912,7 @@
         "coarse_step",
         [VMEM, HBM] + [VMEM] * 9,
         [((19, 2, 16, 128), HBM), out_shape],
-        [(7, 128, 128), (2, 384, 128), (128, 128), (19, 4, 24, 128), (19, 4, 24, 128), (2, 13, 8, 128), (19, 2, 16, 128), dma((3,))],
+        [(7, 128, 128), (2, 384, 128), (128, 128), (19, 4, 24, 128), (19, 4, 24, 128), (2, 11, 8, 128), (19, 2, 16, 128), dma((3,))],
         aliases={1: 1},
     )(done, fine_out, got, crate, coarse_pops, coarse_solid, coarse_covered, ru, rd, ra, rb)
     return (fine_out, coarse_out)

time: 40.7 us -> 39.9 us (0.980)
  Pallas kernels: 10.7 us -> 9.88 us
  waiting for transfers between devices: 0.54 us -> 1.12 us
  starting transfers between devices: 8.2 us -> 7.71 us
    pallas_call x1, Pallas kernels: 3.28 us -> 2.71 us  [shards(): call(inner_kernel, 'substeps_inner', [VMEM] * 3, kept + [((19, 4, 32, 128...]
    ppermute x4, waiting for transfers between devices: 0.29 us -> 0.77 us  [over_quad(): return (lax.ppermute(first, axes, near), lax.ppermute(second, axes, far))]
    ppermute x1, starting transfers between devices: 2.02 us -> 1.61 us  [over_wide(): second = lax.ppermute(second, axes, far)]
    pallas_call x2 -> x3, Pallas kernels: 2.9 us -> 3.1 us  [the longest x1 1.78 us: shards(): call(rows_first_kernel, 'collide_rows', [HBM] * 7, [((Y_FACES, 128), VMEM...]
where the time goes in v5:
time: 39.9 us; the launch traced here: 39.7 us
  blocking collectives  20.2 us (51%)
  Pallas kernels  9.88 us (25%)
  starting transfers between devices  7.71 us (19%)
  waiting for transfers between devices  1.12 us (3%)
  between operations  0.74 us (2%)
    all_to_all x1, blocking collectives, shards(): lax.all_to_all(send.reshape(count, 1, CHUNK * 128), 'wide', split_axis=0,...  20.2 us
    ppermute x4, starting transfers between devices, over_quad(): return (lax.ppermute(first, axes, near), lax.ppermute(second, axes, far))  6.1 us
    pallas_call x1, Pallas kernels, shards(): call(inner_kernel, 'substeps_inner', [VMEM] * 3, kept + [((19, 4, 32, 128...  2.71 us
    pallas_call x1, Pallas kernels, shards(): call(rows_first_kernel, 'collide_rows', [HBM] * 7, [((Y_FACES, 128), VMEM...  1.78 us
    ppermute x1, starting transfers between devices, over_wide(): second = lax.ppermute(second, axes, far)  1.61 us
    pallas_call x1, Pallas kernels, shards(): call(cells_first_kernel, 'collide_cells', [VMEM] * 8, [(ext_shape, VMEM)]...  1.3 us
    pallas_call x1, Pallas kernels, shards(): call(coarse_kernel, 'coarse_step', [VMEM, HBM] + [VMEM] * 9, [((19, 2, 16...  1.27 us
    pallas_call x1, Pallas kernels, shards(): call(second_side_kernel, 'substeps_second_side', [VMEM, HBM] + [VMEM] * 8...  1.17 us
  transfers between devices with their start and end apart: 6, of which 2 were waited for; matrix products, arithmetic and copies ran while one was open for 0% of the time, Pallas kernels for 14%

profile of v5, /device:TPU:1, one launch (start us, length us, event | category | flops | bytes accessed | tf_op | source)
XLA Modules:
  0.0 39.7 jit_solution(16808438432578717928)
XLA Ops:
  0.6 0.0 copy-start.2
  0.6 0.0 copy-start.1
  0.7 0.0 copy-start
  0.7 0.0 copy-start.3
  0.7 1.8 %collide_rows.1 = (f32[176,128]{1,0:T(8,128)S(1)}, f32[176,128]{1,0:T(8,128)S(1)}, s32[8,32,128]{2,1,0:T(8,128)S(1)}, f32[2,32,128]{2,1,0:T(8,128)S(1)}, f32[15,...) custom-call(f32[15]{0:T(128)} %rates_in.1, f32[19,8,32,128]{3,2,1,0:T(8,128)} %f.3, s32[8,32,128]{2,1,0:T(8,128)} %solid_in.1, ...), custom_call_target="tpu_custom_call" | custom-call | flops 1000000000 | tf_op jit(solution)/shard_map/collide_rows/pallas_call | solution.py:814
  2.5 2.2 %collective-permute-start = (f32[176,128]{1,0:T(8,128)S(1)}, f32[176,128]{1,0:T(8,128)S(1)}, u32[]{:S(2)}, u32[]{:S(2)}) collective-permute-start(f32[176,128]{1,0:T(8,128)S(1)} %get-tuple-element.40), channel_id=1, source_target_pairs={{0,1},{1,0},{2,3},{3,2},{4,5},{5,4},{6,7},{7,6},{8,9},{9,8},{10,11... | collective-permute-start | bytes 270344 | tf_op jit(solution)/shard_map/ppermute | solution.py:789
  4.7 1.0 %collective-permute-start.1 = (f32[176,128]{1,0:T(8,128)S(1)}, f32[176,128]{1,0:T(8,128)S(1)}, u32[]{:S(2)}, u32[]{:S(2)}) collective-permute-start(f32[176,128]{1,0:T(8,128)S(1)} %get-tuple-element.41), channel_id=1, source_target_pairs={{0,4},{1,2},{2,1},{3,7},{4,0},{5,6},{6,5},{7,3},{8,12},{9,10},{10,... | collective-permute-start | bytes 270344 | tf_op jit(solution)/shard_map/ppermute | solution.py:789
  5.6 0.0 copy-done.2
  5.6 0.0 copy-done.1
  5.6 0.0 copy-done
  5.6 0.0 copy-done.3
  5.6 1.3 %collide_cells.1 = (f32[20,8,40,128]{3,2,1,0:T(8,128)S(1)}, f32[392,128]{1,0:T(8,128)S(1)}, f32[392,128]{1,0:T(8,128)S(1)}, f32[6,16,128]{2,1,0:T(8,128)S(1)}, f32[6,16,128]{2,1,0:T(8,128)S(1)}) custom-call(f32[15,8,128]{2,1,0:T(8,128)S(1)} %get-tuple-element.33.frate, f32[15,8,128]{2,1,0:T(8,128)S(1)} %get-tuple-element.34.crate, ...), custom_call_target="tpu_custom_call" | custom-call | flops 2000000000 | tf_op jit(solution)/shard_map/collide_cells/pallas_call | solution.py:839
  6.9 1.4 %collective-permute-start.2 = (f32[392,128]{1,0:T(8,128)S(1)}, f32[392,128]{1,0:T(8,128)S(1)}, u32[]{:S(2)}, u32[]{:S(2)}) collective-permute-start(f32[392,128]{1,0:T(8,128)S(1)} %get-tuple-element.44), channel_id=1, source_target_pairs={{0,1},{1,0},{2,3},{3,2},{4,5},{5,4},{6,7},{7,6},{8,9},{9,8},{10,11... | collective-permute-start | bytes 602120 | tf_op jit(solution)/shard_map/ppermute | solution.py:789
  8.4 1.5 %collective-permute-start.3 = (f32[392,128]{1,0:T(8,128)S(1)}, f32[392,128]{1,0:T(8,128)S(1)}, u32[]{:S(2)}, u32[]{:S(2)}) collective-permute-start(f32[392,128]{1,0:T(8,128)S(1)} %get-tuple-element.45), channel_id=1, source_target_pairs={{0,4},{1,2},{2,1},{3,7},{4,0},{5,6},{6,5},{7,3},{8,12},{9,10},{10,... | collective-permute-start | bytes 602120 | tf_op jit(solution)/shard_map/ppermute | solution.py:789
  9.9 0.1 copy_faces.1.planes
  9.9 0.0 collective-permute-done.qa
  9.9 0.0 collective-permute-done.1.qb
  10.0 0.3 substep_one_faces.1
  10.3 1.6 %collective-permute-start.5 = (f32[76,8,128]{2,1,0:T(8,128)S(1)}, f32[76,8,128]{2,1,0:T(8,128)S(1)}, u32[]{:S(2)}, u32[]{:S(2)}) collective-permute-start(f32[76,8,128]{2,1,0:T(8,128)S(1)} %copy_message.1), channel_id=1, source_target_pairs={{0,1},{1,0},{2,3},{3,2},{4,8},{5,9},{6,10},{7,11},{8,4},{9,5},{10,... | collective-permute-start | bytes 933896 | tf_op jit(solution)/shard_map/ppermute | solution.py:803
  11.9 0.0 collective-permute-start.4
  11.9 0.8 %collective-permute-done.2.qa = f32[392,128]{1,0:T(8,128)S(1)} collective-permute-done((f32[392,128]{1,0:T(8,128)S(1)}, f32[392,128]{1,0:T(8,128)S(1)}, u32[]{:S(2)}, u32[]{:S(2)}) %collective-permute-start.2) | collective-permute-done | bytes 200736 | tf_op jit(solution)/shard_map/ppermute | solution.py:789
  12.7 0.0 collective-permute-done.3.qb
  12.7 0.2 fill_rows.1.ext
  12.9 2.7 %substeps_inner.1 = (f32[19,8,40,128]{3,2,1,0:T(8,128)S(1)}, f32[19,8,40,128]{3,2,1,0:T(8,128)S(1)}, f32[19,4,32,128]{3,2,1,0:T(8,128)S(1)}, f32[800,128]{1,0:T(8,128)S(1)}, f32[128,128]{1,0:T(8,128)S(1)}) custom-call(f32[15,8,128]{2,1,0:T(8,128)S(1)} %get-tuple-element.33.frate, f32[20,8,40,128]{3,2,1,0:T(8,128)S(1)} %fill_rows.1.ext, ...), custom_call_target="tpu_custom_call" | custom-call | flops 49999998976 | tf_op jit(solution)/shard_map/substeps_inner/pallas_call | solution.py:880
  15.6 0.0 collective-permute-done.4.message.ra
  15.6 1.0 %substeps_first_side.1 = (f32[19,8,40,128]{3,2,1,0:T(8,128)S(1)}, f32[19,8,40,128]{3,2,1,0:T(8,128)S(1)}, f32[800,128]{1,0:T(8,128)S(1)}, f32[128,128]{1,0:T(8,1...) custom-call(f32[19,4,32,128]{3,2,1,0:T(8,128)S(1)} %get-tuple-elemen, ...), custom_call_target="tpu_custom_call", output_to_operand_aliasing={{0}: (5, {}), {1}: (6, {}), {2}: (7, {}), {3}: (8, {})} | custom-call | flops 2000000000 | tf_op jit(solution)/shard_map/substeps_first_side/pallas_call | solution.py:888
  16.7 0.3 collective-permute-done.5.message.rb
  17.0 1.2 %substeps_second_side.1 = (f32[19,8,40,128]{3,2,1,0:T(8,128)S(1)}, f32[19,8,40,128]{3,2,1,0:T(8,128)S(1)}, f32[800,128]{1,0:T(8,128)S(1)}, f32[128,128]{1,0:T(8,...) custom-call(f32[19,2,32,128]{3,2,1,0:T(8,128)S(1)} %get-tuple-elemen, ...), custom_call_target="tpu_custom_call", output_to_operand_aliasing={{4}: (1, {}), {0}: (6, {}), {1}: (7, {}), {2}: (8, {}), {3}... | custom-call | flops 2000000000 | tf_op jit(solution)/shard_map/substeps_second_side/pallas_call | solution.py:897
  18.2 20.2 %all_to_all.5 = f32[32,1,3200]{2,1,0:T(1,128)S(1)} all-to-all(f32[32,1,3200]{2,1,0:T(1,128)S(1)} %bitcast.2), channel_id=1, replica_groups=mesh['wide'=32,'quad'=4] {'wide'}, dimensions={0} | all-to-all | bytes 819200 | tf_op jit(solution)/shard_map/all_to_all | solution.py:907
  38.4 1.3 %coarse_step.1 = (f32[19,2,16,128]{3,2,1,0:T(8,128)}, f32[19,8,32,128]{3,2,1,0:T(8,128)}) custom-call(f32[19,2,32,128]{3,2,1,0:T(8,128)S(1)} %get-tuple-element.59.done, f32[19,8,32,128]{3,2,1,0:T(8,128)} %get-tuple-element.60.fine_in, f32[800,128]{1,0:T(8,128)S(1)} %bitcast.3, ...), custom_call_target="tpu_custom_call", output_to_operand_aliasing={{1}: (1, {})} | custom-call | flops 1000000000 | tf_op jit(solution)/shard_map/coarse_step/pallas_call | solution.py:910
  (1 shorter events, 0.0 us)
Async XLA Ops:
  0.6 5.0 %copy-start.2 = (s32[2,16,128]{2,1,0:T(8,128)S(1)}, s32[2,16,128]{2,1,0:T(8,128)}, u32[]{:S(2)}) copy-start(s32[2,16,128]{2,1,0:T(8,128)} %c_cov.5) | copy-start | bytes 49156
  0.6 5.0 %copy-start.1 = (s32[2,16,128]{2,1,0:T(8,128)S(1)}, s32[2,16,128]{2,1,0:T(8,128)}, u32[]{:S(2)}) copy-start(s32[2,16,128]{2,1,0:T(8,128)} %c_solid.5) | copy-start | bytes 49156
  0.7 5.0 %copy-start = (f32[19,2,16,128]{3,2,1,0:T(8,128)S(1)}, f32[19,2,16,128]{3,2,1,0:T(8,128)}, u32[]{:S(2)}) copy-start(f32[19,2,16,128]{3,2,1,0:T(8,128)} %cp.5) | copy-start | bytes 933892
  0.7 5.0 %copy-start.3 = (f32[19,8,32,128]{3,2,1,0:T(8,128)S(1)}, f32[19,8,32,128]{3,2,1,0:T(8,128)}, u32[]{:S(2)}) copy-start(f32[19,8,32,128]{3,2,1,0:T(8,128)} %f.3) | copy-start | bytes 7471108
  2.5 7.5 %collective-permute-start = (f32[176,128]{1,0:T(8,128)S(1)}, f32[176,128]{1,0:T(8,128)S(1)}, u32[]{:S(2)}, u32[]{:S(2)}) collective-permute-start(f32[176,128]{1,0:T(8,128)S(1)} %get-tuple-element.40), channel_id=1, source_target_pairs={{0,1},{1,0},{2,3},{3,2},{4,5},{5,4},{6,7},{7,6},{8,9},{9,8},{10,11... | collective-permute-start | bytes 270344 | tf_op jit(solution)/shard_map/ppermute | solution.py:789
  4.7 5.3 %collective-permute-start.1 = (f32[176,128]{1,0:T(8,128)S(1)}, f32[176,128]{1,0:T(8,128)S(1)}, u32[]{:S(2)}, u32[]{:S(2)}) collective-permute-start(f32[176,128]{1,0:T(8,128)S(1)} %get-tuple-element.41), channel_id=1, source_target_pairs={{0,4},{1,2},{2,1},{3,7},{4,0},{5,6},{6,5},{7,3},{8,12},{9,10},{10,... | collective-permute-start | bytes 270344 | tf_op jit(solution)/shard_map/ppermute | solution.py:789
  6.9 5.8 %collective-permute-start.2 = (f32[392,128]{1,0:T(8,128)S(1)}, f32[392,128]{1,0:T(8,128)S(1)}, u32[]{:S(2)}, u32[]{:S(2)}) collective-permute-start(f32[392,128]{1,0:T(8,128)S(1)} %get-tuple-element.44), channel_id=1, source_target_pairs={{0,1},{1,0},{2,3},{3,2},{4,5},{5,4},{6,7},{7,6},{8,9},{9,8},{10,11... | collective-permute-start | bytes 602120 | tf_op jit(solution)/shard_map/ppermute | solution.py:789
  8.4 4.3 %collective-permute-start.3 = (f32[392,128]{1,0:T(8,128)S(1)}, f32[392,128]{1,0:T(8,128)S(1)}, u32[]{:S(2)}, u32[]{:S(2)}) collective-permute-start(f32[392,128]{1,0:T(8,128)S(1)} %get-tuple-element.45), channel_id=1, source_target_pairs={{0,4},{1,2},{2,1},{3,7},{4,0},{5,6},{6,5},{7,3},{8,12},{9,10},{10,... | collective-permute-start | bytes 602120 | tf_op jit(solution)/shard_map/ppermute | solution.py:789
  10.3 6.7 %collective-permute-start.5 = (f32[76,8,128]{2,1,0:T(8,128)S(1)}, f32[76,8,128]{2,1,0:T(8,128)S(1)}, u32[]{:S(2)}, u32[]{:S(2)}) collective-permute-start(f32[76,8,128]{2,1,0:T(8,128)S(1)} %copy_message.1), channel_id=1, source_target_pairs={{0,1},{1,0},{2,3},{3,2},{4,8},{5,9},{6,10},{7,11},{8,4},{9,5},{10,... | collective-permute-start | bytes 933896 | tf_op jit(solution)/shard_map/ppermute | solution.py:803
  11.9 3.7 %collective-permute-start.4 = (f32[76,8,128]{2,1,0:T(8,128)S(1)}, f32[76,8,128]{2,1,0:T(8,128)S(1)}, u32[]{:S(2)}, u32[]{:S(2)}) collective-permute-start(f32[76,8,128]{2,1,0:T(8,128)S(1)} %get-tuple-element.47), channel_id=1, source_target_pairs={{0,4},{1,5},{2,6},{3,7},{4,0},{5,1},{6,2},{7,3},{8,12},{9,13},{10,... | collective-permute-start | bytes 933896 | tf_op jit(solution)/shard_map/ppermute | solution.py:804

commit v6 on v5

--- a/solution.py
+++ b/solution.py
@@ -859,9 +859,6 @@
         [((X_ALL, 8, 128), VMEM)] * 2 + [((Y_FACES, 128), VMEM)] * 2,
         [(20, 1, 40, 128), (5, 40, 128), (8, 128), (2, X_ALL, 8, 128)],
     )(face_planes, zu, zd, qa, qb)
-    (pb,) = call(
-        copy_kernel, "copy_message", [VMEM], [((X_ALL, 8, 128), VMEM)], weight=20
-    )(pb)
     ra, rb = over_wide(pa, pb)
     (ext,) = call(
         fill_kernel,

time: 39.9 us -> 39.8 us (level)
  starting transfers between devices: 7.71 us -> 8.2 us
    ppermute x4, waiting for transfers between devices: 0.77 us -> 0.29 us  [over_quad(): return (lax.ppermute(first, axes, near), lax.ppermute(second, axes, far))]
    ppermute x1, starting transfers between devices: 1.61 us -> 2.02 us  [over_wide(): second = lax.ppermute(second, axes, far)]
where the time goes in v6:
time: 39.8 us; the launch traced here: 39.7 us
  blocking collectives  19.9 us (50%)
  Pallas kernels  9.86 us (25%)
  starting transfers between devices  8.2 us (21%)
  waiting for transfers between devices  0.9 us (2%)
  between operations  0.74 us (2%)
    all_to_all x1, blocking collectives, shards(): lax.all_to_all(send.reshape(count, 1, CHUNK * 128), 'wide', split_axis=0,...  19.9 us
    ppermute x4, starting transfers between devices, over_quad(): return (lax.ppermute(first, axes, near), lax.ppermute(second, axes, far))  6.1 us
    pallas_call x1, Pallas kernels, shards(): call(inner_kernel, 'substeps_inner', [VMEM] * 3, kept + [((19, 4, 32, 128...  2.71 us
    ppermute x1, starting transfers between devices, over_wide(): second = lax.ppermute(second, axes, far)  2.02 us
    pallas_call x1, Pallas kernels, shards(): call(rows_first_kernel, 'collide_rows', [HBM] * 7, [((Y_FACES, 128), VMEM...  1.78 us
    pallas_call x1, Pallas kernels, shards(): call(cells_first_kernel, 'collide_cells', [VMEM] * 8, [(ext_shape, VMEM)]...  1.3 us
    pallas_call x1, Pallas kernels, shards(): call(coarse_kernel, 'coarse_step', [VMEM, HBM] + [VMEM] * 9, [((19, 2, 16...  1.27 us
    pallas_call x1, Pallas kernels, shards(): call(second_side_kernel, 'substeps_second_side', [VMEM, HBM] + [VMEM] * 8...  1.17 us
  transfers between devices with their start and end apart: 6, of which 2 were waited for; matrix products, arithmetic and copies ran while one was open for 0% of the time, Pallas kernels for 14%

profile of v6, /device:TPU:1, one launch (start us, length us, event | category | flops | bytes accessed | tf_op | source)
XLA Modules:
  0.0 39.7 jit_solution(18004657611181219455)
XLA Ops:
  0.6 0.0 copy-start.2
  0.6 0.0 copy-start.1
  0.7 0.0 copy-start
  0.7 0.0 copy-start.3
  0.7 1.8 %collide_rows.1 = (f32[176,128]{1,0:T(8,128)S(1)}, f32[176,128]{1,0:T(8,128)S(1)}, s32[8,32,128]{2,1,0:T(8,128)S(1)}, f32[2,32,128]{2,1,0:T(8,128)S(1)}, f32[15,...) custom-call(f32[15]{0:T(128)} %rates_in.1, f32[19,8,32,128]{3,2,1,0:T(8,128)} %f.3, s32[8,32,128]{2,1,0:T(8,128)} %solid_in.1, ...), custom_call_target="tpu_custom_call" | custom-call | flops 1000000000 | tf_op jit(solution)/shard_map/collide_rows/pallas_call | solution.py:814
  2.5 2.2 %collective-permute-start = (f32[176,128]{1,0:T(8,128)S(1)}, f32[176,128]{1,0:T(8,128)S(1)}, u32[]{:S(2)}, u32[]{:S(2)}) collective-permute-start(f32[176,128]{1,0:T(8,128)S(1)} %get-tuple-element.40), channel_id=1, source_target_pairs={{0,1},{1,0},{2,3},{3,2},{4,5},{5,4},{6,7},{7,6},{8,9},{9,8},{10,11... | collective-permute-start | bytes 270344 | tf_op jit(solution)/shard_map/ppermute | solution.py:789
  4.7 1.0 %collective-permute-start.1 = (f32[176,128]{1,0:T(8,128)S(1)}, f32[176,128]{1,0:T(8,128)S(1)}, u32[]{:S(2)}, u32[]{:S(2)}) collective-permute-start(f32[176,128]{1,0:T(8,128)S(1)} %get-tuple-element.41), channel_id=1, source_target_pairs={{0,4},{1,2},{2,1},{3,7},{4,0},{5,6},{6,5},{7,3},{8,12},{9,10},{10,... | collective-permute-start | bytes 270344 | tf_op jit(solution)/shard_map/ppermute | solution.py:789
  5.6 0.0 copy-done.2
  5.6 0.0 copy-done.1
  5.6 0.0 copy-done
  5.6 0.0 copy-done.3
  5.6 1.3 %collide_cells.1 = (f32[20,8,40,128]{3,2,1,0:T(8,128)S(1)}, f32[392,128]{1,0:T(8,128)S(1)}, f32[392,128]{1,0:T(8,128)S(1)}, f32[6,16,128]{2,1,0:T(8,128)S(1)}, f32[6,16,128]{2,1,0:T(8,128)S(1)}) custom-call(f32[15,8,128]{2,1,0:T(8,128)S(1)} %get-tuple-element.33.frate, f32[15,8,128]{2,1,0:T(8,128)S(1)} %get-tuple-element.34.crate, ...), custom_call_target="tpu_custom_call" | custom-call | flops 2000000000 | tf_op jit(solution)/shard_map/collide_cells/pallas_call | solution.py:839
  6.9 1.4 %collective-permute-start.2 = (f32[392,128]{1,0:T(8,128)S(1)}, f32[392,128]{1,0:T(8,128)S(1)}, u32[]{:S(2)}, u32[]{:S(2)}) collective-permute-start(f32[392,128]{1,0:T(8,128)S(1)} %get-tuple-element.44), channel_id=1, source_target_pairs={{0,1},{1,0},{2,3},{3,2},{4,5},{5,4},{6,7},{7,6},{8,9},{9,8},{10,11... | collective-permute-start | bytes 602120 | tf_op jit(solution)/shard_map/ppermute | solution.py:789
  8.4 1.5 %collective-permute-start.3 = (f32[392,128]{1,0:T(8,128)S(1)}, f32[392,128]{1,0:T(8,128)S(1)}, u32[]{:S(2)}, u32[]{:S(2)}) collective-permute-start(f32[392,128]{1,0:T(8,128)S(1)} %get-tuple-element.45), channel_id=1, source_target_pairs={{0,4},{1,2},{2,1},{3,7},{4,0},{5,6},{6,5},{7,3},{8,12},{9,10},{10,... | collective-permute-start | bytes 602120 | tf_op jit(solution)/shard_map/ppermute | solution.py:789
  9.9 0.1 copy_faces.1.planes
  9.9 0.0 collective-permute-done.qa
  9.9 0.0 collective-permute-done.1.qb
  10.0 0.3 substep_one_faces.1
  10.3 0.1 collective-permute-start.4
  10.4 2.0 %collective-permute-start.5 = (f32[76,8,128]{2,1,0:T(8,128)S(1)}, f32[76,8,128]{2,1,0:T(8,128)S(1)}, u32[]{:S(2)}, u32[]{:S(2)}) collective-permute-start(f32[76,8,128]{2,1,0:T(8,128)S(1)} %get-tuple-element.54), channel_id=1, source_target_pairs={{0,1},{1,0},{2,3},{3,2},{4,8},{5,9},{6,10},{7,11},{8,4},{9,5},{10,... | collective-permute-start | bytes 933896 | tf_op jit(solution)/shard_map/ppermute | solution.py:803
  12.4 0.3 collective-permute-done.2.qa
  12.7 0.0 collective-permute-done.3.qb
  12.7 0.2 fill_rows.1.ext
  12.9 2.7 %substeps_inner.1 = (f32[19,8,40,128]{3,2,1,0:T(8,128)S(1)}, f32[19,8,40,128]{3,2,1,0:T(8,128)S(1)}, f32[19,4,32,128]{3,2,1,0:T(8,128)S(1)}, f32[800,128]{1,0:T(8,128)S(1)}, f32[128,128]{1,0:T(8,128)S(1)}) custom-call(f32[15,8,128]{2,1,0:T(8,128)S(1)} %get-tuple-element.33.frate, f32[20,8,40,128]{3,2,1,0:T(8,128)S(1)} %fill_rows.1.ext, ...), custom_call_target="tpu_custom_call" | custom-call | flops 49999998976 | tf_op jit(solution)/shard_map/substeps_inner/pallas_call | solution.py:877
  15.6 0.0 collective-permute-done.4.message.ra
  15.6 1.0 %substeps_first_side.1 = (f32[19,8,40,128]{3,2,1,0:T(8,128)S(1)}, f32[19,8,40,128]{3,2,1,0:T(8,128)S(1)}, f32[800,128]{1,0:T(8,128)S(1)}, f32[128,128]{1,0:T(8,1...) custom-call(f32[19,4,32,128]{3,2,1,0:T(8,128)S(1)} %get-tuple-elemen, ...), custom_call_target="tpu_custom_call", output_to_operand_aliasing={{0}: (5, {}), {1}: (6, {}), {2}: (7, {}), {3}: (8, {})} | custom-call | flops 2000000000 | tf_op jit(solution)/shard_map/substeps_first_side/pallas_call | solution.py:885
  16.7 0.6 %collective-permute-done.5.message.rb = f32[76,8,128]{2,1,0:T(8,128)S(1)} collective-permute-done((f32[76,8,128]{2,1,0:T(8,128)S(1)}, f32[76,8,128]{2,1,0:T(8,128)S(1)}, u32[]{:S(2)}, u32[]{:S(2)}) %collective-permute-start.5) | collective-permute-done | bytes 311328 | tf_op jit(solution)/shard_map/ppermute | solution.py:803
  17.3 1.2 %substeps_second_side.1 = (f32[19,8,40,128]{3,2,1,0:T(8,128)S(1)}, f32[19,8,40,128]{3,2,1,0:T(8,128)S(1)}, f32[800,128]{1,0:T(8,128)S(1)}, f32[128,128]{1,0:T(8,...) custom-call(f32[19,2,32,128]{3,2,1,0:T(8,128)S(1)} %get-tuple-elemen, ...), custom_call_target="tpu_custom_call", output_to_operand_aliasing={{4}: (1, {}), {0}: (6, {}), {1}: (7, {}), {2}: (8, {}), {3}... | custom-call | flops 2000000000 | tf_op jit(solution)/shard_map/substeps_second_side/pallas_call | solution.py:894
  18.5 19.9 %all_to_all.5 = f32[32,1,3200]{2,1,0:T(1,128)S(1)} all-to-all(f32[32,1,3200]{2,1,0:T(1,128)S(1)} %bitcast.2), channel_id=1, replica_groups=mesh['wide'=32,'quad'=4] {'wide'}, dimensions={0} | all-to-all | bytes 819200 | tf_op jit(solution)/shard_map/all_to_all | solution.py:904
  38.4 1.3 %coarse_step.1 = (f32[19,2,16,128]{3,2,1,0:T(8,128)}, f32[19,8,32,128]{3,2,1,0:T(8,128)}) custom-call(f32[19,2,32,128]{3,2,1,0:T(8,128)S(1)} %get-tuple-element.59.done, f32[19,8,32,128]{3,2,1,0:T(8,128)} %get-tuple-element.60.fine_in, f32[800,128]{1,0:T(8,128)S(1)} %bitcast.3, ...), custom_call_target="tpu_custom_call", output_to_operand_aliasing={{1}: (1, {})} | custom-call | flops 1000000000 | tf_op jit(solution)/shard_map/coarse_step/pallas_call | solution.py:907
Async XLA Ops:
  0.6 5.0 %copy-start.2 = (s32[2,16,128]{2,1,0:T(8,128)S(1)}, s32[2,16,128]{2,1,0:T(8,128)}, u32[]{:S(2)}) copy-start(s32[2,16,128]{2,1,0:T(8,128)} %c_cov.5) | copy-start | bytes 49156
  0.6 5.0 %copy-start.1 = (s32[2,16,128]{2,1,0:T(8,128)S(1)}, s32[2,16,128]{2,1,0:T(8,128)}, u32[]{:S(2)}) copy-start(s32[2,16,128]{2,1,0:T(8,128)} %c_solid.5) | copy-start | bytes 49156
  0.7 5.0 %copy-start = (f32[19,2,16,128]{3,2,1,0:T(8,128)S(1)}, f32[19,2,16,128]{3,2,1,0:T(8,128)}, u32[]{:S(2)}) copy-start(f32[19,2,16,128]{3,2,1,0:T(8,128)} %cp.5) | copy-start | bytes 933892
  0.7 5.0 %copy-start.3 = (f32[19,8,32,128]{3,2,1,0:T(8,128)S(1)}, f32[19,8,32,128]{3,2,1,0:T(8,128)}, u32[]{:S(2)}) copy-start(f32[19,8,32,128]{3,2,1,0:T(8,128)} %f.3) | copy-start | bytes 7471108
  2.5 7.5 %collective-permute-start = (f32[176,128]{1,0:T(8,128)S(1)}, f32[176,128]{1,0:T(8,128)S(1)}, u32[]{:S(2)}, u32[]{:S(2)}) collective-permute-start(f32[176,128]{1,0:T(8,128)S(1)} %get-tuple-element.40), channel_id=1, source_target_pairs={{0,1},{1,0},{2,3},{3,2},{4,5},{5,4},{6,7},{7,6},{8,9},{9,8},{10,11... | collective-permute-start | bytes 270344 | tf_op jit(solution)/shard_map/ppermute | solution.py:789
  4.7 5.3 %collective-permute-start.1 = (f32[176,128]{1,0:T(8,128)S(1)}, f32[176,128]{1,0:T(8,128)S(1)}, u32[]{:S(2)}, u32[]{:S(2)}) collective-permute-start(f32[176,128]{1,0:T(8,128)S(1)} %get-tuple-element.41), channel_id=1, source_target_pairs={{0,4},{1,2},{2,1},{3,7},{4,0},{5,6},{6,5},{7,3},{8,12},{9,10},{10,... | collective-permute-start | bytes 270344 | tf_op jit(solution)/shard_map/ppermute | solution.py:789
  6.9 5.8 %collective-permute-start.2 = (f32[392,128]{1,0:T(8,128)S(1)}, f32[392,128]{1,0:T(8,128)S(1)}, u32[]{:S(2)}, u32[]{:S(2)}) collective-permute-start(f32[392,128]{1,0:T(8,128)S(1)} %get-tuple-element.44), channel_id=1, source_target_pairs={{0,1},{1,0},{2,3},{3,2},{4,5},{5,4},{6,7},{7,6},{8,9},{9,8},{10,11... | collective-permute-start | bytes 602120 | tf_op jit(solution)/shard_map/ppermute | solution.py:789
  8.4 4.3 %collective-permute-start.3 = (f32[392,128]{1,0:T(8,128)S(1)}, f32[392,128]{1,0:T(8,128)S(1)}, u32[]{:S(2)}, u32[]{:S(2)}) collective-permute-start(f32[392,128]{1,0:T(8,128)S(1)} %get-tuple-element.45), channel_id=1, source_target_pairs={{0,4},{1,2},{2,1},{3,7},{4,0},{5,6},{6,5},{7,3},{8,12},{9,10},{10,... | collective-permute-start | bytes 602120 | tf_op jit(solution)/shard_map/ppermute | solution.py:789
  10.3 5.3 %collective-permute-start.4 = (f32[76,8,128]{2,1,0:T(8,128)S(1)}, f32[76,8,128]{2,1,0:T(8,128)S(1)}, u32[]{:S(2)}, u32[]{:S(2)}) collective-permute-start(f32[76,8,128]{2,1,0:T(8,128)S(1)} %get-tuple-element.47), channel_id=1, source_target_pairs={{0,4},{1,5},{2,6},{3,7},{4,0},{5,1},{6,2},{7,3},{8,12},{9,13},{10,... | collective-permute-start | bytes 933896 | tf_op jit(solution)/shard_map/ppermute | solution.py:804
  10.4 6.9 %collective-permute-start.5 = (f32[76,8,128]{2,1,0:T(8,128)S(1)}, f32[76,8,128]{2,1,0:T(8,128)S(1)}, u32[]{:S(2)}, u32[]{:S(2)}) collective-permute-start(f32[76,8,128]{2,1,0:T(8,128)S(1)} %get-tuple-element.54), channel_id=1, source_target_pairs={{0,1},{1,0},{2,3},{3,2},{4,8},{5,9},{6,10},{7,11},{8,4},{9,5},{10,... | collective-permute-start | bytes 933896 | tf_op jit(solution)/shard_map/ppermute | solution.py:803
